TPU v7x, 32 devices: a whole 2x2x4 slice. The times are simulated.
32 devices in a mesh: dp: 8 (over z, y), group: 4 (over x, core).
Axes of the slice: x: 2, y: 2, z: 4, core: 2. Of those that a mesh axis runs over, the one named last changes fastest.
Arguments:
- inputs: bfloat16 [768, 65536], P('group', 'dp'), may hold values from -6 to 6
- labels: int32 [128, 512], P('dp'), may hold values from 0 to 3, never falling along the last dimension, each value on 1 to 256 neighbouring positions
- w_qkv: float32 [4, 192, 576], P('group', 'dp'), may hold values from -0.4375 to 0.4375
- b_qv: float32 [4, 384], P('group'), may hold values from -4 to 4
- w_out: float32 [768, 768], P('dp', 'group'), may hold values from -1.75 to 1.75
- b_out: float32 [768], P('group'), may hold values from -4 to 4
- gain_one: float32 [768], P('group'), may hold values from 0.25 to 1.75
- shift_one: float32 [768], P('group'), may hold values from -4 to 4
- w_up: float32 [4, 192, 768], P('group', 'dp'), may hold values from -0.4375 to 0.4375
- b_up: float32 [4, 768], P('group'), may hold values from -6 to 6
- down_weight: float32 [4, 768, 192], P('group', 'dp'), may hold values from -0.21875 to 0.21875
- down_bias: float32 [4, 192], P('group'), may hold values from -4 to 4
- gain_two: float32 [768], P('group'), may hold values from 0.25 to 1.75
- shift_two: float32 [768], P('group'), may hold values from -4 to 4
- grad_out: bfloat16 [768, 65536], P('group', 'dp'), may hold values from -9 to 9
Outputs:
- result: bfloat16 [768, 65536], P('group', 'dp')
- grad_in: float32 [768, 65536], P('group', 'dp')
- grad_w_qkv: float32 [4, 192, 576], P('group', 'dp')
- grad_b_qv: float32 [4, 384], P('group')
- grad_w_out: float32 [768, 768], P('dp', 'group')
- grad_b_out: float32 [768], P('group')
- grad_gain_one: float32 [768], P('group')
- grad_shift_one: float32 [768], P('group')
- grad_w_up: float32 [4, 192, 768], P('group', 'dp')
- grad_b_up: float32 [4, 768], P('group')
- grad_w_down: float32 [4, 768, 192], P('group', 'dp')
- grad_b_down: float32 [4, 192], P('group')
- grad_gain_two: float32 [768], P('group')
- grad_shift_two: float32 [768], P('group')
Inputs may be any that keep to these rules, and one draw needn't show every extreme that they name: `labels`: in each packed row the ids never fall from one position to the next; every document has 1 to half of 512 positions, and some document has exactly half of 512.
All inputs are finite; a program needn't handle non-finite values.
Results may differ from a plain program's by a relative error of at most 0.012.
The roundings to bfloat16 on the way count: a program that leaves them out, or rounds other values in their place, can miss the bound.
Values may be sent and summed in bfloat16 or wider, within the bound.
A program may use at most 256 MiB of HBM per device.

v0:
```python
import math

import jax
import jax.numpy as jnp
from jax import lax
from jax.sharding import PartitionSpec as P

HD = 64
HG = 3


eps = 1e-12


def cut_along(x, dim, length):
    shape = x.shape
    blocks = x.reshape(*shape[:dim], length, shape[dim] // length, *shape[dim + 1 :])
    return jnp.moveaxis(blocks, dim, 0)


def sum_at_owner(x, axis, dim):
    length = lax.axis_size(axis)
    blocks = lax.all_to_all(cut_along(x, dim, length), axis, 0, 0, tiled=True)
    return jnp.sum(blocks.astype(jnp.float32), axis=0)


def smooth_gate(values):
    return jax.nn.gelu(values, approximate=False)


def contract_rows(left, right):
    return lax.dot_general(
        left, right, (((0,), (0,)), ((), ())), preferred_element_type=jnp.float32
    )


def contract_cols(left, right):
    return lax.dot_general(
        left, right, (((1,), (1,)), ((), ())), preferred_element_type=jnp.float32
    )


def moments(residual, channels):
    totals = lax.psum(jnp.sum(residual, axis=0), "group")
    center = totals / channels
    offset = residual - center[None, :]
    spread = lax.psum(jnp.sum(offset * offset, axis=0), "group") / channels
    inverse = lax.rsqrt(spread + eps)
    return ((residual - center[None, :]) * inverse[None, :], inverse)


def norm_back(incoming, normed, inverse, gain_column, channels):
    scaled = incoming * gain_column[:, None]
    first_sum, second_sum = lax.psum(
        (jnp.sum(scaled, axis=0), jnp.sum(scaled * normed, axis=0)), "group"
    )
    return inverse[None, :] * (
        scaled - first_sum[None, :] / channels - normed * (second_sum[None, :] / channels)
    )


def masked_scores(query_rows, key_rows, label_row):
    factor = 1.0 / math.sqrt(HD)
    scores = (
        jnp.einsum("hdq,hdk->hqk", query_rows, key_rows, preferred_element_type=jnp.float32)
        * factor
    )
    allowed = label_row[:, None] == label_row[None, :]
    return jnp.where(allowed[None], scores, -1000000000.0)


def attend_row(query_rows, key_rows, value_rows, label_row):
    scores = masked_scores(query_rows, key_rows, label_row)
    highest = jnp.max(scores, axis=-1, keepdims=True)
    exponent = jnp.exp(scores - highest)
    totals = jnp.sum(exponent, axis=-1, keepdims=True)
    chances = (exponent / totals).astype(jnp.bfloat16)
    context = jnp.einsum("hqk,hdk->hdq", chances, value_rows, preferred_element_type=jnp.float32)
    return (context.astype(jnp.bfloat16), highest[..., 0] + jnp.log(totals[..., 0]))


def attend_back(query_rows, key_rows, value_rows, label_row, logsum, incoming):
    factor = 1.0 / math.sqrt(HD)
    scores = masked_scores(query_rows, key_rows, label_row)
    exact = jnp.exp(scores - logsum[..., None])
    chances = exact.astype(jnp.bfloat16)
    value_grad = jnp.einsum("hqk,hdq->hdk", chances, incoming, preferred_element_type=jnp.float32)
    prob_grad = jnp.einsum("hdq,hdk->hqk", incoming, value_rows, preferred_element_type=jnp.float32)
    inner_sum = jnp.sum(exact * prob_grad, axis=-1, keepdims=True)
    score_grad = (exact * (prob_grad - inner_sum)).astype(jnp.bfloat16)
    query_grad = (
        jnp.einsum("hqk,hdk->hdq", score_grad, key_rows, preferred_element_type=jnp.float32)
        * factor
    )
    key_grad = (
        jnp.einsum("hqk,hdq->hdk", score_grad, query_rows, preferred_element_type=jnp.float32)
        * factor
    )
    length = query_rows.shape[-1]
    return jnp.concatenate(
        [
            query_grad.reshape(HG * HD, length),
            key_grad.reshape(HG * HD, length),
            value_grad.reshape(HG * HD, length),
        ],
        axis=0,
    )


def per_device(
    inputs,
    labels,
    w_qkv,
    b_qv,
    w_out,
    b_out,
    gain_one,
    shift_one,
    w_up,
    b_up,
    down_weight,
    down_bias,
    gain_two,
    shift_two,
    grad_out,
):
    groups = lax.axis_size("group")
    local, tok_count = inputs.shape
    channels = local * groups
    rows_here, seq_len = labels.shape
    full_qkv, full_out, full_up, full_down = (
        lax.all_gather(w_qkv.astype(jnp.bfloat16), "dp", axis=1, tiled=True),
        lax.all_gather(w_out[None].astype(jnp.bfloat16), "dp", axis=1, tiled=True),
        lax.all_gather(w_up.astype(jnp.bfloat16), "dp", axis=1, tiled=True),
        lax.all_gather(down_weight.astype(jnp.bfloat16), "dp", axis=1, tiled=True),
    )
    mat_qkv = full_qkv[0]
    mat_out = full_out[0]
    mat_up = full_up[0]
    mat_down = full_down[0]
    key_zero = jnp.zeros((local,), jnp.float32)
    qkv_bias = jnp.concatenate([b_qv[0, :local], key_zero, b_qv[0, local:]])
    mixed_low = (contract_rows(mat_qkv, inputs) + qkv_bias[:, None]).astype(jnp.bfloat16)

    def row_pieces(row_index):
        start = row_index * seq_len
        block = lax.dynamic_slice_in_dim(mixed_low, start, seq_len, 1).reshape(3, HG, HD, seq_len)
        label_row = lax.dynamic_slice_in_dim(labels, row_index, 1, 0)[0]
        return (start, block, label_row)

    def forward_row(row_index, carry):
        context_store, logsum_store = carry
        start, block, label_row = row_pieces(row_index)
        context_part, logsum_part = attend_row(block[0], block[1], block[2], label_row)
        context_store = lax.dynamic_update_slice_in_dim(
            context_store, context_part.reshape(local, seq_len), start, 1
        )
        logsum_store = lax.dynamic_update_slice_in_dim(logsum_store, logsum_part, start, 1)
        return (context_store, logsum_store)

    context, logsum = lax.fori_loop(
        0,
        rows_here,
        forward_row,
        (jnp.zeros((local, tok_count), jnp.bfloat16), jnp.zeros((HG, tok_count), jnp.float32)),
    )
    gathered = lax.all_gather(context, "group", axis=0, tiled=True)
    attended = contract_rows(mat_out, gathered) + b_out[:, None]
    normed_one, inverse_one = moments(inputs.astype(jnp.float32) + attended, channels)
    hidden = normed_one * gain_one[:, None] + shift_one[:, None]
    hidden_low = hidden.astype(jnp.bfloat16)
    pre_act = contract_rows(mat_up, hidden_low) + b_up[0][:, None]
    active_values, gate_back = jax.vjp(smooth_gate, pre_act)
    active_low = active_values.astype(jnp.bfloat16)
    branch_output = contract_rows(mat_down, active_low) + down_bias[0][:, None]
    normed_two, inverse_two = moments(hidden + branch_output, channels)
    result = (normed_two * gain_two[:, None] + shift_two[:, None]).astype(jnp.bfloat16)
    upstream = grad_out.astype(jnp.float32)
    resid_two_grad = norm_back(upstream, normed_two, inverse_two, gain_two, channels)
    branch_low = resid_two_grad.astype(jnp.bfloat16)
    down_grad = contract_cols(active_low, branch_low)
    (pre_grad,) = gate_back(jnp.dot(mat_down, branch_low, preferred_element_type=jnp.float32))
    pre_low = pre_grad.astype(jnp.bfloat16)
    up_grad = contract_cols(hidden_low, pre_low)
    hidden_grad = resid_two_grad + jnp.dot(mat_up, pre_low, preferred_element_type=jnp.float32)
    resid_one_grad = norm_back(hidden_grad, normed_one, inverse_one, gain_one, channels)
    attended_low = resid_one_grad.astype(jnp.bfloat16)
    out_grad = contract_cols(gathered, attended_low)
    partial_terms = jnp.dot(mat_out, attended_low, preferred_element_type=jnp.float32)
    context_grad = lax.psum_scatter(partial_terms, "group", scatter_dimension=0, tiled=True).astype(
        jnp.bfloat16
    )

    def backward_row(row_index, score_store):
        start, block, label_row = row_pieces(row_index)
        logsum_part = lax.dynamic_slice_in_dim(logsum, start, seq_len, 1)
        incoming = lax.dynamic_slice_in_dim(context_grad, start, seq_len, 1).reshape(
            HG, HD, seq_len
        )
        terms = attend_back(block[0], block[1], block[2], label_row, logsum_part, incoming)
        return lax.dynamic_update_slice_in_dim(score_store, terms.astype(jnp.bfloat16), start, 1)

    qkv_low = lax.fori_loop(
        0, rows_here, backward_row, jnp.zeros((3 * local, tok_count), jnp.bfloat16)
    )
    qkv_grad = contract_cols(inputs, qkv_low)
    input_grad = jnp.dot(mat_qkv, qkv_low, preferred_element_type=jnp.float32) + resid_one_grad
    token_sums = jnp.sum(qkv_low, axis=1, dtype=jnp.float32)
    qv_sum = jnp.concatenate([token_sums[:local], token_sums[2 * local :]])
    bout_sum = jnp.sum(attended_low, axis=1, dtype=jnp.float32)
    gain_one_sum = jnp.sum(hidden_grad * normed_one, axis=1)
    shift_one_sum = jnp.sum(hidden_grad, axis=1)
    up_sum = jnp.sum(pre_low, axis=1, dtype=jnp.float32)
    down_sum = jnp.sum(branch_low, axis=1, dtype=jnp.float32)
    gain_two_sum = jnp.sum(upstream * normed_two, axis=1)
    shift_two_sum = jnp.sum(upstream, axis=1)
    grads_all = (
        sum_at_owner(qkv_grad[None].astype(jnp.bfloat16), "dp", 1),
        sum_at_owner(out_grad[None].astype(jnp.bfloat16), "dp", 1),
        sum_at_owner(up_grad[None].astype(jnp.bfloat16), "dp", 1),
        sum_at_owner(down_grad[None].astype(jnp.bfloat16), "dp", 1),
    )
    small_sums = lax.psum(
        (
            qv_sum[None],
            bout_sum,
            gain_one_sum,
            shift_one_sum,
            up_sum[None],
            down_sum[None],
            gain_two_sum,
            shift_two_sum,
        ),
        "dp",
    )
    return (
        result,
        input_grad,
        grads_all[0],
        small_sums[0],
        grads_all[1][0],
        small_sums[1],
        small_sums[2],
        small_sums[3],
        grads_all[2],
        small_sums[4],
        grads_all[3],
        small_sums[5],
        small_sums[6],
        small_sums[7],
    )


def solution(mesh):
    placed = (
        P("group", "dp"),
        P("dp", None),
        P("group", "dp", None),
        P("group", None),
        P("dp", "group"),
        P("group"),
        P("group"),
        P("group"),
        P("group", "dp", None),
        P("group", None),
        P("group", "dp", None),
        P("group", None),
        P("group"),
        P("group"),
        P("group", "dp"),
    )
    return jax.shard_map(
        per_device,
        mesh=mesh,
        in_specs=placed,
        out_specs=(
            P("group", "dp"),
            P("group", "dp"),
            P("group", "dp", None),
            P("group", None),
            P("dp", "group"),
            P("group"),
            P("group"),
            P("group"),
            P("group", "dp", None),
            P("group", None),
            P("group", "dp", None),
            P("group", None),
            P("group"),
            P("group"),
        ),
        check_vma=False,
    )
```

profile of v0, /device:TPU:0, one launch (start us, length us, event | category | flops | bytes accessed | tf_op | source)
XLA Modules:
  0.0 926.4 jit_solution(2002516006598238994)
XLA Ops:
  8.9 32.5 %all_gather.15 = bf16[1,192,576]{2,1,0:T(8,128)(2,1)S(1)} all-gather(bf16[1,24,576]{2,1,0:T(8,128)(2,1)S(1)} %convert_element_type.122), channel_id=1, replica_groups=mesh['dp'=8,'group'=4] {'dp'}, dimensions={1}, use_global_device_ids=true | all-gather | bytes 248832 | tf_op jit(solution)/shard_map/all_gather | solution.py:132
  42.1 8.2 add_convert_fusion
  50.7 76.1 %while.28 = (s32[]{:T(128)}, bf16[192,8192]{1,0:T(8,128)(2,1)S(1)}, f32[3,8192]{1,0:T(4,128)S(1)}, bf16[576,8192]{1,0:T(8,128)(2,1)}, s32[16,512]{1,0:T(8,128)},...) while((s32[]{:T(128)}, bf16[192,8192]{1,0:T(8,128)(2,1)S(1)}, ...), condition=%wide.region_3.4_spmd, body=%wide.region_0.3_spmd.sunk | while | flops 211122688 | bytes 12906699 | solution.py:161
  50.8 1.2 fusion.124
  55.6 1.2 fusion.124
  60.3 1.2 fusion.124
  65.1 1.2 fusion.124
  126.9 1.6 copy-done.1
  128.7 31.2 %all-gather = bf16[768,192]{1,0:T(8,128)(2,1)S(1)} all-gather(bf16[96,192]{1,0:T(8,128)(2,1)S(1)} %convert_element_type.124), channel_id=2, replica_groups=mesh['dp'=8,'group'=4] {'dp'}, dimensions={0}, use_global_device_ids=true | all-gather | bytes 331776 | tf_op jit(solution)/shard_map/all_gather | solution.py:133
  159.9 30.9 %all_gather.18 = bf16[1,192,768]{2,1,0:T(8,128)(2,1)S(1)} all-gather(bf16[1,24,768]{2,1,0:T(8,128)(2,1)S(1)} %convert_element_type.127), channel_id=1, replica_groups=mesh['dp'=8,'group'=4] {'dp'}, dimensions={1}, use_global_device_ids=true | all-gather | bytes 331776 | tf_op jit(solution)/shard_map/all_gather | solution.py:134
  190.8 33.0 %all_gather.19 = bf16[1,768,192]{2,1,0:T(8,128)(2,1)} all-gather(bf16[1,96,192]{2,1,0:T(8,128)(2,1)S(1)} %convert_element_type.129), channel_id=1, replica_groups=mesh['dp'=8,'group'=4] {'dp'}, dimensions={1}, use_global_device_ids=true | all-gather | bytes 331776 | tf_op jit(solution)/shard_map/all_gather | solution.py:135
  223.7 11.5 %fusion.70 = (f32[8192]{0:T(1024)S(1)}, f32[192,8192]{1,0:T(8,128)}) fusion(f32[192]{0:T(256)} %param.24, bf16[768,8192]{1,0:T(8,128)(2,1)} %all-gather.3.cloned.1.call-done, bf16[768,192]{1,0:T(8,128)(2,1)S(1)} %all-gather, bf16[192,8192]{1,0:T(8,128)(2,1)} %param.19), kind=kOutput, calls=%fused_computation.131 | convolution fusion | flops 2422202368 | bytes 22348544 | tf_op jit(solution)/shard_map/dot_general | solution.py:32
  235.3 10.4 %psum.112 = f32[8192]{0:T(1024)S(1)} all-reduce(f32[8192]{0:T(1024)S(1)} %get-tuple-element.311), channel_id=1, replica_groups=mesh['dp'=8,'group'=4] {'group'}, use_global_device_ids=true, to_apply=%region_5.6 | all-reduce | flops 8192 | bytes 65536 | tf_op jit(solution)/shard_map/psum | solution.py:44
  245.7 3.5 multiply_reduce_fusion.4
  249.2 11.3 %psum.113 = f32[8192]{0:T(1024)S(1)} all-reduce(f32[8192]{0:T(1024)S(1)} %multiply_reduce_fusion.4), channel_id=1, replica_groups=mesh['dp'=8,'group'=4] {'group'}, use_global_device_ids=true, to_apply=%region_7.8 | all-reduce | flops 8192 | bytes 65536 | tf_op jit(solution)/shard_map/psum | solution.py:47
  260.6 61.0 %fusion.22 = (bf16[768,8192]{0,1:T(8,128)(2,1)}, f32[768,8192]{0,1:T(8,128)}, f32[8192,768]{1,0:T(8,128)}) fusion(f32[768]{0:T(1024)S(1)} %reduce.4, bf16[1,192,768]{2,1,0:T(8,128)(2,1)S(1)} %all_gather.18, f32[192,8192]{1,0:T(8,128)} %get-tuple-element.312, f32[192]{0:T(256)S(1)} %copy-done.27, f32[192]{0:T(256)S(1)} %copy-done.23, ...), kind=kOutput, calls=%fused_computation.47 | convolution fusion | flops 2839019520 | bytes 69571072 | tf_op jit(solution)/shard_map/dot_general | solution.py:32
  321.6 13.8 %fusion.71 = (f32[8192]{0:T(1024)S(1)}, f32[192,8192]{1,0:T(8,128)}) fusion(f32[192]{0:T(256)S(1)} %bitcast.256, bf16[768,8192]{0,1:T(8,128)(2,1)} %get-tuple-element.293, bf16[1,768,192]{2,1,0:T(8,128)(2,1)S(1)} %copy-done.8, f32[192]{0:T(256)S(1)} %copy-done.27, f32[192]{0:T(256)S(1)} %copy-done.23, f32[8192]{0:T(1024)S(1)} %add_rsqrt_fusion.1, ...), kind=kOutput, calls=%fused_computation.132 | convolution fusion | flops 2426920960 | bytes 25561344 | tf_op jit(solution)/shard_map/dot_general | solution.py:32
  335.5 11.1 %psum.114 = f32[8192]{0:T(1024)S(1)} all-reduce(f32[8192]{0:T(1024)S(1)} %get-tuple-element.314), channel_id=1, replica_groups=mesh['dp'=8,'group'=4] {'group'}, use_global_device_ids=true, to_apply=%region_9.10 | all-reduce | flops 8192 | bytes 65536 | tf_op jit(solution)/shard_map/psum | solution.py:44
  346.6 3.5 multiply_reduce_fusion.3
  350.1 11.2 %psum.115 = f32[8192]{0:T(1024)} all-reduce(f32[8192]{0:T(1024)S(1)} %multiply_reduce_fusion.3), channel_id=1, replica_groups=mesh['dp'=8,'group'=4] {'group'}, use_global_device_ids=true, to_apply=%region_11.12 | all-reduce | flops 8192 | bytes 65536 | tf_op jit(solution)/shard_map/psum | solution.py:47
  362.0 5.6 fusion.47
  367.7 31.5 %all-reduce.8.cloned.1.call-done = (f32[8192]{0:T(1024)}, f32[8192]{0:T(1024)}) async-done(((f32[8192]{0:T(1024)}, f32[8192]{0:T(1024)}), (f32[8192]{0:T(1024)}, f32[8192]{0:T(1024)})) %all-reduce.8.cloned.1.call-update) | async-done | bytes 65552 | tf_op jit(solution)/shard_map/psum | solution.py:54
  400.1 8.1 convert_reduce_fusion.3
  408.2 28.8 %convert_reduce_fusion = (f32[768]{0:T(1024)S(1)}, bf16[768,8192]{0,1:T(8,128)(2,1)}) fusion(f32[768,8192]{0,1:T(8,128)} %get-tuple-element.294, bf16[192,8192]{1,0:T(8,128)(2,1)} %get-tuple-element.290, bf16[1,768,192]{2,1,0:T(8,128)(2,1)} %all_gather.19, f32[8192,768]{1,0:T(8,128)} %get-tuple-element.313, f32[768]{0:T(1024)S(1)} %reduce.4), kind=kOutput, calls=%fused_computation.48 | convolution fusion | flops 2522873088 | bytes 66361344 | tf_op jit(solution)/shard_map/dot_general | solution.py:182
  437.0 13.5 %multiply_reduce_fusion.1 = (f32[192]{0:T(256)S(1)}, f32[8192]{0:T(1024)}, f32[8192]{0:T(1024)}, f32[192]{0:T(256)}, f32[192,8192]{1,0:T(8,128)}) fusion(f32[192,8192]{1,0:T(8,128)} %get-tuple-element.312, f32[8192]{0:T(1024)} %copy-done.10, f32[8192]{0:T(1024)S(1)} %broadcast_multiply_fusion.5, f32[192]{0:T(256)S(1)} %copy-done.23, ...), kind=kOutput, calls=%fused_computation.86 | convolution fusion | flops 2444213760 | bytes 35163136 | tf_op jit(solution)/shard_map/dot_general | solution.py:185
  450.7 31.1 %all-reduce.6.cloned.1.call-done = (f32[8192]{0:T(1024)}, f32[8192]{0:T(1024)}) async-done(((f32[8192]{0:T(1024)}, f32[8192]{0:T(1024)}), (f32[8192]{0:T(1024)}, f32[8192]{0:T(1024)})) %all-reduce.6.cloned.1.call-update) | async-done | bytes 65552 | tf_op jit(solution)/shard_map/psum | solution.py:54
  483.4 6.2 convert_reduce_fusion.4
  489.6 2.6 copy-done
  492.2 10.1 %convolution_bitcast_fusion = f32[768,8192]{0,1:T(8,128)} fusion(bf16[768,192]{1,0:T(8,128)(2,1)S(1)} %copy-done.5, f32[192,8192]{1,0:T(8,128)S(1)} %get-tuple-element.292), kind=kOutput, calls=%fused_computation.64 | convolution fusion | flops 2417491968 | bytes 31752192 | tf_op jit(solution)/shard_map/dot_general | solution.py:189
  502.3 24.6 %copy.51 = f32[768,8192]{1,0:T(8,128)} copy(f32[768,8192]{0,1:T(8,128)} %convolution_bitcast_fusion) | data formatting | bytes 50331648
  527.0 1.9 copy-done.3
  528.8 8.1 convolution_convert_fusion
  538.2 5.1 all-to-all-start.3
  543.4 14.4 %convolution_convert_fusion.1 = bf16[192,768]{1,0:T(8,128)(2,1)} fusion(bf16[768,8192]{0,1:T(8,128)(2,1)} %get-tuple-element.318, f32[192,8192]{1,0:T(8,128)} %get-tuple-element.312, f32[192]{0:T(256)S(1)} %copy-done.28, f32[192]{0:T(256)S(1)} %copy-done.23, f32[8192]{0:T(1024)S(1)} %copy-done.11, f32[8192]{0:T(1024)S(1)} %broadcast_multiply_fusion.5), kind=kOutput, calls=%fused_computation.99 | convolution fusion | flops 2423930880 | bytes 19236352 | tf_op jit(solution)/shard_map/dot_general | solution.py:38
  557.8 5.9 all-to-all-start.2
  563.8 11.6 %convolution_convert_fusion.2 = bf16[768,192]{0,1:T(8,128)(2,1)S(1)} fusion(bf16[768,8192]{1,0:T(8,128)(2,1)} %all-gather.3.cloned.1.call-done, f32[192,8192]{1,0:T(8,128)} %copy-done), kind=kOutput, calls=%fused_computation.100 | convolution fusion | flops 2417639424 | bytes 19169280 | tf_op jit(solution)/shard_map/dot_general | solution.py:38
  576.7 6.3 all-to-all-start.1
  584.5 7.7 all-to-all-done.1
  592.9 114.6 %reduce-scatter.4.cloned.1.call-done = f32[192,8192]{1,0:T(8,128)} async-done(((f32[768,8192]{1,0:T(8,128)}), f32[192,8192]{1,0:T(8,128)}) %reduce-scatter.4.cloned.1.call-update) | async-done | bytes 6291472
  707.5 7.0 copy.52
  714.5 4.6 copy.38
  719.1 4.8 broadcast_in_dim.115
  723.9 127.7 %while.29 = (s32[]{:T(128)}, bf16[576,8192]{1,0:T(8,128)(2,1)}, bf16[576,8192]{1,0:T(8,128)(2,1)}, s32[16,512]{1,0:T(8,128)}, f32[3,8192]{1,0:T(4,128)}, /*index...) while((s32[]{:T(128)}, bf16[576,8192]{1,0:T(8,128)(2,1)}, ...), condition=%wide.region_23.24_spmd, body=%wide.region_21.23_spmd.sunk | while | flops 512915968 | bytes 28872916 | solution.py:203
  723.9 1.2 fusion.138
  731.9 1.2 fusion.138
  740.0 1.2 fusion.138
  748.0 1.2 fusion.138
  755.9 1.2 fusion.138
  763.9 1.2 fusion.138
  771.9 1.2 fusion.138
  779.9 1.2 fusion.138
  787.8 1.2 fusion.138
  795.8 1.2 fusion.138
  803.7 1.2 fusion.138
  811.7 1.2 fusion.138
  819.6 1.2 fusion.138
  827.6 1.2 fusion.138
  835.6 1.2 fusion.138
  843.5 1.2 fusion.138
  851.6 10.9 %fusion.35 = f32[192,8192]{1,0:T(8,128)} fusion(f32[192,8192]{1,0:T(8,128)} %copy-done, bf16[576,8192]{1,0:T(8,128)(2,1)} %get-tuple-element.220, bf16[1,192,576]{2,1,0:T(8,128)(2,1)S(1)} %copy-done.7), kind=kOutput, calls=%fused_computation.67 | convolution fusion | flops 1813512192 | bytes 22241280 | tf_op jit(solution)/shard_map/dot_general | solution.py:207
  862.5 8.0 convolution_convert_fusion.3
  870.5 5.7 all-to-all-start
  876.1 5.0 convert_reduce_fusion.1
  881.3 37.6 %all-reduce = (f32[1,384]{1,0:T(1,128)}, f32[192]{0:T(256)}, f32[192]{0:T(256)}, f32[192]{0:T(256)}, f32[1,768]{1,0:T(1,128)}, /*index=5*/f32[1,192]{1,0:T(1,128)}, f32[192]{0:T(256)}, f32[192]{0:T(256)}) all-reduce(f32[1,384]{1,0:T(1,128)S(1)} %broadcast_in_dim.116, ...), channel_id=1, replica_groups=mesh['dp'=8,'group'=4] {'dp'}, use_global_device_ids=true, to_apply=%region_26.27 | all-reduce | flops 2304 | bytes 18432 | tf_op jit(solution)/shard_map/psum | solution.py:223
  (382 shorter events, 190.4 us)
Async XLA Ops:
  7.2 216.6 %all-gather.3.cloned.1.call-start = ((), (), s32[]{:S(2)}) async-start(), calls=%async_computation.5 | async-start | bytes 15728640 | tf_op jit(solution)/shard_map/all_gather | solution.py:167
  41.4 0.7 copy-start.6
  50.7 77.9 %copy-start.14 = (f32[96,192]{1,0:T(8,128)S(1)}, f32[96,192]{1,0:T(8,128)}, u32[]{:S(2)}) copy-start(f32[96,192]{1,0:T(8,128)} %param.23) | copy-start | bytes 221188
  50.7 77.9 %copy-start.16 = (f32[1,24,768]{2,1,0:T(8,128)S(1)}, f32[1,24,768]{2,1,0:T(8,128)}, u32[]{:S(2)}) copy-start(f32[1,24,768]{2,1,0:T(8,128)} %param.27) | copy-start | bytes 221188
  50.7 77.9 %copy-start.15 = (f32[1,96,192]{2,1,0:T(8,128)S(1)}, f32[1,96,192]{2,1,0:T(8,128)}, u32[]{:S(2)}) copy-start(f32[1,96,192]{2,1,0:T(8,128)} %param.29) | copy-start | bytes 221188
  50.7 78.0 %copy-start.21 = (f32[1,768]{1,0:T(1,128)S(1)}, f32[1,768]{1,0:T(1,128)}, u32[]{:S(2)}) copy-start(f32[1,768]{1,0:T(1,128)} %param.28) | copy-start | bytes 9220
  126.9 1.7 copy-start.1
  126.9 1.8 copy-start.9
  128.5 270.7 %all-reduce.8.cloned.1.call-start = ((), (), s32[]{:S(2)}) async-start(), calls=%async_computation.8 | async-start | bytes 131072 | tf_op jit(solution)/shard_map/psum | solution.py:54
  159.9 75.4 %copy-start.4 = (bf16[768,192]{1,0:T(8,128)(2,1)}, bf16[768,192]{1,0:T(8,128)(2,1)S(1)}, u32[]{:S(2)}) copy-start(bf16[768,192]{1,0:T(8,128)(2,1)S(1)} %all-gather) | copy-start | bytes 884740
  235.3 25.3 %copy-start.23 = (f32[192]{0:T(256)S(1)}, f32[192]{0:T(256)}, u32[]{:S(2)}) copy-start(f32[192]{0:T(256)} %param.25) | copy-start | bytes 2308
  235.3 25.3 %copy-start.27 = (f32[192]{0:T(256)S(1)}, f32[192]{0:T(256)}, u32[]{:S(2)}) copy-start(f32[192]{0:T(256)} %param.26) | copy-start | bytes 2308
  260.6 61.1 %copy-start.10 = (f32[8192]{0:T(1024)}, f32[8192]{0:T(1024)S(1)}, u32[]{:S(2)}) copy-start(f32[8192]{0:T(1024)S(1)} %add_rsqrt_fusion.1) | copy-start | bytes 98308
  260.6 61.0 %copy-start.8 = (bf16[1,768,192]{2,1,0:T(8,128)(2,1)S(1)}, bf16[1,768,192]{2,1,0:T(8,128)(2,1)}, u32[]{:S(2)}) copy-start(bf16[1,768,192]{2,1,0:T(8,128)(2,1)} %all_gather.19) | copy-start | bytes 884740
  260.6 61.0 %copy-start.26 = (f32[1,192]{1,0:T(1,128)S(1)}, f32[1,192]{1,0:T(1,128)}, u32[]{:S(2)}) copy-start(f32[1,192]{1,0:T(1,128)} %param.30) | copy-start | bytes 2308
  335.5 26.6 %copy-start.2 = (bf16[192,8192]{1,0:T(8,128)(2,1)S(1)}, bf16[192,8192]{1,0:T(8,128)(2,1)}, u32[]{:S(2)}) copy-start(bf16[192,8192]{1,0:T(8,128)(2,1)} %param.33) | copy-start | bytes 9437188
  335.5 26.6 %copy-start.17 = (f32[192]{0:T(256)S(1)}, f32[192]{0:T(256)}, u32[]{:S(2)}) copy-start(f32[192]{0:T(256)} %param.31) | copy-start | bytes 2308
  350.0 50.0 %copy-start.22 = (f32[192]{0:T(256)S(1)}, f32[192]{0:T(256)}, u32[]{:S(2)}) copy-start(f32[192]{0:T(256)} %param.32) | copy-start | bytes 2308
  367.7 114.2 %all-reduce.6.cloned.1.call-start = ((), (), s32[]{:S(2)}) async-start(), calls=%async_computation.7 | async-start | bytes 131072 | tf_op jit(solution)/shard_map/psum | solution.py:54
  400.1 8.1 copy-start.12
  400.1 8.1 copy-start.13
  450.5 257.0 %reduce-scatter.4.cloned.1.call-start = ((), (), s32[]{:S(2)}) async-start(), calls=%async_computation.6 | async-start | bytes 31457280
  483.4 8.8 copy-start.5
  489.5 2.7 copy-start
  526.9 1.9 copy-start.3
  528.8 14.6 %copy-start.11 = (f32[8192]{0:T(1024)S(1)}, f32[8192]{0:T(1024)}, u32[]{:S(2)}) copy-start(f32[8192]{0:T(1024)} %copy-done.10) | copy-start | bytes 98308
  528.8 14.6 %copy-start.28 = (f32[192]{0:T(256)S(1)}, f32[192]{0:T(256)}, u32[]{:S(2)}) copy-start(f32[192]{0:T(256)} %param.26) | copy-start | bytes 2308
  538.2 19.6 %all-to-all-start.3 = ((bf16[8,1,96,192]{2,3,1,0:T(8,128)(2,1)}), bf16[8,1,96,192]{2,3,1,0:T(8,128)(2,1)S(1)}, u32[]{:S(2)}, u32[]{:S(2)}) async-start(bf16[8,1,96,192]{2,3,1,0:T(8,128)(2,1)} %copy.43), calls=%async_computation.3 | async-start | bytes 786432 | tf_op jit(solution)/shard_map/all_to_all | solution.py:23
  557.8 18.8 %all-to-all-start.2 = ((bf16[8,1,24,768]{3,2,1,0:T(8,128)(2,1)}), bf16[8,1,24,768]{3,2,1,0:T(8,128)(2,1)S(1)}, u32[]{:S(2)}, u32[]{:S(2)}) async-start(bf16[8,1,24,768]{3,2,1,0:T(8,128)(2,1)} %bitcast.32), calls=%async_computation.2 | async-start | bytes 589824 | tf_op jit(solution)/shard_map/all_to_all | solution.py:23
  576.7 15.4 %all-to-all-start.1 = ((bf16[8,1,96,192]{2,3,1,0:T(8,128)(2,1)}), bf16[8,1,96,192]{2,3,1,0:T(8,128)(2,1)S(1)}, u32[]{:S(2)}, u32[]{:S(2)}) async-start(bf16[8,1,96,192]{2,3,1,0:T(8,128)(2,1)} %copy.40), calls=%async_computation.1 | async-start | bytes 786432 | tf_op jit(solution)/shard_map/all_to_all | solution.py:23
  723.9 127.7 %copy-start.7 = (bf16[1,192,576]{2,1,0:T(8,128)(2,1)S(1)}, bf16[1,192,576]{2,1,0:T(8,128)(2,1)}, u32[]{:S(2)}) copy-start(bf16[1,192,576]{2,1,0:T(8,128)(2,1)} %copy-done.6) | copy-start | bytes 663556
  851.6 11.0 %copy-start.25 = (bf16[192,8192]{1,0:T(8,128)(2,1)S(1)}, bf16[192,8192]{1,0:T(8,128)(2,1)}, u32[]{:S(2)}) copy-start(bf16[192,8192]{1,0:T(8,128)(2,1)} %param.19) | copy-start | bytes 9437188
  870.5 10.8 %copy-start.18 = (f32[192]{0:T(256)S(1)}, f32[192]{0:T(256)}, u32[]{:S(2)}) copy-start(f32[192]{0:T(256)} %get-tuple-element.249) | copy-start | bytes 2308
  870.5 10.8 %copy-start.19 = (f32[192]{0:T(256)S(1)}, f32[192]{0:T(256)}, u32[]{:S(2)}) copy-start(f32[192]{0:T(256)} %get-tuple-element.254) | copy-start | bytes 2308
  870.5 10.8 %copy-start.20 = (f32[192]{0:T(256)S(1)}, f32[192]{0:T(256)}, u32[]{:S(2)}) copy-start(f32[192]{0:T(256)} %get-tuple-element.289) | copy-start | bytes 2308
  870.5 10.8 %copy-start.24 = (f32[192]{0:T(256)S(1)}, f32[192]{0:T(256)}, u32[]{:S(2)}) copy-start(f32[192]{0:T(256)} %get-tuple-element.252) | copy-start | bytes 2308
  870.5 48.4 %all-to-all-start = ((bf16[8,1,24,576]{3,2,1,0:T(8,128)(2,1)}), bf16[8,1,24,576]{3,2,1,0:T(8,128)(2,1)S(1)}, u32[]{:S(2)}, u32[]{:S(2)}) async-start(bf16[8,1,24,576]{3,2,1,0:T(8,128)(2,1)} %bitcast.29), calls=%async_computation | async-start | bytes 491520 | tf_op jit(solution)/shard_map/all_to_all | solution.py:23
Sparse Core Ops, SparseCore 0:
  128.7 83.0 all-gather.2
  367.8 31.4 all-reduce.7
  450.6 31.1 all-reduce.5
  527.1 180.4 reduce-scatter.3
where the time goes:
time: 939 us; the launch traced here: 926 us
  matrix products  283 us (30%)
  blocking collectives  209 us (22%)
  waiting for transfers between devices  185 us (20%)
  local copies, waits for them, and re-layouts  126 us (13%)
  other arithmetic  84 us (9%)
  starting transfers between devices  23.3 us (2%)
  between operations  14.6 us (2%)
    unnamed x5, waiting for transfers between devices  115 us
    dot_general x4, matrix products, contract_rows(): lax.dot_general(left, right, (((0,), (0,)), ((), ())), preferred_element_...  94.6 us
    psum x2, waiting for transfers between devices, norm_back(): lax.psum((jnp.sum(scaled, axis=0), jnp.sum(scaled * normed, axis=0)), 'gr...  62.7 us
    dot_general x4, matrix products, contract_cols(): lax.dot_general(left, right, (((1,), (1,)), ((), ())), preferred_element_...  42.2 us
    unnamed x62, local copies, waits for them, and re-layouts  40 us
    psum x1, blocking collectives, per_device(): lax.psum((qv_sum[None], bout_sum, gain_one_sum, shift_one_sum, up_sum[Non...  37.6 us
    all_gather x1, blocking collectives, per_device(): lax.all_gather(down_weight.astype(jnp.bfloat16), 'dp', axis=1, tiled=True)  33 us
    all_gather x1, blocking collectives, per_device(): lax.all_gather(w_qkv.astype(jnp.bfloat16), 'dp', axis=1, tiled=True)  32.5 us
  transfers between devices with their start and end apart: 8, of which 4 were waited for; matrix products, arithmetic and copies ran while one was open for 5% of the time, Pallas kernels for 0%

commit v1 on v0

v1 whole, which is shorter than its diff:
```python
import functools
import math

import jax
import jax.numpy as jnp
from jax import lax
from jax.experimental import pallas as pl
from jax.experimental.pallas import tpu as pltpu
from jax.sharding import PartitionSpec as P

HD = 64
HG = 3
LANES = 128
SPLIT = 2
DELAY = 5

eps = 1e-12
f32 = jnp.float32
bf16 = jnp.bfloat16
MESH = pl.DeviceIdType.MESH


def mm(left, right):
    return jnp.dot(left, right, preferred_element_type=f32)


def mm_nt(left, right):
    return lax.dot_general(left, right, (((1,), (1,)), ((), ())), preferred_element_type=f32)


def mm_tn(left, right):
    return lax.dot_general(left, right, (((0,), (0,)), ((), ())), preferred_element_type=f32)


def row_sum(x):
    return jnp.sum(x, axis=0, keepdims=True)


def remote(src, dst, send, recv, device):
    return pltpu.make_async_remote_copy(
        src_ref=src, dst_ref=dst, send_sem=send, recv_sem=recv, device_id=device, device_id_type=MESH
    )


def gather_kernel(dp, groups, *refs):
    shards, fulls, out_rows = refs[:4], refs[4:8], refs[8]
    send, recv, send_rows, recv_rows, local_sem = refs[9:]
    d = lax.axis_index("dp")
    g = lax.axis_index("group")
    per = dp // groups
    for shard, full in zip(shards, fulls):
        full[d] = shard[...].astype(bf16)

    def column_copy(k, which, slot, peer):
        return remote(
            fulls[which].at[slot],
            fulls[which].at[slot],
            send.at[which, k],
            recv.at[which, k],
            {"dp": peer, "group": g},
        )

    def row_copy(k, source_d, source_g, peer, target):
        return remote(
            fulls[1].at[d],
            out_rows.at[lax.rem(source_d, per), source_g],
            send_rows.at[k],
            recv_rows.at[lax.rem(source_d, per), source_g],
            {"dp": peer, "group": target},
        )

    target = d // per
    for which in range(4):

        def start(k, carry):
            column_copy(k, which, d, lax.rem(d + k, dp)).start()
            return carry

        lax.fori_loop(1, dp, start, 0)

    def start_rows(k, carry):
        peer = lax.rem(d + k, dp)

        @pl.when(jnp.logical_or(k != 0, target != g))
        def _():
            row_copy(k, d, g, peer, target).start()

        return carry

    lax.fori_loop(0, dp, start_rows, 0)

    @pl.when(target == g)
    def _():
        copy = pltpu.make_async_copy(fulls[1].at[d], out_rows.at[lax.rem(d, per), g], local_sem)
        copy.start()
        copy.wait()

    for which in range(4):

        def finish(k, carry):
            column_copy(k, which, lax.rem(d - k + dp, dp), lax.rem(d + k, dp)).wait()
            return carry

        lax.fori_loop(1, dp, finish, 0)

    def finish_rows(k, carry):
        @pl.when(jnp.logical_or(k != 0, target != g))
        def _():
            row_copy(k, d, g, lax.rem(d + k, dp), target).wait_send()

        return carry

    lax.fori_loop(0, dp, finish_rows, 0)
    for source in range(groups):

        def arrive(k, carry):
            source_d = g * per + k

            @pl.when(jnp.logical_or(source_d != d, source != g))
            def _():
                row_copy(k, source_d, source, d, g).wait_recv()

            return carry

        lax.fori_loop(0, per, arrive, 0)


def gather_weights(w_qkv, w_out, w_up, down_weight):
    dp = lax.axis_size("dp")
    groups = lax.axis_size("group")
    shards = (w_qkv, w_out, w_up, down_weight)
    full_shapes = tuple(jax.ShapeDtypeStruct((dp, *w.shape), bf16) for w in shards)
    rows_shape = jax.ShapeDtypeStruct((dp // groups, groups, *w_out.shape), bf16)
    vmem = pl.BlockSpec(memory_space=pltpu.VMEM)
    return pl.pallas_call(
        functools.partial(gather_kernel, dp, groups),
        out_shape=(*full_shapes, rows_shape),
        in_specs=[vmem] * 4,
        out_specs=tuple([vmem] * 5),
        scratch_shapes=[
            pltpu.SemaphoreType.DMA((4, dp)),
            pltpu.SemaphoreType.DMA((4, dp)),
            pltpu.SemaphoreType.DMA((dp,)),
            pltpu.SemaphoreType.DMA((dp // groups, groups)),
            pltpu.SemaphoreType.DMA,
        ],
        compiler_params=pltpu.CompilerParams(has_side_effects=True, vmem_limit_bytes=48 << 20),
        name="gather_weights",
    )(*shards)


def scatter_kernel(dp, *refs):
    grads, outs, sums_out = refs[:4], refs[5:9], refs[9]
    sums = refs[4]
    staged, landed = refs[10:14], refs[14:18]
    sums_all, send, recv = refs[18:]
    d = lax.axis_index("dp")
    g = lax.axis_index("group")
    for grad, stage in zip(grads, staged):
        stage[...] = grad[...].astype(bf16)
    total = jnp.sum(sums[...], axis=-1)
    sums_all[d] = total

    def copies(k, slot_from, slot_to, peer):
        device = {"dp": peer, "group": g}
        made = [
            remote(staged[w].at[slot_from], landed[w].at[slot_to], send.at[w, k], recv.at[w, k], device)
            for w in range(4)
        ]
        made.append(
            remote(sums_all.at[slot_to], sums_all.at[slot_to], send.at[4, k], recv.at[4, k], device)
        )
        return made

    def start(k, carry):
        peer = lax.rem(d + k, dp)
        for copy in copies(k, peer, d, peer):
            copy.start()
        return carry

    lax.fori_loop(1, dp, start, 0)
    for w in range(4):
        outs[w][...] = staged[w][d].astype(f32)

    def finish(k, carry):
        source = lax.rem(d - k + dp, dp)
        for copy in copies(k, lax.rem(d + k, dp), source, lax.rem(d + k, dp)):
            copy.wait()
        for w in range(4):
            outs[w][...] += landed[w][source].astype(f32)
        return carry

    lax.fori_loop(1, dp, finish, 0)
    sums_out[...] = jnp.sum(sums_all[...], axis=0)


def scatter_grads(grads, sums):
    dp = lax.axis_size("dp")
    vmem = pl.BlockSpec(memory_space=pltpu.VMEM)
    cut = tuple(g.reshape(dp, g.shape[0] // dp, g.shape[1]) for g in grads)
    sums = sums.reshape(-1, LANES, LANES)
    return pl.pallas_call(
        functools.partial(scatter_kernel, dp),
        out_shape=(
            *(jax.ShapeDtypeStruct(c.shape[1:], f32) for c in cut),
            jax.ShapeDtypeStruct(sums.shape[:2], f32),
        ),
        in_specs=[vmem] * 5,
        out_specs=tuple([vmem] * 5),
        scratch_shapes=[
            *(pltpu.VMEM(c.shape, bf16) for c in cut),
            *(pltpu.VMEM(c.shape, bf16) for c in cut),
            pltpu.VMEM((dp, *sums.shape[:2]), f32),
            pltpu.SemaphoreType.DMA((5, dp)),
            pltpu.SemaphoreType.DMA((5, dp)),
        ],
        compiler_params=pltpu.CompilerParams(has_side_effects=True, vmem_limit_bytes=48 << 20),
        name="scatter_grads",
    )(*cut, sums)


def layer_kernel(
    rows,
    groups,
    place,
    inp,
    gout_in,
    wqkv_t,
    wqkv,
    wout_t,
    wout_rows,
    wup_t,
    wup,
    wdown_t,
    wdown,
    b_qkv,
    b_up,
    cols,
    result,
    grad_in,
    g_qkv,
    g_out,
    g_up,
    g_down,
    sums,
    ctx_all,
    att_all,
    stat_one,
    stat_two,
    sum_one,
    x_ring,
    mix_ring,
    prob_ring,
    mask,
    x_one,
    n_one,
    inv_one,
    hid,
    hid_low,
    pre,
    act,
    slope,
    x_two,
    upstream,
    res,
    rtg,
    br_low,
    pre_low,
    hid_grad,
    rog_ring,
    ctx_grad,
    mix_grad,
    send_blocks,
    recv_blocks,
    send_stats,
    recv_stats,
):
    i = pl.program_id(0)
    steps = pl.num_programs(0)
    g = lax.axis_index("group")
    across = lax.rem(g + 2, groups)
    beside = g + 1 - 2 * lax.rem(g, 2)
    corner = lax.rem(beside + 2, groups)
    local, seq = inp.shape
    half = seq // SPLIT
    channels = local * groups
    parts = seq // LANES
    hidden_units = wup_t.shape[0]
    ring = x_ring.shape[0]
    lanes = [slice(k * LANES, (k + 1) * LANES) for k in range(parts)]
    col = lambda n: cols[n * local : (n + 1) * local, :]
    B_OUT, GAIN1, SHIFT1, B_DOWN, GAIN2, SHIFT2 = range(6)
    S_BOUT, S_GAIN1, S_SHIFT1, S_BDOWN, S_GAIN2, S_SHIFT2 = range(6)

    def accumulate(slot, chunk):
        sums[slot * local : (slot + 1) * local, :] += chunk

    def block_copy(buf, base, kind, r, slot):
        peer = across if kind == 0 else beside
        return remote(
            buf.at[r, slot],
            buf.at[r, slot],
            send_blocks.at[base + kind, r],
            recv_blocks.at[base + kind, r],
            {"group": peer},
        )

    def send_own(buf, base, r):
        block_copy(buf, base, 0, r, g).start()
        block_copy(buf, base, 1, r, g).start()

    def pass_on(buf, base, r):
        block_copy(buf, base, 0, r, across).wait_recv()
        block_copy(buf, base, 2, r, across).start()

    def blocks_ready(buf, base, r):
        block_copy(buf, base, 1, r, beside).wait_recv()
        block_copy(buf, base, 2, r, corner).wait_recv()

    def blocks_sent(buf, base, r):
        block_copy(buf, base, 0, r, g).wait_send()
        block_copy(buf, base, 1, r, g).wait_send()
        block_copy(buf, base, 2, r, across).wait_send()

    def stat_copy(buf, base, offset, r, slot):
        return remote(
            buf.at[r, slot],
            buf.at[r, slot],
            send_stats.at[base + offset - 1, r],
            recv_stats.at[base + offset - 1, r],
            {"group": lax.rem(g + offset, groups)},
        )

    def send_stat(buf, base, r):
        for offset in range(1, groups):
            stat_copy(buf, base, offset, r, g).start()

    def stat_ready(buf, base, r):
        for offset in range(1, groups):
            stat_copy(buf, base, offset, r, lax.rem(g + groups - offset, groups)).wait_recv()

    def stat_sent(buf, base, r):
        for offset in range(1, groups):
            stat_copy(buf, base, offset, r, g).wait_send()

    CTX, ATT = 0, 3
    ONE, TWO, BACK = 0, groups - 1, 2 * (groups - 1)

    @pl.when(i == 0)
    def _():
        barrier = pltpu.get_barrier_semaphore()
        for offset in range(1, groups):
            pl.semaphore_signal(
                barrier, inc=1, device_id={"group": lax.rem(g + offset, groups)}, device_id_type=MESH
            )
        pl.semaphore_wait(barrier, groups - 1)
        for ref in (g_qkv, g_out, g_up, g_down, sums):
            ref[...] = jnp.zeros_like(ref)

    def stage_residual(r):
        blocks_ready(ctx_all, CTX, r)
        attended = mm(wout_t[...], ctx_all[r].reshape(channels, seq))
        xr = x_ring.at[lax.rem(r, ring)]
        for k, s in enumerate(lanes):
            x = xr[:, s].astype(f32) + attended[:, s] + col(B_OUT)
            x_one[:, s] = x
            mean = row_sum(x) * (1.0 / local)
            off = x - mean
            stat_one[r, g, k : k + 1, :] = mean
            stat_one[r, g, parts + k : parts + k + 1, :] = row_sum(off * off)
        send_stat(stat_one, ONE, r)

    def stage_attend(r):
        slot = lax.rem(r, ring)
        rolled = pltpu.roll(inp[...].astype(f32), place[r, 0], 1).astype(bf16)
        x_ring[slot] = rolled
        mixed = mm(wqkv_t[...], rolled)
        for s in lanes:
            mix_ring[slot, :, s] = (mixed[:, s] + b_qkv[...]).astype(bf16)
        first, second = place[r, 2], place[r, 3]
        down = lax.broadcasted_iota(jnp.int32, (half, half), 0)
        along = lax.broadcasted_iota(jnp.int32, (half, half), 1)
        own = lambda at: (at >= first).astype(jnp.int32) + (at >= second).astype(jnp.int32)
        mask[...] = jnp.where(own(down) == own(along), 0.0, -1000000000.0)
        scale = math.log2(math.e) / math.sqrt(HD)
        for h in range(HG):
            heads = slice(h * HD, (h + 1) * HD)
            keys = slice(local + h * HD, local + (h + 1) * HD)
            values = slice(2 * local + h * HD, 2 * local + (h + 1) * HD)
            for b in range(SPLIT):
                toks = slice(b * half, (b + 1) * half)
                scores = mm_tn(mix_ring[slot, keys, toks], mix_ring[slot, heads, toks])
                if b:
                    scores = scores + mask[...]
                highest = jnp.max(scores, axis=0, keepdims=True)
                exponent = jnp.exp2((scores - highest) * scale)
                chances = (exponent * (1.0 / row_sum(exponent))).astype(bf16)
                prob_ring[slot, h * SPLIT + b] = chances
                ctx_all[r, g, heads, toks] = mm(mix_ring[slot, values, toks], chances).astype(bf16)
        send_own(ctx_all, CTX, r)

    def stage_norm_back(r):
        stat_ready(sum_one, BACK, r)
        slot = lax.rem(r, rog_ring.shape[0])
        for k, s in enumerate(lanes):
            first = sum_one[r, 0, k : k + 1, :]
            second = sum_one[r, 0, parts + k : parts + k + 1, :]
            for p in range(1, groups):
                first += sum_one[r, p, k : k + 1, :]
                second += sum_one[r, p, parts + k : parts + k + 1, :]
            first = first * (1.0 / channels)
            second = second * (1.0 / channels)
            scaled = hid_grad[:, s] * col(GAIN1)
            back = inv_one[k : k + 1, :] * (scaled - first - n_one[:, s] * second)
            rog_ring[slot, :, s] = back
            low = back.astype(bf16)
            att_all[r, g, :, s] = low
            accumulate(S_BOUT, low.astype(f32))
        send_own(att_all, ATT, r)
        g_out[...] += mm_nt(ctx_all[r].reshape(channels, seq), att_all[r, g])

    def stage_feed(r):
        stat_ready(stat_one, ONE, r)
        for k, s in enumerate(lanes):
            means = [stat_one[r, p, k : k + 1, :] for p in range(groups)]
            center = sum(means[1:], means[0]) * (1.0 / groups)
            spread = stat_one[r, 0, parts + k : parts + k + 1, :]
            for p in range(1, groups):
                spread += stat_one[r, p, parts + k : parts + k + 1, :]
            for mean in means:
                spread += local * (mean - center) * (mean - center)
            inverse = lax.rsqrt(spread * (1.0 / channels) + eps)
            inv_one[k : k + 1, :] = inverse
            normed = (x_one[:, s] - center) * inverse
            n_one[:, s] = normed
            h = normed * col(GAIN1) + col(SHIFT1)
            hid[:, s] = h
            hid_low[:, s] = h.astype(bf16)
        pre[...] = mm(wup_t[...], hid_low[...])
        for j in range(hidden_units // local):
            units = slice(j * local, (j + 1) * local)
            for s in lanes:
                u = pre[units, s] + b_up[units, :]
                cdf = 0.5 + 0.5 * lax.erf(u * math.sqrt(0.5))
                act[units, s] = (u * cdf).astype(bf16)
                bell = jnp.exp2(u * u * (-0.5 * math.log2(math.e))) * (1.0 / math.sqrt(2.0 * math.pi))
                slope[units, s] = cdf + u * bell
        branch = mm(wdown_t[...], act[...])
        upstream[...] = pltpu.roll(gout_in[...].astype(f32), place[r, 0], 1)
        for k, s in enumerate(lanes):
            x = hid[:, s] + branch[:, s] + col(B_DOWN)
            x_two[:, s] = x
            mean = row_sum(x) * (1.0 / local)
            off = x - mean
            scaled = upstream[:, s] * col(GAIN2)
            tile = (mean, row_sum(off * off), row_sum(scaled), row_sum(scaled * off))
            for n, value in enumerate(tile):
                stat_two[r, g, n * parts + k : n * parts + k + 1, :] = value
        send_stat(stat_two, TWO, r)

    def stage_attend_back(r):
        slot = lax.rem(r, ring)
        blocks_ready(att_all, ATT, r)
        ctx_grad[...] = mm(wout_rows[...], att_all[r].reshape(channels, seq)).astype(bf16)
        factor = 1.0 / math.sqrt(HD)
        for h in range(HG):
            heads = slice(h * HD, (h + 1) * HD)
            keys = slice(local + h * HD, local + (h + 1) * HD)
            values = slice(2 * local + h * HD, 2 * local + (h + 1) * HD)
            for b in range(SPLIT):
                toks = slice(b * half, (b + 1) * half)
                incoming = ctx_grad[heads, toks]
                chances = prob_ring[slot, h * SPLIT + b]
                prob_grad = mm_tn(mix_ring[slot, values, toks], incoming)
                inner = row_sum(incoming.astype(f32) * ctx_all[r, g, heads, toks].astype(f32))
                score_grad = (chances.astype(f32) * (prob_grad - inner)).astype(bf16)
                mix_grad[values, toks] = mm_nt(incoming, chances).astype(bf16)
                mix_grad[heads, toks] = (mm(mix_ring[slot, keys, toks], score_grad) * factor).astype(bf16)
                mix_grad[keys, toks] = (mm_nt(mix_ring[slot, heads, toks], score_grad) * factor).astype(bf16)
        g_qkv[...] += mm_nt(mix_grad[...], x_ring[slot])
        total = mm(wqkv[...], mix_grad[...]) + rog_ring[lax.rem(r, rog_ring.shape[0])]
        grad_in[...] = pltpu.roll(total, place[r, 1], 1)
        base = 6 * local + hidden_units
        for n, start in ((0, 0), (1, 2 * local)):
            chunk = mix_grad[start : start + local, lanes[0]].astype(f32)
            for s in lanes[1:]:
                chunk += mix_grad[start : start + local, s].astype(f32)
            sums[base + n * local : base + (n + 1) * local, :] += chunk

    def stage_feed_back(r):
        stat_ready(stat_two, TWO, r)
        for k, s in enumerate(lanes):
            row = lambda p, n: stat_two[r, p, n * parts + k : n * parts + k + 1, :]
            means = [row(p, 0) for p in range(groups)]
            center = sum(means[1:], means[0]) * (1.0 / groups)
            spread, first, second = row(0, 1), row(0, 2), row(0, 3)
            for p in range(1, groups):
                spread += row(p, 1)
                first += row(p, 2)
                second += row(p, 3)
            for p, mean in enumerate(means):
                spread += local * (mean - center) * (mean - center)
                second += (mean - center) * row(p, 2)
            inverse = lax.rsqrt(spread * (1.0 / channels) + eps)
            first = first * (1.0 / channels)
            second = second * inverse * (1.0 / channels)
            normed = (x_two[:, s] - center) * inverse
            res[:, s] = normed * col(GAIN2) + col(SHIFT2)
            up = upstream[:, s]
            back = inverse * (up * col(GAIN2) - first - normed * second)
            rtg[:, s] = back
            low = back.astype(bf16)
            br_low[:, s] = low
            accumulate(S_GAIN2, up * normed)
            accumulate(S_SHIFT2, up)
            accumulate(S_BDOWN, low.astype(f32))
        result[...] = pltpu.roll(res[...], place[r, 1], 1).astype(bf16)
        pre[...] = mm(wdown[...], br_low[...])
        g_down[...] += mm_nt(act[...], br_low[...])
        base = 6 * local
        for j in range(hidden_units // local):
            units = slice(j * local, (j + 1) * local)
            for s in lanes:
                low = (slope[units, s] * pre[units, s]).astype(bf16)
                pre_low[units, s] = low
                sums[base + j * local : base + (j + 1) * local, :] += low.astype(f32)
        g_up[...] += mm_nt(pre_low[...], hid_low[...])
        change = mm(wup[...], pre_low[...])
        for k, s in enumerate(lanes):
            total = rtg[:, s] + change[:, s]
            hid_grad[:, s] = total
            normed = n_one[:, s]
            scaled = total * col(GAIN1)
            sum_one[r, g, k : k + 1, :] = row_sum(scaled)
            sum_one[r, g, parts + k : parts + k + 1, :] = row_sum(scaled * normed)
            accumulate(S_GAIN1, total * normed)
            accumulate(S_SHIFT1, total)
        send_stat(sum_one, BACK, r)

    def at(delay, stage):
        r = i - delay

        @pl.when(jnp.logical_and(r >= 0, r < rows))
        def _():
            stage(r)

    at(2, stage_residual)
    at(0, stage_attend)
    at(3, stage_norm_back)
    at(2, stage_feed)
    at(DELAY, stage_attend_back)
    at(1, lambda r: pass_on(ctx_all, CTX, r))
    at(4, lambda r: pass_on(att_all, ATT, r))
    at(2, stage_feed_back)

    @pl.when(i == steps - 1)
    def _():
        def drain(r, carry):
            blocks_sent(ctx_all, CTX, r)
            blocks_sent(att_all, ATT, r)
            stat_sent(stat_one, ONE, r)
            stat_sent(stat_two, TWO, r)
            stat_sent(sum_one, BACK, r)
            return carry

        lax.fori_loop(0, rows, drain, 0)


def run_layer(place, inputs, grad_out, mats, b_qkv, b_up, cols):
    groups = lax.axis_size("group")
    local, tok_count = inputs.shape
    rows = place.shape[0]
    seq = tok_count // rows
    half = seq // SPLIT
    parts = seq // LANES
    units = b_up.shape[0]
    last = rows - 1
    ring = DELAY + 1
    vmem = pl.BlockSpec(memory_space=pltpu.VMEM)

    def rows_at(delay):
        return pl.BlockSpec((local, seq), lambda i: (0, jnp.clip(i - delay, 0, last)))

    def whole(shape):
        return pl.BlockSpec(shape, lambda i: (0,) * len(shape))

    acc_shapes = ((3 * local, local), (groups * local, local), (units, local), (units, local))
    sums_shape = (6 * local + units + 2 * local, LANES)
    block = (rows, groups, local, seq)
    return pl.pallas_call(
        functools.partial(layer_kernel, rows, groups),
        grid=(rows + DELAY,),
        out_shape=(
            jax.ShapeDtypeStruct((local, tok_count), bf16),
            jax.ShapeDtypeStruct((local, tok_count), f32),
            *(jax.ShapeDtypeStruct(s, f32) for s in acc_shapes),
            jax.ShapeDtypeStruct(sums_shape, f32),
        ),
        in_specs=[
            pl.BlockSpec(memory_space=pltpu.SMEM),
            rows_at(0),
            rows_at(2),
            *([vmem] * (len(mats) + 3)),
        ],
        out_specs=(
            rows_at(2),
            rows_at(DELAY),
            *(whole(s) for s in acc_shapes),
            whole(sums_shape),
        ),
        scratch_shapes=[
            pltpu.VMEM(block, bf16),
            pltpu.VMEM(block, bf16),
            pltpu.VMEM((rows, groups, 2 * parts, LANES), f32),
            pltpu.VMEM((rows, groups, 4 * parts, LANES), f32),
            pltpu.VMEM((rows, groups, 2 * parts, LANES), f32),
            pltpu.VMEM((ring, local, seq), bf16),
            pltpu.VMEM((ring, 3 * local, seq), bf16),
            pltpu.VMEM((ring, HG * SPLIT, half, half), bf16),
            pltpu.VMEM((half, half), f32),
            pltpu.VMEM((local, seq), f32),
            pltpu.VMEM((local, seq), f32),
            pltpu.VMEM((parts, LANES), f32),
            pltpu.VMEM((local, seq), f32),
            pltpu.VMEM((local, seq), bf16),
            pltpu.VMEM((units, seq), f32),
            pltpu.VMEM((units, seq), bf16),
            pltpu.VMEM((units, seq), f32),
            pltpu.VMEM((local, seq), f32),
            pltpu.VMEM((local, seq), f32),
            pltpu.VMEM((local, seq), f32),
            pltpu.VMEM((local, seq), f32),
            pltpu.VMEM((local, seq), bf16),
            pltpu.VMEM((units, seq), bf16),
            pltpu.VMEM((local, seq), f32),
            pltpu.VMEM((3, local, seq), f32),
            pltpu.VMEM((local, seq), bf16),
            pltpu.VMEM((3 * local, seq), bf16),
            pltpu.SemaphoreType.DMA((6, rows)),
            pltpu.SemaphoreType.DMA((6, rows)),
            pltpu.SemaphoreType.DMA((3 * (groups - 1), rows)),
            pltpu.SemaphoreType.DMA((3 * (groups - 1), rows)),
        ],
        compiler_params=pltpu.CompilerParams(
            collective_id=0, has_side_effects=True, vmem_limit_bytes=60 << 20
        ),
        name="layer",
    )(place, inputs, grad_out, *mats, b_qkv, b_up, cols)


def row_places(labels):
    seq = labels.shape[1]
    half = seq // SPLIT
    counts = [jnp.sum((labels == v).astype(jnp.int32), axis=1) for v in range(4)]
    start = jnp.zeros_like(counts[0])
    first = jnp.zeros_like(start)
    second = jnp.zeros_like(start)
    found = jnp.zeros_like(start)
    begin = jnp.zeros_like(start)
    for v in range(4):
        hit = jnp.where(counts[v] == half, 1 - found, 0)
        start = start + hit * begin
        first = first + hit * counts[(v + 1) % 4]
        second = second + hit * (counts[(v + 1) % 4] + counts[(v + 2) % 4])
        found = found + hit
        begin = begin + counts[v]
    return jnp.stack([(seq - start) % seq, start, first, second], axis=1)


def per_device(
    inputs,
    labels,
    w_qkv,
    b_qv,
    w_out,
    b_out,
    gain_one,
    shift_one,
    w_up,
    b_up,
    down_weight,
    down_bias,
    gain_two,
    shift_two,
    grad_out,
):
    groups = lax.axis_size("group")
    local = inputs.shape[0]
    units = b_up.shape[1]
    channels = local * groups
    gathered = gather_weights(w_qkv[0], w_out, w_up[0], down_weight[0])
    mat_qkv = gathered[0].reshape(local, 3 * local)
    mat_out = gathered[1].reshape(channels, local)
    mat_up = gathered[2].reshape(local, units)
    mat_down = gathered[3].reshape(units, local)
    out_rows = jnp.swapaxes(gathered[4], 1, 2).reshape(local, channels)
    mats = (
        mat_qkv.T,
        mat_qkv,
        mat_out.T,
        out_rows,
        mat_up.T,
        mat_up,
        mat_down.T,
        mat_down,
    )
    wide = lambda v: jnp.broadcast_to(v[:, None], (v.shape[0], LANES))
    key_zero = jnp.zeros((local,), f32)
    qkv_bias = jnp.concatenate([b_qv[0, :local], key_zero, b_qv[0, local:]])
    cols = jnp.concatenate([b_out, gain_one, shift_one, down_bias[0], gain_two, shift_two])
    result, input_grad, qkv_t, out_grad, up_t, down_grad, sums = run_layer(
        row_places(labels), inputs, grad_out, mats, wide(qkv_bias), wide(b_up[0]), wide(cols)
    )
    grads = scatter_grads((qkv_t.T, out_grad, up_t.T, down_grad), sums)
    flat = grads[4].reshape(-1)
    piece = lambda n: flat[n * local : (n + 1) * local]
    base = 6 * local
    return (
        result,
        input_grad,
        grads[0][None],
        flat[base + units :][None],
        grads[1],
        piece(0),
        piece(1),
        piece(2),
        grads[2][None],
        flat[base : base + units][None],
        grads[3][None],
        piece(3)[None],
        piece(4),
        piece(5),
    )


def solution(mesh):
    placed = (
        P("group", "dp"),
        P("dp", None),
        P("group", "dp", None),
        P("group", None),
        P("dp", "group"),
        P("group"),
        P("group"),
        P("group"),
        P("group", "dp", None),
        P("group", None),
        P("group", "dp", None),
        P("group", None),
        P("group"),
        P("group"),
        P("group", "dp"),
    )
    return jax.shard_map(
        per_device,
        mesh=mesh,
        in_specs=placed,
        out_specs=(
            P("group", "dp"),
            P("group", "dp"),
            P("group", "dp", None),
            P("group", None),
            P("dp", "group"),
            P("group"),
            P("group"),
            P("group"),
            P("group", "dp", None),
            P("group", None),
            P("group", "dp", None),
            P("group", None),
            P("group"),
            P("group"),
        ),
        check_vma=False,
    )
```

time: 939 us -> 375 us (0.40)
  the two profiles are of different devices: /device:TPU:0 before, /device:TPU:12 now
where the time goes in v1:
time: 375 us; the launch traced here: 374 us
  Pallas kernels  342 us (91%)
  local copies, waits for them, and re-layouts  29.7 us (8%)
    pallas_call x1, Pallas kernels, run_layer(): pl.pallas_call(functools.partial(layer_kernel, rows, groups), grid=(rows...  260 us
    pallas_call x1, Pallas kernels, gather_weights(): pl.pallas_call(functools.partial(gather_kernel, dp, groups), out_shape=(*...  44.1 us
    pallas_call x1, Pallas kernels, scatter_grads(): pl.pallas_call(functools.partial(scatter_kernel, dp), out_shape=(*(jax.Sh...  37.6 us
    unnamed x34, local copies, waits for them, and re-layouts  16.1 us

profile of v1, /device:TPU:12, one launch (start us, length us, event | category | flops | bytes accessed | tf_op | source)
XLA Modules:
  0.0 374.2 jit_solution(13614580979215324314)
XLA Ops:
  0.6 0.9 convert_reduce_fusion.3
  1.6 0.8 fusion.14
  2.4 0.1 pad_maximum_fusion
  2.5 0.7 reduce
  3.2 0.7 copy.56.place
  3.9 0.8 concatenate.7
  4.7 0.9 broadcast_in_dim.49.b_qkv
  5.6 0.9 broadcast_in_dim.51.b_up
  6.5 1.0 broadcast_in_dim.52.cols
  7.5 0.0 copy-start.6
  7.5 0.9 copy-done.6
  8.4 0.0 copy-start.7
  8.4 0.9 copy-done.7
  9.3 0.0 copy-start.8
  9.3 0.9 copy-done.8
  10.2 0.0 copy-start.9
  10.2 0.8 copy-done.9
  11.0 44.1 %gather_weights.1 = (bf16[8,24,576]{2,1,0:T(8,128)(2,1)S(1)}, bf16[8,96,192]{2,1,0:T(8,128)(2,1)S(1)}, bf16[8,24,768]{2,1,0:T(8,128)(2,1)S(1)}, bf16[8,96,192]{2...) custom-call(f32[24,576]{1,0:T(8,128)S(1)} %bitcast.159, f32[96,192]{1,0:T(8,128)S(1)} %copy-done.6, f32[24,768]{1,0:T(8,128)S(1)} %bitcast.158, ...), custom_call_target="tpu_custom_call" | custom-call | tf_op jit(solution)/shard_map/gather_weights/pallas_call | solution.py:135
  55.2 0.0 copy-start
  55.2 0.0 copy-start.1
  55.2 0.0 copy-start.3
  55.2 1.0 copy.62
  56.2 0.3 copy.55
  56.5 1.1 reshape.281.wout_rows
  57.6 0.9 copy.59.wdown_t
  58.4 0.9 copy.57.wqkv_t
  59.3 0.9 copy.58.wup_t
  60.2 0.0 copy-done
  60.2 0.0 copy-done.1
  60.2 0.0 copy-done.3
  60.2 260.3 %layer.1 = (bf16[192,8192]{1,0:T(8,128)(2,1)}, f32[192,8192]{1,0:T(8,128)}, f32[576,192]{1,0:T(8,128)}, f32[768,192]{1,0:T(8,128)}, f32[768,192]{1,0:T(8,128)}, /*index=5*/f32[768,192]{1,0:T(8,128)}, f32[2304,128]{1,0:T(8,128)}) custom-call(s32[16,4]{1,0:T(8,128)} %copy.56.place, bf16[192,8192]{1,0:T(8,128)(2,1)} %inp.1, bf16[192,8192]{1,0:T(8,128)(2,1)} %gout_in.1, ...), custom_call_target="tpu_custom_call" | custom-call | tf_op jit(solution)/shard_map/layer/pallas_call | solution.py:590
  320.6 0.0 copy-start.2
  320.6 1.4 copy.60
  322.0 1.4 copy.61
  323.4 0.0 copy-done.2
  323.4 0.0 copy-start.4
  323.4 1.1 copy-done.4
  324.5 0.0 copy-start.5
  324.5 1.1 copy-done.5
  325.6 0.0 copy-start.11
  325.6 37.6 %scatter_grads.1 = (f32[24,576]{1,0:T(8,128)S(1)}, f32[96,192]{1,0:T(8,128)S(1)}, f32[24,768]{1,0:T(8,128)S(1)}, f32[96,192]{1,0:T(8,128)S(1)}, f32[18,128]{1,0:T(8,128)S(1)}) custom-call(f32[8,24,576]{2,1,0:T(8,128)S(1)} %bitcast.143, f32[8,96,192]{2,1,0:T(8,128)S(1)} %bitcast.151, f32[8,24,768]{2,1,0:T(8,128)S(1)} %bitcast.142, ...), custom_call_target="tpu_custom_call" | custom-call | tf_op jit(solution)/shard_map/scatter_grads/pallas_call | solution.py:202
  363.2 0.6 copy.68
  363.8 0.6 copy.67
  364.4 0.6 fusion.13
  365.0 0.0 copy-done.11
  365.0 0.0 copy-start.10
  365.0 1.7 copy.75
  366.7 2.2 copy-done.10
  369.0 2.7 copy.76
  371.7 0.6 copy.77
  372.3 0.6 copy.78
  372.9 0.6 copy.79
  373.6 0.6 copy.80
  (5 shorter events, 0.0 us)
Async XLA Ops:
  7.5 0.9 copy-start.6
  8.4 0.9 copy-start.7
  9.3 0.9 copy-start.8
  10.2 0.8 copy-start.9
  55.2 5.1 %copy-start = (bf16[8,96,192]{2,1,0:T(8,128)(2,1)}, bf16[8,96,192]{2,1,0:T(8,128)(2,1)S(1)}, u32[]{:S(2)}) copy-start(bf16[8,96,192]{2,1,0:T(8,128)(2,1)S(1)} %get-tuple-element.35) | copy-start | bytes 884740
  55.2 5.1 %copy-start.1 = (bf16[8,24,768]{2,1,0:T(8,128)(2,1)}, bf16[8,24,768]{2,1,0:T(8,128)(2,1)S(1)}, u32[]{:S(2)}) copy-start(bf16[8,24,768]{2,1,0:T(8,128)(2,1)S(1)} %get-tuple-element.34) | copy-start | bytes 884740
  55.2 5.1 %copy-start.3 = (bf16[8,24,576]{2,1,0:T(8,128)(2,1)}, bf16[8,24,576]{2,1,0:T(8,128)(2,1)S(1)}, u32[]{:S(2)}) copy-start(bf16[8,24,576]{2,1,0:T(8,128)(2,1)S(1)} %get-tuple-element.31) | copy-start | bytes 663556
  320.6 2.8 copy-start.2
  323.4 1.1 copy-start.4
  324.5 1.1 copy-start.5
  325.6 39.4 %copy-start.11 = (bf16[192,8192]{1,0:T(8,128)(2,1)S(1)}, bf16[192,8192]{1,0:T(8,128)(2,1)}, u32[]{:S(2)}) copy-start(bf16[192,8192]{1,0:T(8,128)(2,1)} %get-tuple-element.78) | copy-start | bytes 9437188
  365.0 3.9 %copy-start.10 = (f32[192,8192]{1,0:T(8,128)S(1)}, f32[192,8192]{1,0:T(8,128)}, u32[]{:S(2)}) copy-start(f32[192,8192]{1,0:T(8,128)} %get-tuple-element.79) | copy-start | bytes 18874372

commit v2 on v1

--- a/solution.py
+++ b/solution.py
@@ -12,7 +12,7 @@
 HG = 3
 LANES = 128
 SPLIT = 2
-DELAY = 5
+DELAY = 7
 
 eps = 1e-12
 f32 = jnp.float32
@@ -42,189 +42,27 @@
     )
 
 
-def gather_kernel(dp, groups, *refs):
-    shards, fulls, out_rows = refs[:4], refs[4:8], refs[8]
-    send, recv, send_rows, recv_rows, local_sem = refs[9:]
-    d = lax.axis_index("dp")
-    g = lax.axis_index("group")
-    per = dp // groups
-    for shard, full in zip(shards, fulls):
-        full[d] = shard[...].astype(bf16)
-
-    def column_copy(k, which, slot, peer):
-        return remote(
-            fulls[which].at[slot],
-            fulls[which].at[slot],
-            send.at[which, k],
-            recv.at[which, k],
-            {"dp": peer, "group": g},
-        )
-
-    def row_copy(k, source_d, source_g, peer, target):
-        return remote(
-            fulls[1].at[d],
-            out_rows.at[lax.rem(source_d, per), source_g],
-            send_rows.at[k],
-            recv_rows.at[lax.rem(source_d, per), source_g],
-            {"dp": peer, "group": target},
-        )
-
-    target = d // per
-    for which in range(4):
-
-        def start(k, carry):
-            column_copy(k, which, d, lax.rem(d + k, dp)).start()
-            return carry
-
-        lax.fori_loop(1, dp, start, 0)
-
-    def start_rows(k, carry):
-        peer = lax.rem(d + k, dp)
-
-        @pl.when(jnp.logical_or(k != 0, target != g))
-        def _():
-            row_copy(k, d, g, peer, target).start()
-
-        return carry
-
-    lax.fori_loop(0, dp, start_rows, 0)
-
-    @pl.when(target == g)
-    def _():
-        copy = pltpu.make_async_copy(fulls[1].at[d], out_rows.at[lax.rem(d, per), g], local_sem)
-        copy.start()
-        copy.wait()
-
-    for which in range(4):
-
-        def finish(k, carry):
-            column_copy(k, which, lax.rem(d - k + dp, dp), lax.rem(d + k, dp)).wait()
-            return carry
-
-        lax.fori_loop(1, dp, finish, 0)
-
-    def finish_rows(k, carry):
-        @pl.when(jnp.logical_or(k != 0, target != g))
-        def _():
-            row_copy(k, d, g, lax.rem(d + k, dp), target).wait_send()
-
-        return carry
-
-    lax.fori_loop(0, dp, finish_rows, 0)
-    for source in range(groups):
-
-        def arrive(k, carry):
-            source_d = g * per + k
-
-            @pl.when(jnp.logical_or(source_d != d, source != g))
-            def _():
-                row_copy(k, source_d, source, d, g).wait_recv()
-
-            return carry
-
-        lax.fori_loop(0, per, arrive, 0)
-
-
-def gather_weights(w_qkv, w_out, w_up, down_weight):
-    dp = lax.axis_size("dp")
-    groups = lax.axis_size("group")
-    shards = (w_qkv, w_out, w_up, down_weight)
-    full_shapes = tuple(jax.ShapeDtypeStruct((dp, *w.shape), bf16) for w in shards)
-    rows_shape = jax.ShapeDtypeStruct((dp // groups, groups, *w_out.shape), bf16)
-    vmem = pl.BlockSpec(memory_space=pltpu.VMEM)
-    return pl.pallas_call(
-        functools.partial(gather_kernel, dp, groups),
-        out_shape=(*full_shapes, rows_shape),
-        in_specs=[vmem] * 4,
-        out_specs=tuple([vmem] * 5),
-        scratch_shapes=[
-            pltpu.SemaphoreType.DMA((4, dp)),
-            pltpu.SemaphoreType.DMA((4, dp)),
-            pltpu.SemaphoreType.DMA((dp,)),
-            pltpu.SemaphoreType.DMA((dp // groups, groups)),
-            pltpu.SemaphoreType.DMA,
-        ],
-        compiler_params=pltpu.CompilerParams(has_side_effects=True, vmem_limit_bytes=48 << 20),
-        name="gather_weights",
-    )(*shards)
-
-
-def scatter_kernel(dp, *refs):
-    grads, outs, sums_out = refs[:4], refs[5:9], refs[9]
-    sums = refs[4]
-    staged, landed = refs[10:14], refs[14:18]
-    sums_all, send, recv = refs[18:]
-    d = lax.axis_index("dp")
-    g = lax.axis_index("group")
-    for grad, stage in zip(grads, staged):
-        stage[...] = grad[...].astype(bf16)
-    total = jnp.sum(sums[...], axis=-1)
-    sums_all[d] = total
-
-    def copies(k, slot_from, slot_to, peer):
-        device = {"dp": peer, "group": g}
-        made = [
-            remote(staged[w].at[slot_from], landed[w].at[slot_to], send.at[w, k], recv.at[w, k], device)
-            for w in range(4)
-        ]
-        made.append(
-            remote(sums_all.at[slot_to], sums_all.at[slot_to], send.at[4, k], recv.at[4, k], device)
-        )
-        return made
-
-    def start(k, carry):
-        peer = lax.rem(d + k, dp)
-        for copy in copies(k, peer, d, peer):
-            copy.start()
-        return carry
-
-    lax.fori_loop(1, dp, start, 0)
-    for w in range(4):
-        outs[w][...] = staged[w][d].astype(f32)
-
-    def finish(k, carry):
-        source = lax.rem(d - k + dp, dp)
-        for copy in copies(k, lax.rem(d + k, dp), source, lax.rem(d + k, dp)):
-            copy.wait()
-        for w in range(4):
-            outs[w][...] += landed[w][source].astype(f32)
-        return carry
-
-    lax.fori_loop(1, dp, finish, 0)
-    sums_out[...] = jnp.sum(sums_all[...], axis=0)
-
-
-def scatter_grads(grads, sums):
-    dp = lax.axis_size("dp")
-    vmem = pl.BlockSpec(memory_space=pltpu.VMEM)
-    cut = tuple(g.reshape(dp, g.shape[0] // dp, g.shape[1]) for g in grads)
-    sums = sums.reshape(-1, LANES, LANES)
-    return pl.pallas_call(
-        functools.partial(scatter_kernel, dp),
-        out_shape=(
-            *(jax.ShapeDtypeStruct(c.shape[1:], f32) for c in cut),
-            jax.ShapeDtypeStruct(sums.shape[:2], f32),
-        ),
-        in_specs=[vmem] * 5,
-        out_specs=tuple([vmem] * 5),
-        scratch_shapes=[
-            *(pltpu.VMEM(c.shape, bf16) for c in cut),
-            *(pltpu.VMEM(c.shape, bf16) for c in cut),
-            pltpu.VMEM((dp, *sums.shape[:2]), f32),
-            pltpu.SemaphoreType.DMA((5, dp)),
-            pltpu.SemaphoreType.DMA((5, dp)),
-        ],
-        compiler_params=pltpu.CompilerParams(has_side_effects=True, vmem_limit_bytes=48 << 20),
-        name="scatter_grads",
-    )(*cut, sums)
-
-
 def layer_kernel(
     rows,
     groups,
+    dp,
     place,
     inp,
     gout_in,
+    w_qkv,
+    w_out,
+    w_up,
+    w_down,
+    b_qkv,
+    b_up,
+    cols,
+    result,
+    grad_in,
+    o_qkv,
+    o_out,
+    o_up,
+    o_down,
+    o_sums,
     wqkv_t,
     wqkv,
     wout_t,
@@ -233,16 +71,23 @@
     wup,
     wdown_t,
     wdown,
-    b_qkv,
-    b_up,
-    cols,
-    result,
-    grad_in,
+    all_qkv,
+    all_out,
+    all_up,
+    all_down,
+    out_rows,
+    wide_mat,
+    tall_mat,
     g_qkv,
     g_out,
     g_up,
     g_down,
     sums,
+    land_qkv,
+    land_out,
+    land_up,
+    land_down,
+    all_sums,
     ctx_all,
     att_all,
     stat_one,
@@ -262,7 +107,6 @@
     slope,
     x_two,
     upstream,
-    res,
     rtg,
     br_low,
     pre_low,
@@ -274,10 +118,17 @@
     recv_blocks,
     send_stats,
     recv_stats,
+    send_weights,
+    recv_weights,
+    send_rows,
+    recv_rows,
+    send_grads,
+    recv_grads,
 ):
     i = pl.program_id(0)
     steps = pl.num_programs(0)
     g = lax.axis_index("group")
+    d = lax.axis_index("dp")
     across = lax.rem(g + 2, groups)
     beside = g + 1 - 2 * lax.rem(g, 2)
     corner = lax.rem(beside + 2, groups)
@@ -346,6 +197,45 @@
     CTX, ATT = 0, 3
     ONE, TWO, BACK = 0, groups - 1, 2 * (groups - 1)
 
+    shards = (w_qkv, w_out, w_up, w_down)
+    fulls = (all_qkv, all_out, all_up, all_down)
+    QKV, OUT, UP, DOWN = range(4)
+
+    def weight_copy(which, k, slot):
+        full = fulls[which]
+        return remote(
+            full.at[slot],
+            full.at[slot],
+            send_weights.at[which, k],
+            recv_weights.at[which, k],
+            {"dp": lax.rem(d + k, dp)},
+        )
+
+    def each_peer(action):
+        def body(k, carry):
+            action(k)
+            return carry
+
+        lax.fori_loop(1, dp, body, 0)
+
+    def weights_ready(which, into):
+        each_peer(lambda k: weight_copy(which, k, lax.rem(d - k + dp, dp)).wait_recv())
+        full = fulls[which]
+        count, width = full.shape[1:]
+        for slot in range(dp):
+            into[slot * count : (slot + 1) * count, :width] = full[slot].astype(f32)
+
+    per = dp // groups
+
+    def rows_copy(offset, source, target):
+        return remote(
+            all_out.at[pl.ds(target * per, per)],
+            out_rows.at[source],
+            send_rows.at[offset - 1],
+            recv_rows.at[offset - 1],
+            {"group": target},
+        )
+
     @pl.when(i == 0)
     def _():
         barrier = pltpu.get_barrier_semaphore()
@@ -353,9 +243,90 @@
             pl.semaphore_signal(
                 barrier, inc=1, device_id={"group": lax.rem(g + offset, groups)}, device_id_type=MESH
             )
-        pl.semaphore_wait(barrier, groups - 1)
+        each_peer(
+            lambda k: pl.semaphore_signal(
+                barrier, inc=1, device_id={"dp": lax.rem(d + k, dp)}, device_id_type=MESH
+            )
+        )
+        for shard, full in zip(shards, fulls):
+            full[d] = shard[...].astype(bf16)
+        pl.semaphore_wait(barrier, groups - 1 + dp - 1)
+        for which in range(4):
+            each_peer(lambda k, which=which: weight_copy(which, k, d).start())
         for ref in (g_qkv, g_out, g_up, g_down, sums):
             ref[...] = jnp.zeros_like(ref)
+        weights_ready(QKV, wide_mat)
+        mat = wide_mat[:, : 3 * local]
+        wqkv[...] = mat.astype(bf16)
+        wqkv_t[...] = mat.T.astype(bf16)
+
+    @pl.when(i == 2)
+    def _():
+        weights_ready(OUT, tall_mat)
+        for offset in range(1, groups):
+            rows_copy(offset, g, lax.rem(g + offset, groups)).start()
+        out_rows[g] = all_out[pl.ds(g * per, per)]
+        wout_t[...] = tall_mat[...].T.astype(bf16)
+
+    @pl.when(i == 3)
+    def _():
+        weights_ready(UP, wide_mat)
+        mat = wide_mat[...]
+        wup[...] = mat.astype(bf16)
+        wup_t[...] = mat.T.astype(bf16)
+        weights_ready(DOWN, tall_mat)
+        mat = tall_mat[...]
+        wdown[...] = mat.astype(bf16)
+        wdown_t[...] = mat.T.astype(bf16)
+
+    @pl.when(i == DELAY)
+    def _():
+        for offset in range(1, groups):
+            rows_copy(offset, lax.rem(g + groups - offset, groups), g).wait_recv()
+        count = local // per
+        for p in range(groups):
+            for n in range(per):
+                wide_mat[n * count : (n + 1) * count, :local] = out_rows[p, n].astype(f32)
+            tall_mat[p * local : (p + 1) * local, :] = wide_mat[:, :local].T
+        wout_rows[...] = tall_mat[...].T.astype(bf16)
+
+    stages = fulls
+    lands = (land_qkv, land_out, land_up, land_down)
+
+    def grad_copy(which, k, slot):
+        return remote(
+            stages[which].at[lax.rem(d + k, dp)],
+            lands[which].at[slot],
+            send_grads.at[which, k],
+            recv_grads.at[which, k],
+            {"dp": lax.rem(d + k, dp)},
+        )
+
+    def sums_copy(k, slot):
+        return remote(
+            all_sums.at[slot],
+            all_sums.at[slot],
+            send_grads.at[4, k],
+            recv_grads.at[4, k],
+            {"dp": lax.rem(d + k, dp)},
+        )
+
+    def send_grad(which, mat):
+        stage = stages[which]
+        count = stage.shape[1]
+        for slot in range(dp):
+            stage[slot] = mat[slot * count : (slot + 1) * count].astype(bf16)
+        each_peer(lambda k: grad_copy(which, k, d).start())
+
+    def grad_sum(which, out):
+        out[...] = stages[which][d].astype(f32)
+
+        def add(k):
+            slot = lax.rem(d - k + dp, dp)
+            grad_copy(which, k, slot).wait()
+            out[...] += lands[which][slot].astype(f32)
+
+        each_peer(add)
 
     def stage_residual(r):
         blocks_ready(ctx_all, CTX, r)
@@ -402,6 +373,7 @@
     def stage_norm_back(r):
         stat_ready(sum_one, BACK, r)
         slot = lax.rem(r, rog_ring.shape[0])
+        two = lax.rem(r, 2)
         for k, s in enumerate(lanes):
             first = sum_one[r, 0, k : k + 1, :]
             second = sum_one[r, 0, parts + k : parts + k + 1, :]
@@ -411,7 +383,7 @@
             first = first * (1.0 / channels)
             second = second * (1.0 / channels)
             scaled = hid_grad[:, s] * col(GAIN1)
-            back = inv_one[k : k + 1, :] * (scaled - first - n_one[:, s] * second)
+            back = inv_one[two, k : k + 1, :] * (scaled - first - n_one[two, :, s] * second)
             rog_ring[slot, :, s] = back
             low = back.astype(bf16)
             att_all[r, g, :, s] = low
@@ -421,6 +393,7 @@
 
     def stage_feed(r):
         stat_ready(stat_one, ONE, r)
+        two = lax.rem(r, 2)
         for k, s in enumerate(lanes):
             means = [stat_one[r, p, k : k + 1, :] for p in range(groups)]
             center = sum(means[1:], means[0]) * (1.0 / groups)
@@ -430,9 +403,9 @@
             for mean in means:
                 spread += local * (mean - center) * (mean - center)
             inverse = lax.rsqrt(spread * (1.0 / channels) + eps)
-            inv_one[k : k + 1, :] = inverse
+            inv_one[two, k : k + 1, :] = inverse
             normed = (x_one[:, s] - center) * inverse
-            n_one[:, s] = normed
+            n_one[two, :, s] = normed
             h = normed * col(GAIN1) + col(SHIFT1)
             hid[:, s] = h
             hid_low[:, s] = h.astype(bf16)
@@ -478,8 +451,7 @@
                 mix_grad[heads, toks] = (mm(mix_ring[slot, keys, toks], score_grad) * factor).astype(bf16)
                 mix_grad[keys, toks] = (mm_nt(mix_ring[slot, heads, toks], score_grad) * factor).astype(bf16)
         g_qkv[...] += mm_nt(mix_grad[...], x_ring[slot])
-        total = mm(wqkv[...], mix_grad[...]) + rog_ring[lax.rem(r, rog_ring.shape[0])]
-        grad_in[...] = pltpu.roll(total, place[r, 1], 1)
+        grad_in[...] = mm(wqkv[...], mix_grad[...]) + rog_ring[lax.rem(r, rog_ring.shape[0])]
         base = 6 * local + hidden_units
         for n, start in ((0, 0), (1, 2 * local)):
             chunk = mix_grad[start : start + local, lanes[0]].astype(f32)
@@ -505,7 +477,7 @@
             first = first * (1.0 / channels)
             second = second * inverse * (1.0 / channels)
             normed = (x_two[:, s] - center) * inverse
-            res[:, s] = normed * col(GAIN2) + col(SHIFT2)
+            result[:, s] = (normed * col(GAIN2) + col(SHIFT2)).astype(bf16)
             up = upstream[:, s]
             back = inverse * (up * col(GAIN2) - first - normed * second)
             rtg[:, s] = back
@@ -514,7 +486,6 @@
             accumulate(S_GAIN2, up * normed)
             accumulate(S_SHIFT2, up)
             accumulate(S_BDOWN, low.astype(f32))
-        result[...] = pltpu.roll(res[...], place[r, 1], 1).astype(bf16)
         pre[...] = mm(wdown[...], br_low[...])
         g_down[...] += mm_nt(act[...], br_low[...])
         base = 6 * local
@@ -529,7 +500,7 @@
         for k, s in enumerate(lanes):
             total = rtg[:, s] + change[:, s]
             hid_grad[:, s] = total
-            normed = n_one[:, s]
+            normed = n_one[lax.rem(r, 2), :, s]
             scaled = total * col(GAIN1)
             sum_one[r, g, k : k + 1, :] = row_sum(scaled)
             sum_one[r, g, parts + k : parts + k + 1, :] = row_sum(scaled * normed)
@@ -544,17 +515,44 @@
         def _():
             stage(r)
 
+    at(5, stage_norm_back)
+    at(4, stage_feed_back)
+    at(DELAY, stage_attend_back)
+    at(3, stage_feed)
     at(2, stage_residual)
     at(0, stage_attend)
-    at(3, stage_norm_back)
-    at(2, stage_feed)
-    at(DELAY, stage_attend_back)
     at(1, lambda r: pass_on(ctx_all, CTX, r))
-    at(4, lambda r: pass_on(att_all, ATT, r))
-    at(2, stage_feed_back)
+    at(6, lambda r: pass_on(att_all, ATT, r))
+
+    @pl.when(i == rows - 1 + 4)
+    def _():
+        for which in range(4):
+            each_peer(lambda k, which=which: weight_copy(which, k, d).wait_send())
+        for offset in range(1, groups):
+            rows_copy(offset, g, lax.rem(g + offset, groups)).wait_send()
+        send_grad(UP, g_up[...].T)
+        send_grad(DOWN, g_down[...])
+
+    @pl.when(i == rows - 1 + 5)
+    def _():
+        send_grad(OUT, g_out[...])
 
     @pl.when(i == steps - 1)
     def _():
+        send_grad(QKV, g_qkv[...].T)
+        mine = all_sums.at[d]
+        for n in range(6):
+            mine[n : n + 1, :local] = row_sum(sums[n * local : (n + 1) * local, :].T)
+        base = 6 * local
+        mine[6:7, :] = row_sum(sums[base : base + hidden_units, :].T)
+        base += hidden_units
+        mine[7:8, : 2 * local] = row_sum(sums[base : base + 2 * local, :].T)
+        each_peer(lambda k: sums_copy(k, d).start())
+        for which, out in ((UP, o_up), (DOWN, o_down), (OUT, o_out), (QKV, o_qkv)):
+            grad_sum(which, out)
+        each_peer(lambda k: sums_copy(k, lax.rem(d - k + dp, dp)).wait())
+        o_sums[...] = jnp.sum(all_sums[...], axis=0)
+
         def drain(r, carry):
             blocks_sent(ctx_all, CTX, r)
             blocks_sent(att_all, ATT, r)
@@ -566,16 +564,18 @@
         lax.fori_loop(0, rows, drain, 0)
 
 
-def run_layer(place, inputs, grad_out, mats, b_qkv, b_up, cols):
+def run_layer(place, inputs, grad_out, shards, b_qkv, b_up, cols):
     groups = lax.axis_size("group")
+    dp = lax.axis_size("dp")
     local, tok_count = inputs.shape
     rows = place.shape[0]
+    channels = groups * local
     seq = tok_count // rows
     half = seq // SPLIT
     parts = seq // LANES
     units = b_up.shape[0]
     last = rows - 1
-    ring = DELAY + 1
+    ring = DELAY
     vmem = pl.BlockSpec(memory_space=pltpu.VMEM)
 
     def rows_at(delay):
@@ -586,29 +586,48 @@
 
     acc_shapes = ((3 * local, local), (groups * local, local), (units, local), (units, local))
     sums_shape = (6 * local + units + 2 * local, LANES)
+    shard_shapes = tuple(w.shape for w in shards)
+    slots = tuple((dp, *s) for s in shard_shapes)
+    row_sums = (8, units)
     block = (rows, groups, local, seq)
     return pl.pallas_call(
-        functools.partial(layer_kernel, rows, groups),
+        functools.partial(layer_kernel, rows, groups, dp),
         grid=(rows + DELAY,),
         out_shape=(
             jax.ShapeDtypeStruct((local, tok_count), bf16),
             jax.ShapeDtypeStruct((local, tok_count), f32),
-            *(jax.ShapeDtypeStruct(s, f32) for s in acc_shapes),
-            jax.ShapeDtypeStruct(sums_shape, f32),
+            *(jax.ShapeDtypeStruct(s, f32) for s in shard_shapes),
+            jax.ShapeDtypeStruct(row_sums, f32),
         ),
         in_specs=[
             pl.BlockSpec(memory_space=pltpu.SMEM),
             rows_at(0),
-            rows_at(2),
-            *([vmem] * (len(mats) + 3)),
+            rows_at(3),
+            *([vmem] * (len(shards) + 3)),
         ],
         out_specs=(
-            rows_at(2),
+            rows_at(4),
             rows_at(DELAY),
-            *(whole(s) for s in acc_shapes),
-            whole(sums_shape),
+            *(whole(s) for s in shard_shapes),
+            whole(row_sums),
         ),
         scratch_shapes=[
+            pltpu.VMEM((3 * local, local), bf16),
+            pltpu.VMEM((local, 3 * local), bf16),
+            pltpu.VMEM((local, channels), bf16),
+            pltpu.VMEM((local, channels), bf16),
+            pltpu.VMEM((units, local), bf16),
+            pltpu.VMEM((local, units), bf16),
+            pltpu.VMEM((local, units), bf16),
+            pltpu.VMEM((units, local), bf16),
+            *(pltpu.VMEM(s, bf16) for s in slots),
+            pltpu.VMEM((groups, dp // groups, *shard_shapes[1]), bf16),
+            pltpu.VMEM((local, units), f32),
+            pltpu.VMEM((units, local), f32),
+            *(pltpu.VMEM(s, f32) for s in acc_shapes),
+            pltpu.VMEM(sums_shape, f32),
+            *(pltpu.VMEM(s, bf16) for s in slots),
+            pltpu.VMEM((dp, *row_sums), f32),
             pltpu.VMEM(block, bf16),
             pltpu.VMEM(block, bf16),
             pltpu.VMEM((rows, groups, 2 * parts, LANES), f32),
@@ -619,14 +638,13 @@
             pltpu.VMEM((ring, HG * SPLIT, half, half), bf16),
             pltpu.VMEM((half, half), f32),
             pltpu.VMEM((local, seq), f32),
-            pltpu.VMEM((local, seq), f32),
-            pltpu.VMEM((parts, LANES), f32),
+            pltpu.VMEM((2, local, seq), f32),
+            pltpu.VMEM((2, parts, LANES), f32),
             pltpu.VMEM((local, seq), f32),
             pltpu.VMEM((local, seq), bf16),
             pltpu.VMEM((units, seq), f32),
             pltpu.VMEM((units, seq), bf16),
             pltpu.VMEM((units, seq), f32),
-            pltpu.VMEM((local, seq), f32),
             pltpu.VMEM((local, seq), f32),
             pltpu.VMEM((local, seq), f32),
             pltpu.VMEM((local, seq), f32),
@@ -640,31 +658,111 @@
             pltpu.SemaphoreType.DMA((6, rows)),
             pltpu.SemaphoreType.DMA((3 * (groups - 1), rows)),
             pltpu.SemaphoreType.DMA((3 * (groups - 1), rows)),
+            pltpu.SemaphoreType.DMA((4, dp)),
+            pltpu.SemaphoreType.DMA((4, dp)),
+            pltpu.SemaphoreType.DMA((groups - 1,)),
+            pltpu.SemaphoreType.DMA((groups - 1,)),
+            pltpu.SemaphoreType.DMA((5, dp)),
+            pltpu.SemaphoreType.DMA((5, dp)),
         ],
         compiler_params=pltpu.CompilerParams(
-            collective_id=0, has_side_effects=True, vmem_limit_bytes=60 << 20
+            collective_id=0, has_side_effects=True, vmem_limit_bytes=63 << 20
         ),
         name="layer",
-    )(place, inputs, grad_out, *mats, b_qkv, b_up, cols)
-
-
-def row_places(labels):
-    seq = labels.shape[1]
+    )(place, inputs, grad_out, *shards, b_qkv, b_up, cols)
+
+
+def prepare_kernel(labels, b_qv, b_up, b_out, gain_one, shift_one, b_down, gain_two, shift_two, place, o_qkv, o_up, o_cols):
+    rows, seq = labels.shape
     half = seq // SPLIT
-    counts = [jnp.sum((labels == v).astype(jnp.int32), axis=1) for v in range(4)]
+    local = b_out.shape[1]
+    ids = labels[...]
+    counts = [
+        jnp.sum(jnp.where(ids == v, 1.0, 0.0), axis=1, keepdims=True) for v in range(4)
+    ]
     start = jnp.zeros_like(counts[0])
     first = jnp.zeros_like(start)
     second = jnp.zeros_like(start)
     found = jnp.zeros_like(start)
     begin = jnp.zeros_like(start)
     for v in range(4):
-        hit = jnp.where(counts[v] == half, 1 - found, 0)
+        hit = jnp.where(counts[v] == half, 1.0 - found, 0.0)
         start = start + hit * begin
         first = first + hit * counts[(v + 1) % 4]
         second = second + hit * (counts[(v + 1) % 4] + counts[(v + 2) % 4])
         found = found + hit
         begin = begin + counts[v]
-    return jnp.stack([(seq - start) % seq, start, first, second], axis=1)
+    turn = jnp.where(start == 0.0, 0.0, seq - start)
+    lane = lax.broadcasted_iota(jnp.int32, (rows, LANES), 1)
+    table = jnp.zeros((rows, LANES), f32)
+    for n, value in enumerate((turn, start, first, second)):
+        table = jnp.where(lane == n, value, table)
+    place[...] = table.astype(jnp.int32)
+
+    def column(row):
+        return jnp.broadcast_to(row, (LANES, row.shape[1])).T
+
+    o_qkv[:local, :] = column(b_qv[:, :local])
+    o_qkv[local : 2 * local, :] = jnp.zeros((local, LANES), f32)
+    o_qkv[2 * local :, :] = column(b_qv[...])[local:, :]
+    o_up[...] = column(b_up[...])
+    for n, ref in enumerate((b_out, gain_one, shift_one, b_down, gain_two, shift_two)):
+        o_cols[n * local : (n + 1) * local, :] = column(ref[...])
+
+
+def prepare(labels, b_qv, b_up, *vectors):
+    local = vectors[0].shape[-1]
+    vmem = pl.BlockSpec(memory_space=pltpu.VMEM)
+    return pl.pallas_call(
+        prepare_kernel,
+        out_shape=(
+            jax.ShapeDtypeStruct((labels.shape[0], LANES), jnp.int32),
+            jax.ShapeDtypeStruct((3 * local, LANES), f32),
+            jax.ShapeDtypeStruct((b_up.shape[1], LANES), f32),
+            jax.ShapeDtypeStruct((6 * local, LANES), f32),
+        ),
+        in_specs=[vmem] * (3 + len(vectors)),
+        out_specs=(vmem,) * 4,
+        name="prepare",
+    )(labels, b_qv, b_up, *(v.reshape(1, local) for v in vectors))
+
+
+def finish_kernel(place, result, grad_in, qkv, out, up, down, sums, *outs):
+    i = pl.program_id(0)
+    outs[0][...] = pltpu.roll(result[...].astype(f32), place[i, 1], 1).astype(bf16)
+    outs[1][...] = pltpu.roll(grad_in[...], place[i, 1], 1)
+
+    @pl.when(i == 0)
+    def _():
+        local = result.shape[0]
+        for target, source in zip(outs[2:6], (qkv, out, up, down)):
+            target[...] = source[...]
+        for n in range(6):
+            outs[6 + n][...] = sums[n : n + 1, :local]
+        outs[12][...] = sums[6:7, :]
+        outs[13][...] = sums[7:8, : 2 * local]
+
+
+def finish(place, result, grad_in, *small):
+    local, tok_count = result.shape
+    rows = place.shape[0]
+    seq = tok_count // rows
+    units = small[4].shape[1]
+    block = pl.BlockSpec((local, seq), lambda i: (0, i))
+    vmem = pl.BlockSpec(memory_space=pltpu.VMEM)
+    shapes = (*(s.shape for s in small[:4]), *((1, local),) * 6, (1, units), (1, 2 * local))
+    return pl.pallas_call(
+        finish_kernel,
+        grid=(rows,),
+        out_shape=(
+            jax.ShapeDtypeStruct(result.shape, bf16),
+            jax.ShapeDtypeStruct(grad_in.shape, f32),
+            *(jax.ShapeDtypeStruct(s, f32) for s in shapes),
+        ),
+        in_specs=[pl.BlockSpec(memory_space=pltpu.SMEM), block, block, *[vmem] * 5],
+        out_specs=(block, block, *(vmem,) * len(shapes)),
+        name="finish",
+    )(place, result, grad_in, *small)
 
 
 def per_device(
@@ -684,52 +782,28 @@
     shift_two,
     grad_out,
 ):
-    groups = lax.axis_size("group")
-    local = inputs.shape[0]
-    units = b_up.shape[1]
-    channels = local * groups
-    gathered = gather_weights(w_qkv[0], w_out, w_up[0], down_weight[0])
-    mat_qkv = gathered[0].reshape(local, 3 * local)
-    mat_out = gathered[1].reshape(channels, local)
-    mat_up = gathered[2].reshape(local, units)
-    mat_down = gathered[3].reshape(units, local)
-    out_rows = jnp.swapaxes(gathered[4], 1, 2).reshape(local, channels)
-    mats = (
-        mat_qkv.T,
-        mat_qkv,
-        mat_out.T,
-        out_rows,
-        mat_up.T,
-        mat_up,
-        mat_down.T,
-        mat_down,
+    place, qkv_col, up_col, cols = prepare(
+        labels, b_qv, b_up, b_out, gain_one, shift_one, down_bias, gain_two, shift_two
     )
-    wide = lambda v: jnp.broadcast_to(v[:, None], (v.shape[0], LANES))
-    key_zero = jnp.zeros((local,), f32)
-    qkv_bias = jnp.concatenate([b_qv[0, :local], key_zero, b_qv[0, local:]])
-    cols = jnp.concatenate([b_out, gain_one, shift_one, down_bias[0], gain_two, shift_two])
-    result, input_grad, qkv_t, out_grad, up_t, down_grad, sums = run_layer(
-        row_places(labels), inputs, grad_out, mats, wide(qkv_bias), wide(b_up[0]), wide(cols)
-    )
-    grads = scatter_grads((qkv_t.T, out_grad, up_t.T, down_grad), sums)
-    flat = grads[4].reshape(-1)
-    piece = lambda n: flat[n * local : (n + 1) * local]
-    base = 6 * local
+    shards = (w_qkv[0], w_out, w_up[0], down_weight[0])
+    raw = run_layer(place, inputs, grad_out, shards, qkv_col, up_col, cols)
+    result, input_grad, qkv, out, up, down, *sums = finish(place, *raw)
+    flat = [s.reshape(-1) for s in sums]
     return (
         result,
         input_grad,
-        grads[0][None],
-        flat[base + units :][None],
-        grads[1],
-        piece(0),
-        piece(1),
-        piece(2),
-        grads[2][None],
-        flat[base : base + units][None],
-        grads[3][None],
-        piece(3)[None],
-        piece(4),
-        piece(5),
+        qkv[None],
+        sums[7],
+        out,
+        flat[0],
+        flat[1],
+        flat[2],
+        up[None],
+        sums[6],
+        down[None],
+        sums[3],
+        flat[4],
+        flat[5],
     )
 
 

time: 375 us -> 240 us (0.64)
  the two profiles are of different devices: /device:TPU:12 before, /device:TPU:0 now
where the time goes in v2:
time: 240 us
  Pallas kernels  239 us (100%)
    pallas_call x1, Pallas kernels, run_layer(): pl.pallas_call(functools.partial(layer_kernel, rows, groups, dp), grid=(r...  223 us
    pallas_call x1, Pallas kernels, finish(): pl.pallas_call(finish_kernel, grid=(rows,), out_shape=(jax.ShapeDtypeStru...  14.5 us

profile of v2, /device:TPU:0, one launch (start us, length us, event | category | flops | bytes accessed | tf_op | source)
XLA Modules:
  0.0 239.9 jit_solution(7470299780702261920)
XLA Ops:
  0.6 2.1 prepare.1
  2.8 222.6 %layer.1 = (bf16[192,8192]{1,0:T(8,128)(2,1)}, f32[192,8192]{1,0:T(8,128)}, f32[24,576]{1,0:T(8,128)}, f32[96,192]{1,0:T(8,128)}, f32[24,768]{1,0:T(8,128)}, /*index=5*/f32[96,192]{1,0:T(8,128)}, f32[8,768]{1,0:T(8,128)}) custom-call(s32[16,128]{1,0:T(8,128)} %get-tuple-element.39.place, bf16[192,8192]{1,0:T(8,128)(2,1)} %inp.1, bf16[192,8192]{1,0:T(8,128)(2,1)} %gout_in.1, ...), custom_call_target="tpu_custom_call" | custom-call | tf_op jit(solution)/shard_map/layer/pallas_call | solution.py:593
  225.4 14.5 %finish.1 = (bf16[192,8192]{1,0:T(8,128)(2,1)}, f32[192,8192]{1,0:T(8,128)}, f32[24,576]{1,0:T(8,128)}, f32[96,192]{1,0:T(8,128)}, f32[24,768]{1,0:T(8,128)}, /*...) custom-call(s32[16,128]{1,0:T(8,128)} %get-tuple-element.39.place, ...), custom_call_target="tpu_custom_call" | custom-call | tf_op jit(solution)/shard_map/finish/pallas_call | solution.py:754

commit v3 on v2

--- a/solution.py
+++ b/solution.py
@@ -12,7 +12,9 @@
 HG = 3
 LANES = 128
 SPLIT = 2
-DELAY = 7
+FINISH_ROWS = 4
+PASS_CTX, RESIDUAL, FEED, FEED_BACK, NORM_BACK, PASS_ATT, DELAY = 1, 4, 5, 6, 7, 8, 9
+CTX_SLOTS, ATT_SLOTS = DELAY + 1, 4
 
 eps = 1e-12
 f32 = jnp.float32
@@ -30,6 +32,40 @@
 
 def mm_tn(left, right):
     return lax.dot_general(left, right, (((0,), (0,)), ((), ())), preferred_element_type=f32)
+
+
+def packed_rows(count, width):
+    tail = 0 if width % LANES == 0 else count // (2 - count % 2)
+    return -(-(width // LANES * count + tail) // 16) * 16
+
+
+def pack(into, x):
+    count, width = x.shape
+    whole = width // LANES
+    for k in range(whole):
+        into[k * count : (k + 1) * count, :] = x[:, k * LANES : (k + 1) * LANES]
+    if width % LANES:
+        left = width - whole * LANES
+        folds = 2 - count % 2
+        part = count // folds
+        for n in range(folds):
+            into[whole * count : whole * count + part, n * left : (n + 1) * left] = x[
+                n * part : (n + 1) * part, whole * LANES :
+            ]
+
+
+def unpack(into, start, count, width, x):
+    whole = width // LANES
+    for k in range(whole):
+        into[start : start + count, k * LANES : (k + 1) * LANES] = x[k * count : (k + 1) * count, :]
+    if width % LANES:
+        left = width - whole * LANES
+        folds = 2 - count % 2
+        part = count // folds
+        for n in range(folds):
+            into[start + n * part : start + (n + 1) * part, whole * LANES : width] = x[
+                whole * count : whole * count + part, n * left : (n + 1) * left
+            ]
 
 
 def row_sum(x):
@@ -83,6 +119,7 @@
     g_up,
     g_down,
     sums,
+    flat,
     land_qkv,
     land_out,
     land_up,
@@ -90,9 +127,7 @@
     all_sums,
     ctx_all,
     att_all,
-    stat_one,
-    stat_two,
-    sum_one,
+    stats,
     x_ring,
     mix_ring,
     prob_ring,
@@ -148,9 +183,10 @@
 
     def block_copy(buf, base, kind, r, slot):
         peer = across if kind == 0 else beside
+        at_row = lax.rem(r, buf.shape[0])
         return remote(
-            buf.at[r, slot],
-            buf.at[r, slot],
+            buf.at[at_row, slot],
+            buf.at[at_row, slot],
             send_blocks.at[base + kind, r],
             recv_blocks.at[base + kind, r],
             {"group": peer},
@@ -173,29 +209,32 @@
         block_copy(buf, base, 1, r, g).wait_send()
         block_copy(buf, base, 2, r, across).wait_send()
 
-    def stat_copy(buf, base, offset, r, slot):
+    def stat_copy(step, offset, slot):
         return remote(
-            buf.at[r, slot],
-            buf.at[r, slot],
-            send_stats.at[base + offset - 1, r],
-            recv_stats.at[base + offset - 1, r],
+            stats.at[step, slot],
+            stats.at[step, slot],
+            send_stats.at[offset - 1, step],
+            recv_stats.at[offset - 1, step],
             {"group": lax.rem(g + offset, groups)},
         )
 
-    def send_stat(buf, base, r):
+    def stats_send():
         for offset in range(1, groups):
-            stat_copy(buf, base, offset, r, g).start()
-
-    def stat_ready(buf, base, r):
+            stat_copy(i, offset, g).start()
+
+    def stats_ready():
         for offset in range(1, groups):
-            stat_copy(buf, base, offset, r, lax.rem(g + groups - offset, groups)).wait_recv()
-
-    def stat_sent(buf, base, r):
-        for offset in range(1, groups):
-            stat_copy(buf, base, offset, r, g).wait_send()
-
+            stat_copy(i - 1, offset, lax.rem(g + groups - offset, groups)).wait_recv()
+            stat_copy(i - 1, offset, g).wait_send()
+
+    def put_stat(first, k, value):
+        stats[i, g, first + k : first + k + 1, :] = value
+
+    def get_stat(first, k, p):
+        return stats[i - 1, p, first + k : first + k + 1, :]
+
+    ONE, TWO, BACK = 0, 2 * parts, 6 * parts
     CTX, ATT = 0, 3
-    ONE, TWO, BACK = 0, groups - 1, 2 * (groups - 1)
 
     shards = (w_qkv, w_out, w_up, w_down)
     fulls = (all_qkv, all_out, all_up, all_down)
@@ -220,10 +259,9 @@
 
     def weights_ready(which, into):
         each_peer(lambda k: weight_copy(which, k, lax.rem(d - k + dp, dp)).wait_recv())
-        full = fulls[which]
-        count, width = full.shape[1:]
+        count, width = shards[which].shape
         for slot in range(dp):
-            into[slot * count : (slot + 1) * count, :width] = full[slot].astype(f32)
+            unpack(into, slot * count, count, width, fulls[which][slot].astype(f32))
 
     per = dp // groups
 
@@ -248,19 +286,22 @@
                 barrier, inc=1, device_id={"dp": lax.rem(d + k, dp)}, device_id_type=MESH
             )
         )
+        flat[...] = jnp.zeros_like(flat)
         for shard, full in zip(shards, fulls):
-            full[d] = shard[...].astype(bf16)
+            pack(flat, shard[...])
+            full[d] = flat[: full.shape[1], :].astype(bf16)
         pl.semaphore_wait(barrier, groups - 1 + dp - 1)
-        for which in range(4):
-            each_peer(lambda k, which=which: weight_copy(which, k, d).start())
+        each_peer(lambda k: weight_copy(QKV, k, d).start())
         for ref in (g_qkv, g_out, g_up, g_down, sums):
             ref[...] = jnp.zeros_like(ref)
         weights_ready(QKV, wide_mat)
+        for which in (OUT, UP, DOWN):
+            each_peer(lambda k, which=which: weight_copy(which, k, d).start())
         mat = wide_mat[:, : 3 * local]
         wqkv[...] = mat.astype(bf16)
         wqkv_t[...] = mat.T.astype(bf16)
 
-    @pl.when(i == 2)
+    @pl.when(i == RESIDUAL)
     def _():
         weights_ready(OUT, tall_mat)
         for offset in range(1, groups):
@@ -268,7 +309,7 @@
         out_rows[g] = all_out[pl.ds(g * per, per)]
         wout_t[...] = tall_mat[...].T.astype(bf16)
 
-    @pl.when(i == 3)
+    @pl.when(i == FEED)
     def _():
         weights_ready(UP, wide_mat)
         mat = wide_mat[...]
@@ -286,7 +327,7 @@
         count = local // per
         for p in range(groups):
             for n in range(per):
-                wide_mat[n * count : (n + 1) * count, :local] = out_rows[p, n].astype(f32)
+                unpack(wide_mat, n * count, count, local, out_rows[p, n].astype(f32))
             tall_mat[p * local : (p + 1) * local, :] = wide_mat[:, :local].T
         wout_rows[...] = tall_mat[...].T.astype(bf16)
 
@@ -313,33 +354,36 @@
 
     def send_grad(which, mat):
         stage = stages[which]
-        count = stage.shape[1]
+        count = shards[which].shape[0]
         for slot in range(dp):
-            stage[slot] = mat[slot * count : (slot + 1) * count].astype(bf16)
+            pack(flat, mat[slot * count : (slot + 1) * count])
+            stage[slot] = flat[: stage.shape[1], :].astype(bf16)
         each_peer(lambda k: grad_copy(which, k, d).start())
 
     def grad_sum(which, out):
-        out[...] = stages[which][d].astype(f32)
+        count = stages[which].shape[1]
+        flat[:count, :] = stages[which][d].astype(f32)
 
         def add(k):
             slot = lax.rem(d - k + dp, dp)
             grad_copy(which, k, slot).wait()
-            out[...] += lands[which][slot].astype(f32)
+            flat[:count, :] += lands[which][slot].astype(f32)
 
         each_peer(add)
+        unpack(out, 0, *out.shape, flat[...])
 
     def stage_residual(r):
         blocks_ready(ctx_all, CTX, r)
-        attended = mm(wout_t[...], ctx_all[r].reshape(channels, seq))
+        attended = mm(wout_t[...], ctx_all[lax.rem(r, CTX_SLOTS)].reshape(channels, seq))
         xr = x_ring.at[lax.rem(r, ring)]
         for k, s in enumerate(lanes):
             x = xr[:, s].astype(f32) + attended[:, s] + col(B_OUT)
             x_one[:, s] = x
             mean = row_sum(x) * (1.0 / local)
             off = x - mean
-            stat_one[r, g, k : k + 1, :] = mean
-            stat_one[r, g, parts + k : parts + k + 1, :] = row_sum(off * off)
-        send_stat(stat_one, ONE, r)
+            put_stat(ONE, k, mean)
+            put_stat(ONE + parts, k, row_sum(off * off))
+        blocks_sent(ctx_all, CTX, r)
 
     def stage_attend(r):
         slot = lax.rem(r, ring)
@@ -354,52 +398,78 @@
         own = lambda at: (at >= first).astype(jnp.int32) + (at >= second).astype(jnp.int32)
         mask[...] = jnp.where(own(down) == own(along), 0.0, -1000000000.0)
         scale = math.log2(math.e) / math.sqrt(HD)
-        for h in range(HG):
-            heads = slice(h * HD, (h + 1) * HD)
-            keys = slice(local + h * HD, local + (h + 1) * HD)
-            values = slice(2 * local + h * HD, 2 * local + (h + 1) * HD)
-            for b in range(SPLIT):
-                toks = slice(b * half, (b + 1) * half)
-                scores = mm_tn(mix_ring[slot, keys, toks], mix_ring[slot, heads, toks])
-                if b:
-                    scores = scores + mask[...]
-                highest = jnp.max(scores, axis=0, keepdims=True)
-                exponent = jnp.exp2((scores - highest) * scale)
-                chances = (exponent * (1.0 / row_sum(exponent))).astype(bf16)
-                prob_ring[slot, h * SPLIT + b] = chances
-                ctx_all[r, g, heads, toks] = mm(mix_ring[slot, values, toks], chances).astype(bf16)
+        blocks = [(h, b) for h in range(HG) for b in range(SPLIT)]
+
+        def piece(part, n):
+            h, b = blocks[n]
+            start = part * local + h * HD
+            return mix_ring[slot, start : start + HD, b * half : (b + 1) * half]
+
+        def score(n):
+            return mm_tn(piece(1, n), piece(0, n))
+
+        def soften(n, scores):
+            if blocks[n][1]:
+                scores = scores + mask[...]
+            highest = jnp.max(scores, axis=0, keepdims=True)
+            return jnp.exp2((scores - highest) * scale)
+
+        def norm(n, exponent):
+            chances = (exponent * (1.0 / row_sum(exponent))).astype(bf16)
+            prob_ring[slot, n] = chances
+            return chances
+
+        def blend(n, chances):
+            h, b = blocks[n]
+            ctx_all[lax.rem(r, CTX_SLOTS), g, h * HD : (h + 1) * HD, b * half : (b + 1) * half] = mm(
+                piece(2, n), chances
+            ).astype(bf16)
+
+        held = {}
+        for step in range(len(blocks) + 3):
+            n = step - 0
+            if 0 <= n < len(blocks):
+                held[0, n] = score(n)
+            n = step - 1
+            if 0 <= n < len(blocks):
+                held[1, n] = soften(n, held.pop((0, n)))
+            n = step - 2
+            if 0 <= n < len(blocks):
+                held[2, n] = norm(n, held.pop((1, n)))
+            n = step - 3
+            if 0 <= n < len(blocks):
+                blend(n, held.pop((2, n)))
         send_own(ctx_all, CTX, r)
 
     def stage_norm_back(r):
-        stat_ready(sum_one, BACK, r)
         slot = lax.rem(r, rog_ring.shape[0])
         two = lax.rem(r, 2)
         for k, s in enumerate(lanes):
-            first = sum_one[r, 0, k : k + 1, :]
-            second = sum_one[r, 0, parts + k : parts + k + 1, :]
+            first = get_stat(BACK, k, 0)
+            second = get_stat(BACK + parts, k, 0)
             for p in range(1, groups):
-                first += sum_one[r, p, k : k + 1, :]
-                second += sum_one[r, p, parts + k : parts + k + 1, :]
+                first += get_stat(BACK, k, p)
+                second += get_stat(BACK + parts, k, p)
             first = first * (1.0 / channels)
             second = second * (1.0 / channels)
             scaled = hid_grad[:, s] * col(GAIN1)
             back = inv_one[two, k : k + 1, :] * (scaled - first - n_one[two, :, s] * second)
             rog_ring[slot, :, s] = back
             low = back.astype(bf16)
-            att_all[r, g, :, s] = low
+            att_all[lax.rem(r, ATT_SLOTS), g, :, s] = low
             accumulate(S_BOUT, low.astype(f32))
         send_own(att_all, ATT, r)
-        g_out[...] += mm_nt(ctx_all[r].reshape(channels, seq), att_all[r, g])
+        contexts = ctx_all[lax.rem(r, CTX_SLOTS)].reshape(channels, seq)
+        g_out[...] += mm_nt(contexts, att_all[lax.rem(r, ATT_SLOTS), g])
 
     def stage_feed(r):
-        stat_ready(stat_one, ONE, r)
         two = lax.rem(r, 2)
         for k, s in enumerate(lanes):
-            means = [stat_one[r, p, k : k + 1, :] for p in range(groups)]
+            means = [get_stat(ONE, k, p) for p in range(groups)]
             center = sum(means[1:], means[0]) * (1.0 / groups)
-            spread = stat_one[r, 0, parts + k : parts + k + 1, :]
+            spread = get_stat(ONE + parts, k, 0)
             for p in range(1, groups):
-                spread += stat_one[r, p, parts + k : parts + k + 1, :]
+                spread += get_stat(ONE + parts, k, p)
             for mean in means:
                 spread += local * (mean - center) * (mean - center)
             inverse = lax.rsqrt(spread * (1.0 / channels) + eps)
@@ -428,29 +498,62 @@
             scaled = upstream[:, s] * col(GAIN2)
             tile = (mean, row_sum(off * off), row_sum(scaled), row_sum(scaled * off))
             for n, value in enumerate(tile):
-                stat_two[r, g, n * parts + k : n * parts + k + 1, :] = value
-        send_stat(stat_two, TWO, r)
+                put_stat(TWO + n * parts, k, value)
 
     def stage_attend_back(r):
         slot = lax.rem(r, ring)
         blocks_ready(att_all, ATT, r)
-        ctx_grad[...] = mm(wout_rows[...], att_all[r].reshape(channels, seq)).astype(bf16)
+        ctx_grad[...] = mm(
+            wout_rows[...], att_all[lax.rem(r, ATT_SLOTS)].reshape(channels, seq)
+        ).astype(bf16)
         factor = 1.0 / math.sqrt(HD)
-        for h in range(HG):
-            heads = slice(h * HD, (h + 1) * HD)
-            keys = slice(local + h * HD, local + (h + 1) * HD)
-            values = slice(2 * local + h * HD, 2 * local + (h + 1) * HD)
-            for b in range(SPLIT):
-                toks = slice(b * half, (b + 1) * half)
-                incoming = ctx_grad[heads, toks]
-                chances = prob_ring[slot, h * SPLIT + b]
-                prob_grad = mm_tn(mix_ring[slot, values, toks], incoming)
-                inner = row_sum(incoming.astype(f32) * ctx_all[r, g, heads, toks].astype(f32))
-                score_grad = (chances.astype(f32) * (prob_grad - inner)).astype(bf16)
-                mix_grad[values, toks] = mm_nt(incoming, chances).astype(bf16)
-                mix_grad[heads, toks] = (mm(mix_ring[slot, keys, toks], score_grad) * factor).astype(bf16)
-                mix_grad[keys, toks] = (mm_nt(mix_ring[slot, heads, toks], score_grad) * factor).astype(bf16)
+        blocks = [(h, b) for h in range(HG) for b in range(SPLIT)]
+
+        def at_block(part, n):
+            h, b = blocks[n]
+            start = part * local + h * HD
+            return slice(start, start + HD), slice(b * half, (b + 1) * half)
+
+        def piece(part, n):
+            return mix_ring[slot, *at_block(part, n)]
+
+        def spread(n):
+            incoming = ctx_grad[at_block(0, n)]
+            mix_grad[at_block(2, n)] = mm_nt(incoming, prob_ring[slot, n]).astype(bf16)
+
+        def open_up(n):
+            return mm_tn(piece(2, n), ctx_grad[at_block(0, n)])
+
+        def center(n, prob_grad):
+            at_n = at_block(0, n)
+            inner = row_sum(ctx_grad[at_n].astype(f32) * ctx_all[lax.rem(r, CTX_SLOTS), g, *at_n].astype(f32))
+            return (prob_ring[slot, n].astype(f32) * (prob_grad - inner)).astype(bf16)
+
+        def queries(n, score_grad):
+            mix_grad[at_block(0, n)] = (mm(piece(1, n), score_grad) * factor).astype(bf16)
+
+        def keys(n, score_grad):
+            mix_grad[at_block(1, n)] = (mm_nt(piece(0, n), score_grad) * factor).astype(bf16)
+
+        held = {}
+        for step in range(len(blocks) + 2):
+            n = step - 0
+            if 0 <= n < len(blocks):
+                held[0, n] = open_up(n)
+            n = step - 0
+            if 0 <= n < len(blocks):
+                spread(n)
+            n = step - 1
+            if 0 <= n < len(blocks):
+                held[1, n] = center(n, held.pop((0, n)))
+            n = step - 2
+            if 0 <= n < len(blocks):
+                queries(n, held[1, n])
+            n = step - 2
+            if 0 <= n < len(blocks):
+                keys(n, held.pop((1, n)))
         g_qkv[...] += mm_nt(mix_grad[...], x_ring[slot])
+        blocks_sent(att_all, ATT, r)
         grad_in[...] = mm(wqkv[...], mix_grad[...]) + rog_ring[lax.rem(r, rog_ring.shape[0])]
         base = 6 * local + hidden_units
         for n, start in ((0, 0), (1, 2 * local)):
@@ -460,9 +563,8 @@
             sums[base + n * local : base + (n + 1) * local, :] += chunk
 
     def stage_feed_back(r):
-        stat_ready(stat_two, TWO, r)
         for k, s in enumerate(lanes):
-            row = lambda p, n: stat_two[r, p, n * parts + k : n * parts + k + 1, :]
+            row = lambda p, n: get_stat(TWO + n * parts, k, p)
             means = [row(p, 0) for p in range(groups)]
             center = sum(means[1:], means[0]) * (1.0 / groups)
             spread, first, second = row(0, 1), row(0, 2), row(0, 3)
@@ -502,11 +604,10 @@
             hid_grad[:, s] = total
             normed = n_one[lax.rem(r, 2), :, s]
             scaled = total * col(GAIN1)
-            sum_one[r, g, k : k + 1, :] = row_sum(scaled)
-            sum_one[r, g, parts + k : parts + k + 1, :] = row_sum(scaled * normed)
+            put_stat(BACK, k, row_sum(scaled))
+            put_stat(BACK + parts, k, row_sum(scaled * normed))
             accumulate(S_GAIN1, total * normed)
             accumulate(S_SHIFT1, total)
-        send_stat(sum_one, BACK, r)
 
     def at(delay, stage):
         r = i - delay
@@ -515,16 +616,25 @@
         def _():
             stage(r)
 
-    at(5, stage_norm_back)
-    at(4, stage_feed_back)
+    @pl.when(jnp.logical_and(i > RESIDUAL, i <= rows + FEED_BACK))
+    def _():
+        stats_ready()
+
+    at(NORM_BACK, stage_norm_back)
+    at(FEED_BACK, stage_feed_back)
+    at(FEED, stage_feed)
+    at(RESIDUAL, stage_residual)
+
+    @pl.when(jnp.logical_and(i >= RESIDUAL, i < rows + FEED_BACK))
+    def _():
+        stats_send()
+
     at(DELAY, stage_attend_back)
-    at(3, stage_feed)
-    at(2, stage_residual)
     at(0, stage_attend)
-    at(1, lambda r: pass_on(ctx_all, CTX, r))
-    at(6, lambda r: pass_on(att_all, ATT, r))
-
-    @pl.when(i == rows - 1 + 4)
+    at(PASS_CTX, lambda r: pass_on(ctx_all, CTX, r))
+    at(PASS_ATT, lambda r: pass_on(att_all, ATT, r))
+
+    @pl.when(i == rows - 1 + FEED_BACK)
     def _():
         for which in range(4):
             each_peer(lambda k, which=which: weight_copy(which, k, d).wait_send())
@@ -533,7 +643,7 @@
         send_grad(UP, g_up[...].T)
         send_grad(DOWN, g_down[...])
 
-    @pl.when(i == rows - 1 + 5)
+    @pl.when(i == rows - 1 + NORM_BACK)
     def _():
         send_grad(OUT, g_out[...])
 
@@ -553,16 +663,6 @@
         each_peer(lambda k: sums_copy(k, lax.rem(d - k + dp, dp)).wait())
         o_sums[...] = jnp.sum(all_sums[...], axis=0)
 
-        def drain(r, carry):
-            blocks_sent(ctx_all, CTX, r)
-            blocks_sent(att_all, ATT, r)
-            stat_sent(stat_one, ONE, r)
-            stat_sent(stat_two, TWO, r)
-            stat_sent(sum_one, BACK, r)
-            return carry
-
-        lax.fori_loop(0, rows, drain, 0)
-
 
 def run_layer(place, inputs, grad_out, shards, b_qkv, b_up, cols):
     groups = lax.axis_size("group")
@@ -587,9 +687,9 @@
     acc_shapes = ((3 * local, local), (groups * local, local), (units, local), (units, local))
     sums_shape = (6 * local + units + 2 * local, LANES)
     shard_shapes = tuple(w.shape for w in shards)
-    slots = tuple((dp, *s) for s in shard_shapes)
+    slots = tuple((dp, packed_rows(*s), LANES) for s in shard_shapes)
     row_sums = (8, units)
-    block = (rows, groups, local, seq)
+    block = (groups, local, seq)
     return pl.pallas_call(
         functools.partial(layer_kernel, rows, groups, dp),
         grid=(rows + DELAY,),
@@ -602,11 +702,11 @@
         in_specs=[
             pl.BlockSpec(memory_space=pltpu.SMEM),
             rows_at(0),
-            rows_at(3),
+            rows_at(FEED),
             *([vmem] * (len(shards) + 3)),
         ],
         out_specs=(
-            rows_at(4),
+            rows_at(FEED_BACK),
             rows_at(DELAY),
             *(whole(s) for s in shard_shapes),
             whole(row_sums),
@@ -621,18 +721,17 @@
             pltpu.VMEM((local, units), bf16),
             pltpu.VMEM((units, local), bf16),
             *(pltpu.VMEM(s, bf16) for s in slots),
-            pltpu.VMEM((groups, dp // groups, *shard_shapes[1]), bf16),
+            pltpu.VMEM((groups, dp // groups, *slots[1][1:]), bf16),
             pltpu.VMEM((local, units), f32),
             pltpu.VMEM((units, local), f32),
             *(pltpu.VMEM(s, f32) for s in acc_shapes),
             pltpu.VMEM(sums_shape, f32),
+            pltpu.VMEM((max(s[1] for s in slots), LANES), f32),
             *(pltpu.VMEM(s, bf16) for s in slots),
             pltpu.VMEM((dp, *row_sums), f32),
-            pltpu.VMEM(block, bf16),
-            pltpu.VMEM(block, bf16),
-            pltpu.VMEM((rows, groups, 2 * parts, LANES), f32),
-            pltpu.VMEM((rows, groups, 4 * parts, LANES), f32),
-            pltpu.VMEM((rows, groups, 2 * parts, LANES), f32),
+            pltpu.VMEM((CTX_SLOTS, *block), bf16),
+            pltpu.VMEM((ATT_SLOTS, *block), bf16),
+            pltpu.VMEM((rows + DELAY, groups, 8 * parts, LANES), f32),
             pltpu.VMEM((ring, local, seq), bf16),
             pltpu.VMEM((ring, 3 * local, seq), bf16),
             pltpu.VMEM((ring, HG * SPLIT, half, half), bf16),
@@ -656,8 +755,8 @@
             pltpu.VMEM((3 * local, seq), bf16),
             pltpu.SemaphoreType.DMA((6, rows)),
             pltpu.SemaphoreType.DMA((6, rows)),
-            pltpu.SemaphoreType.DMA((3 * (groups - 1), rows)),
-            pltpu.SemaphoreType.DMA((3 * (groups - 1), rows)),
+            pltpu.SemaphoreType.DMA((groups - 1, rows + DELAY)),
+            pltpu.SemaphoreType.DMA((groups - 1, rows + DELAY)),
             pltpu.SemaphoreType.DMA((4, dp)),
             pltpu.SemaphoreType.DMA((4, dp)),
             pltpu.SemaphoreType.DMA((groups - 1,)),
@@ -727,10 +826,13 @@
     )(labels, b_qv, b_up, *(v.reshape(1, local) for v in vectors))
 
 
-def finish_kernel(place, result, grad_in, qkv, out, up, down, sums, *outs):
+def finish_kernel(many, seq, place, result, grad_in, qkv, out, up, down, sums, *outs):
     i = pl.program_id(0)
-    outs[0][...] = pltpu.roll(result[...].astype(f32), place[i, 1], 1).astype(bf16)
-    outs[1][...] = pltpu.roll(grad_in[...], place[i, 1], 1)
+    for n in range(many):
+        toks = slice(n * seq, (n + 1) * seq)
+        turn = place[i * many + n, 1]
+        outs[0][:, toks] = pltpu.roll(result[:, toks].astype(f32), turn, 1).astype(bf16)
+        outs[1][:, toks] = pltpu.roll(grad_in[:, toks], turn, 1)
 
     @pl.when(i == 0)
     def _():
@@ -748,12 +850,13 @@
     rows = place.shape[0]
     seq = tok_count // rows
     units = small[4].shape[1]
-    block = pl.BlockSpec((local, seq), lambda i: (0, i))
+    many = math.gcd(rows, FINISH_ROWS)
+    block = pl.BlockSpec((local, many * seq), lambda i: (0, i))
     vmem = pl.BlockSpec(memory_space=pltpu.VMEM)
     shapes = (*(s.shape for s in small[:4]), *((1, local),) * 6, (1, units), (1, 2 * local))
     return pl.pallas_call(
-        finish_kernel,
-        grid=(rows,),
+        functools.partial(finish_kernel, many, seq),
+        grid=(rows // many,),
         out_shape=(
             jax.ShapeDtypeStruct(result.shape, bf16),
             jax.ShapeDtypeStruct(grad_in.shape, f32),
@@ -761,6 +864,7 @@
         ),
         in_specs=[pl.BlockSpec(memory_space=pltpu.SMEM), block, block, *[vmem] * 5],
         out_specs=(block, block, *(vmem,) * len(shapes)),
+        compiler_params=pltpu.CompilerParams(vmem_limit_bytes=48 << 20),
         name="finish",
     )(place, result, grad_in, *small)
 

time: 240 us -> 225 us (0.938)
  Pallas kernels: 239 us -> 217 us
  local copies, waits for them, and re-layouts: 0 us -> 6.12 us
    pallas_call x1, Pallas kernels: 223 us -> 207 us  [run_layer(): pl.pallas_call(functools.partial(layer_kernel, rows, groups, dp), grid=(r...]
    pallas_call x1, Pallas kernels: 14.5 us -> 8.22 us  [finish(): pl.pallas_call(functools.partial(finish_kernel, many, seq), grid=(rows //...]
    unnamed x0 -> x14, local copies, waits for them, and re-layouts: none -> 6.12 us
where the time goes in v3:
time: 225 us; the launch traced here: 224 us
  Pallas kernels  217 us (96%)
  local copies, waits for them, and re-layouts  6.12 us (3%)
    pallas_call x1, Pallas kernels, run_layer(): pl.pallas_call(functools.partial(layer_kernel, rows, groups, dp), grid=(r...  207 us
    pallas_call x1, Pallas kernels, finish(): pl.pallas_call(functools.partial(finish_kernel, many, seq), grid=(rows //...  8.22 us
    unnamed x14, local copies, waits for them, and re-layouts  6.12 us

profile of v3, /device:TPU:0, one launch (start us, length us, event | category | flops | bytes accessed | tf_op | source)
XLA Modules:
  0.0 224.2 jit_solution(18127926334248526147)
XLA Ops:
  0.6 2.1 prepare.1
  2.8 0.0 copy-start.5
  2.8 207.0 %layer.1 = (bf16[192,8192]{1,0:T(8,128)(2,1)}, f32[192,8192]{1,0:T(8,128)}, f32[24,576]{1,0:T(8,128)}, f32[96,192]{1,0:T(8,128)}, f32[24,768]{1,0:T(8,128)}, /*index=5*/f32[96,192]{1,0:T(8,128)}, f32[8,768]{1,0:T(8,128)}) custom-call(s32[16,128]{1,0:T(8,128)} %get-tuple-element.39.place, bf16[192,8192]{1,0:T(8,128)(2,1)} %inp.1, bf16[192,8192]{1,0:T(8,128)(2,1)} %gout_in.1, ...), custom_call_target="tpu_custom_call" | custom-call | tf_op jit(solution)/shard_map/layer/pallas_call | solution.py:693
  209.8 0.0 copy-done.5
  209.8 0.0 copy-start
  209.8 1.9 copy-done
  211.7 0.0 copy-start.1
  211.7 0.9 copy-done.1
  212.6 0.0 copy-start.2
  212.6 0.9 copy-done.2
  213.5 0.0 copy-start.3
  213.5 0.9 copy-done.3
  214.4 0.0 copy-start.4
  214.4 0.8 copy-done.4
  215.2 0.0 copy-start.6
  215.2 0.7 copy-done.6
  216.0 8.2 %finish.1 = (bf16[192,8192]{1,0:T(8,128)(2,1)}, f32[192,8192]{1,0:T(8,128)}, f32[24,576]{1,0:T(8,128)}, f32[96,192]{1,0:T(8,128)}, f32[24,768]{1,0:T(8,128)}, /*...) custom-call(s32[16,128]{1,0:T(8,128)S(1)} %copy-done.5, ...), custom_call_target="tpu_custom_call" | custom-call | tf_op jit(solution)/shard_map/finish/pallas_call | solution.py:857
Async XLA Ops:
  2.8 207.1 %copy-start.5 = (s32[16,128]{1,0:T(8,128)S(1)}, s32[16,128]{1,0:T(8,128)}, u32[]{:S(2)}) copy-start(s32[16,128]{1,0:T(8,128)} %get-tuple-element.39.place) | copy-start | bytes 24580
  209.8 1.9 copy-start
  211.7 0.9 copy-start.1
  212.6 0.9 copy-start.2
  213.5 0.9 copy-start.3
  214.4 0.8 copy-start.4
  215.2 0.7 copy-start.6

commit v4 on v3

--- a/solution.py
+++ b/solution.py
@@ -13,8 +13,9 @@
 LANES = 128
 SPLIT = 2
 FINISH_ROWS = 4
-PASS_CTX, RESIDUAL, FEED, FEED_BACK, NORM_BACK, PASS_ATT, DELAY = 1, 4, 5, 6, 7, 8, 9
-CTX_SLOTS, ATT_SLOTS = DELAY + 1, 4
+PASS_CTX, RESIDUAL, FEED, FEED_BACK, NORM_BACK, PASS_ATT, DELAY = 1, 3, 4, 5, 7, 8, 9
+CTX_SLOTS, ATT_SLOTS = DELAY + 1, 5
+GRAD_LAG = NORM_BACK - FEED_BACK
 
 eps = 1e-12
 f32 = jnp.float32
@@ -230,8 +231,8 @@
     def put_stat(first, k, value):
         stats[i, g, first + k : first + k + 1, :] = value
 
-    def get_stat(first, k, p):
-        return stats[i - 1, p, first + k : first + k + 1, :]
+    def get_stat(first, k, p, ago=1):
+        return stats[i - ago, p, first + k : first + k + 1, :]
 
     ONE, TWO, BACK = 0, 2 * parts, 6 * parts
     CTX, ATT = 0, 3
@@ -443,17 +444,17 @@
 
     def stage_norm_back(r):
         slot = lax.rem(r, rog_ring.shape[0])
-        two = lax.rem(r, 2)
+        kept = lax.rem(r, (NORM_BACK - FEED + 1))
         for k, s in enumerate(lanes):
-            first = get_stat(BACK, k, 0)
-            second = get_stat(BACK + parts, k, 0)
+            first = get_stat(BACK, k, 0, GRAD_LAG)
+            second = get_stat(BACK + parts, k, 0, GRAD_LAG)
             for p in range(1, groups):
-                first += get_stat(BACK, k, p)
-                second += get_stat(BACK + parts, k, p)
+                first += get_stat(BACK, k, p, GRAD_LAG)
+                second += get_stat(BACK + parts, k, p, GRAD_LAG)
             first = first * (1.0 / channels)
             second = second * (1.0 / channels)
-            scaled = hid_grad[:, s] * col(GAIN1)
-            back = inv_one[two, k : k + 1, :] * (scaled - first - n_one[two, :, s] * second)
+            scaled = hid_grad[lax.rem(r, (GRAD_LAG + 1)), :, s] * col(GAIN1)
+            back = inv_one[kept, k : k + 1, :] * (scaled - first - n_one[kept, :, s] * second)
             rog_ring[slot, :, s] = back
             low = back.astype(bf16)
             att_all[lax.rem(r, ATT_SLOTS), g, :, s] = low
@@ -463,7 +464,7 @@
         g_out[...] += mm_nt(contexts, att_all[lax.rem(r, ATT_SLOTS), g])
 
     def stage_feed(r):
-        two = lax.rem(r, 2)
+        kept = lax.rem(r, (NORM_BACK - FEED + 1))
         for k, s in enumerate(lanes):
             means = [get_stat(ONE, k, p) for p in range(groups)]
             center = sum(means[1:], means[0]) * (1.0 / groups)
@@ -473,9 +474,9 @@
             for mean in means:
                 spread += local * (mean - center) * (mean - center)
             inverse = lax.rsqrt(spread * (1.0 / channels) + eps)
-            inv_one[two, k : k + 1, :] = inverse
+            inv_one[kept, k : k + 1, :] = inverse
             normed = (x_one[:, s] - center) * inverse
-            n_one[two, :, s] = normed
+            n_one[kept, :, s] = normed
             h = normed * col(GAIN1) + col(SHIFT1)
             hid[:, s] = h
             hid_low[:, s] = h.astype(bf16)
@@ -601,8 +602,8 @@
         change = mm(wup[...], pre_low[...])
         for k, s in enumerate(lanes):
             total = rtg[:, s] + change[:, s]
-            hid_grad[:, s] = total
-            normed = n_one[lax.rem(r, 2), :, s]
+            hid_grad[lax.rem(r, (GRAD_LAG + 1)), :, s] = total
+            normed = n_one[lax.rem(r, (NORM_BACK - FEED + 1)), :, s]
             scaled = total * col(GAIN1)
             put_stat(BACK, k, row_sum(scaled))
             put_stat(BACK + parts, k, row_sum(scaled * normed))
@@ -616,22 +617,22 @@
         def _():
             stage(r)
 
-    @pl.when(jnp.logical_and(i > RESIDUAL, i <= rows + FEED_BACK))
+    @pl.when(jnp.logical_and(i > RESIDUAL, i < rows + NORM_BACK))
     def _():
         stats_ready()
 
-    at(NORM_BACK, stage_norm_back)
     at(FEED_BACK, stage_feed_back)
     at(FEED, stage_feed)
     at(RESIDUAL, stage_residual)
 
-    @pl.when(jnp.logical_and(i >= RESIDUAL, i < rows + FEED_BACK))
+    @pl.when(jnp.logical_and(i >= RESIDUAL, i < rows + NORM_BACK - 1))
     def _():
         stats_send()
 
+    at(0, stage_attend)
+    at(NORM_BACK, stage_norm_back)
+    at(PASS_CTX, lambda r: pass_on(ctx_all, CTX, r))
     at(DELAY, stage_attend_back)
-    at(0, stage_attend)
-    at(PASS_CTX, lambda r: pass_on(ctx_all, CTX, r))
     at(PASS_ATT, lambda r: pass_on(att_all, ATT, r))
 
     @pl.when(i == rows - 1 + FEED_BACK)
@@ -675,7 +676,7 @@
     parts = seq // LANES
     units = b_up.shape[0]
     last = rows - 1
-    ring = DELAY
+    ring = DELAY + 1
     vmem = pl.BlockSpec(memory_space=pltpu.VMEM)
 
     def rows_at(delay):
@@ -737,8 +738,8 @@
             pltpu.VMEM((ring, HG * SPLIT, half, half), bf16),
             pltpu.VMEM((half, half), f32),
             pltpu.VMEM((local, seq), f32),
-            pltpu.VMEM((2, local, seq), f32),
-            pltpu.VMEM((2, parts, LANES), f32),
+            pltpu.VMEM(((NORM_BACK - FEED + 1), local, seq), f32),
+            pltpu.VMEM(((NORM_BACK - FEED + 1), parts, LANES), f32),
             pltpu.VMEM((local, seq), f32),
             pltpu.VMEM((local, seq), bf16),
             pltpu.VMEM((units, seq), f32),
@@ -749,7 +750,7 @@
             pltpu.VMEM((local, seq), f32),
             pltpu.VMEM((local, seq), bf16),
             pltpu.VMEM((units, seq), bf16),
-            pltpu.VMEM((local, seq), f32),
+            pltpu.VMEM(((GRAD_LAG + 1), local, seq), f32),
             pltpu.VMEM((3, local, seq), f32),
             pltpu.VMEM((local, seq), bf16),
             pltpu.VMEM((3 * local, seq), bf16),

time: 225 us -> 214 us (0.951)
  Pallas kernels: 217 us -> 207 us
    pallas_call x1, Pallas kernels: 207 us -> 197 us  [run_layer(): pl.pallas_call(functools.partial(layer_kernel, rows, groups, dp), grid=(r...]
where the time goes in v4:
time: 214 us
  Pallas kernels  207 us (97%)
  local copies, waits for them, and re-layouts  6.12 us (3%)
    pallas_call x1, Pallas kernels, run_layer(): pl.pallas_call(functools.partial(layer_kernel, rows, groups, dp), grid=(r...  197 us
    pallas_call x1, Pallas kernels, finish(): pl.pallas_call(functools.partial(finish_kernel, many, seq), grid=(rows //...  8.22 us
    unnamed x14, local copies, waits for them, and re-layouts  6.12 us

profile of v4, /device:TPU:0, one launch (start us, length us, event | category | flops | bytes accessed | tf_op | source)
XLA Modules:
  0.0 213.8 jit_solution(18342395161467196051)
XLA Ops:
  0.6 2.1 prepare.1
  2.8 0.0 copy-start.5
  2.8 196.7 %layer.1 = (bf16[192,8192]{1,0:T(8,128)(2,1)}, f32[192,8192]{1,0:T(8,128)}, f32[24,576]{1,0:T(8,128)}, f32[96,192]{1,0:T(8,128)}, f32[24,768]{1,0:T(8,128)}, /*index=5*/f32[96,192]{1,0:T(8,128)}, f32[8,768]{1,0:T(8,128)}) custom-call(s32[16,128]{1,0:T(8,128)} %get-tuple-element.39.place, bf16[192,8192]{1,0:T(8,128)(2,1)} %inp.1, bf16[192,8192]{1,0:T(8,128)(2,1)} %gout_in.1, ...), custom_call_target="tpu_custom_call" | custom-call | tf_op jit(solution)/shard_map/layer/pallas_call | solution.py:694
  199.5 0.0 copy-done.5
  199.5 0.0 copy-start
  199.5 1.9 copy-done
  201.4 0.0 copy-start.1
  201.4 0.9 copy-done.1
  202.2 0.0 copy-start.2
  202.3 0.9 copy-done.2
  203.1 0.0 copy-start.3
  203.1 0.9 copy-done.3
  204.0 0.0 copy-start.4
  204.0 0.8 copy-done.4
  204.9 0.0 copy-start.6
  204.9 0.7 copy-done.6
  205.6 8.2 %finish.1 = (bf16[192,8192]{1,0:T(8,128)(2,1)}, f32[192,8192]{1,0:T(8,128)}, f32[24,576]{1,0:T(8,128)}, f32[96,192]{1,0:T(8,128)}, f32[24,768]{1,0:T(8,128)}, /*...) custom-call(s32[16,128]{1,0:T(8,128)S(1)} %copy-done.5, ...), custom_call_target="tpu_custom_call" | custom-call | tf_op jit(solution)/shard_map/finish/pallas_call | solution.py:858
Async XLA Ops:
  2.8 196.7 %copy-start.5 = (s32[16,128]{1,0:T(8,128)S(1)}, s32[16,128]{1,0:T(8,128)}, u32[]{:S(2)}) copy-start(s32[16,128]{1,0:T(8,128)} %get-tuple-element.39.place) | copy-start | bytes 24580
  199.5 1.9 copy-start
  201.4 0.9 copy-start.1
  202.2 0.9 copy-start.2
  203.1 0.9 copy-start.3
  204.0 0.8 copy-start.4
  204.9 0.7 copy-start.6

commit v5 on v0

v5 whole, which is shorter than its diff:
```python
import functools
import math

import jax
import jax.numpy as jnp
from jax import lax
from jax.experimental import pallas as pl
from jax.experimental.pallas import tpu as pltpu
from jax.sharding import PartitionSpec as P

HD = 64
HG = 3
LANES = 128
SPLIT = 2
FINISH_ROWS = 4
PASS_CTX, RESIDUAL, FEED, FEED_BACK, NORM_BACK, PASS_ATT, DELAY = 1, 3, 4, 5, 7, 8, 9
CTX_SLOTS, ATT_SLOTS, SEMS = DELAY + 1, 5, 5
GRAD_LAG = NORM_BACK - FEED_BACK

eps = 1e-12
f32 = jnp.float32
bf16 = jnp.bfloat16
MESH = pl.DeviceIdType.MESH


def mm(left, right):
    return jnp.dot(left, right, preferred_element_type=f32)


def mm_nt(left, right):
    return lax.dot_general(left, right, (((1,), (1,)), ((), ())), preferred_element_type=f32)


def mm_tn(left, right):
    return lax.dot_general(left, right, (((0,), (0,)), ((), ())), preferred_element_type=f32)


def packed_rows(count, width):
    tail = 0 if width % LANES == 0 else count // (2 - count % 2)
    return -(-(width // LANES * count + tail) // 16) * 16


def pack(into, x):
    count, width = x.shape
    whole = width // LANES
    for k in range(whole):
        into[k * count : (k + 1) * count, :] = x[:, k * LANES : (k + 1) * LANES]
    if width % LANES:
        left = width - whole * LANES
        folds = 2 - count % 2
        part = count // folds
        for n in range(folds):
            into[whole * count : whole * count + part, n * left : (n + 1) * left] = x[
                n * part : (n + 1) * part, whole * LANES :
            ]


def unpack(into, start, count, width, x):
    whole = width // LANES
    for k in range(whole):
        into[start : start + count, k * LANES : (k + 1) * LANES] = x[k * count : (k + 1) * count, :]
    if width % LANES:
        left = width - whole * LANES
        folds = 2 - count % 2
        part = count // folds
        for n in range(folds):
            into[start + n * part : start + (n + 1) * part, whole * LANES : width] = x[
                whole * count : whole * count + part, n * left : (n + 1) * left
            ]


def row_sum(x):
    return jnp.sum(x, axis=0, keepdims=True)


def remote(src, dst, send, recv, device):
    return pltpu.make_async_remote_copy(
        src_ref=src, dst_ref=dst, send_sem=send, recv_sem=recv, device_id=device, device_id_type=MESH
    )


def layer_kernel(
    rows,
    groups,
    dp,
    labels,
    inp,
    gout_in,
    w_qkv,
    w_out,
    w_up,
    w_down,
    in_qv,
    in_up,
    in_out,
    in_gain_one,
    in_shift_one,
    in_down,
    in_gain_two,
    in_shift_two,
    result,
    grad_in,
    o_qkv,
    o_out,
    o_up,
    o_down,
    o_sums,
    o_place,
    place,
    b_qkv,
    b_up,
    cols,
    inp_rows,
    gout_rows,
    res_ring,
    gin_ring,
    wqkv_t,
    wqkv,
    wout_t,
    wout_rows,
    wup_t,
    wup,
    wdown_t,
    wdown,
    all_qkv,
    all_out,
    all_up,
    all_down,
    out_rows,
    wide_mat,
    tall_mat,
    g_qkv,
    g_out,
    g_up,
    g_down,
    sums,
    flat,
    land_qkv,
    land_out,
    land_up,
    land_down,
    all_sums,
    ctx_all,
    att_all,
    stats,
    x_ring,
    mix_ring,
    prob_ring,
    mask,
    x_one,
    n_one,
    inv_one,
    hid,
    hid_low,
    pre,
    act,
    slope,
    x_two,
    upstream,
    rtg,
    br_low,
    pre_low,
    hid_grad,
    rog_ring,
    ctx_grad,
    mix_grad,
    send_blocks,
    recv_blocks,
    send_stats,
    recv_stats,
    send_weights,
    recv_weights,
    send_rows,
    recv_rows,
    send_grads,
    recv_grads,
    fetch,
    store,
    place_sem,
):
    steps = rows + DELAY
    local = w_out.shape[1]
    seq = inp.shape[1] // rows

    def inp_copy(r):
        toks = pl.ds(pl.multiple_of(r * seq, seq), seq)
        return pltpu.make_async_copy(inp.at[:, toks], inp_rows.at[r], fetch.at[0, r])

    def gout_copy(r):
        toks = pl.ds(pl.multiple_of(r * seq, seq), seq)
        return pltpu.make_async_copy(gout_in.at[:, toks], gout_rows.at[r], fetch.at[1, r])

    def result_copy(r):
        toks = pl.ds(pl.multiple_of(r * seq, seq), seq)
        slot = lax.rem(r, 2)
        return pltpu.make_async_copy(res_ring.at[slot], result.at[:, toks], store.at[0, slot])

    def grad_in_copy(r):
        toks = pl.ds(pl.multiple_of(r * seq, seq), seq)
        slot = lax.rem(r, 2)
        return pltpu.make_async_copy(gin_ring.at[slot], grad_in.at[:, toks], store.at[1, slot])

    def find_places():
        ids = labels[...]
        counts = [
            jnp.sum(jnp.where(ids == v, 1.0, 0.0), axis=1, keepdims=True) for v in range(4)
        ]
        start = jnp.zeros_like(counts[0])
        first = jnp.zeros_like(start)
        second = jnp.zeros_like(start)
        found = jnp.zeros_like(start)
        begin = jnp.zeros_like(start)
        for v in range(4):
            hit = jnp.where(counts[v] == seq // SPLIT, 1.0 - found, 0.0)
            start = start + hit * begin
            first = first + hit * counts[(v + 1) % 4]
            second = second + hit * (counts[(v + 1) % 4] + counts[(v + 2) % 4])
            found = found + hit
            begin = begin + counts[v]
        turn = jnp.where(start == 0.0, 0.0, seq - start)
        lane = lax.broadcasted_iota(jnp.int32, (rows, LANES), 1)
        table = jnp.zeros((rows, LANES), f32)
        for n, value in enumerate((turn, start, first, second)):
            table = jnp.where(lane == n, value, table)
        o_place[...] = table.astype(jnp.int32)
        copy = pltpu.make_async_copy(o_place, place, place_sem)
        copy.start()
        copy.wait()

    def spread_vectors():
        def column(row):
            return jnp.broadcast_to(row, (LANES, row.shape[1])).T

        qv = column(in_qv[...])
        b_qkv[:local, :] = qv[:local]
        b_qkv[local : 2 * local, :] = jnp.zeros((local, LANES), f32)
        b_qkv[2 * local :, :] = qv[local:]
        b_up[...] = column(in_up[...])
        vectors = (in_out, in_gain_one, in_shift_one, in_down, in_gain_two, in_shift_two)
        for n, ref in enumerate(vectors):
            cols[n * local : (n + 1) * local, :] = column(ref[...])

    def step(i, carry):
        g = lax.axis_index("group")
        d = lax.axis_index("dp")
        across = lax.rem(g + 2, groups)
        beside = g + 1 - 2 * lax.rem(g, 2)
        corner = lax.rem(beside + 2, groups)
        half = seq // SPLIT
        channels = local * groups
        parts = seq // LANES
        hidden_units = wup_t.shape[0]
        ring = x_ring.shape[0]
        lanes = [slice(k * LANES, (k + 1) * LANES) for k in range(parts)]
        col = lambda n: cols[n * local : (n + 1) * local, :]
        B_OUT, GAIN1, SHIFT1, B_DOWN, GAIN2, SHIFT2 = range(6)
        S_BOUT, S_GAIN1, S_SHIFT1, S_BDOWN, S_GAIN2, S_SHIFT2 = range(6)

        def accumulate(slot, chunk):
            sums[slot * local : (slot + 1) * local, :] += chunk

        def block_copy(buf, base, kind, r, slot):
            peer = across if kind == 0 else beside
            at_row = lax.rem(r, buf.shape[0])
            return remote(
                buf.at[at_row, slot],
                buf.at[at_row, slot],
                send_blocks.at[base + kind, lax.rem(r, SEMS)],
                recv_blocks.at[base + kind, lax.rem(r, SEMS)],
                {"group": peer},
            )

        def send_own(buf, base, r):
            block_copy(buf, base, 0, r, g).start()
            block_copy(buf, base, 1, r, g).start()

        def pass_on(buf, base, r):
            block_copy(buf, base, 0, r, across).wait_recv()
            block_copy(buf, base, 2, r, across).start()

        def blocks_ready(buf, base, r):
            block_copy(buf, base, 1, r, beside).wait_recv()
            block_copy(buf, base, 2, r, corner).wait_recv()

        def blocks_sent(buf, base, r):
            block_copy(buf, base, 0, r, g).wait_send()
            block_copy(buf, base, 1, r, g).wait_send()
            block_copy(buf, base, 2, r, across).wait_send()

        def stat_copy(step, offset, slot):
            return remote(
                stats.at[step, slot],
                stats.at[step, slot],
                send_stats.at[offset - 1, lax.rem(step, SEMS)],
                recv_stats.at[offset - 1, lax.rem(step, SEMS)],
                {"group": lax.rem(g + offset, groups)},
            )

        def stats_send():
            for offset in range(1, groups):
                stat_copy(i, offset, g).start()

        def stats_ready():
            for offset in range(1, groups):
                stat_copy(i - 1, offset, lax.rem(g + groups - offset, groups)).wait_recv()
                stat_copy(i - 1, offset, g).wait_send()

        def put_stat(first, k, value):
            stats[i, g, first + k : first + k + 1, :] = value

        def get_stat(first, k, p, ago=1):
            return stats[i - ago, p, first + k : first + k + 1, :]

        ONE, TWO, BACK = 0, 2 * parts, 6 * parts
        CTX, ATT = 0, 3

        shards = (w_qkv, w_out, w_up, w_down)
        fulls = (all_qkv, all_out, all_up, all_down)
        QKV, OUT, UP, DOWN = range(4)

        def weight_copy(which, k, slot):
            full = fulls[which]
            return remote(
                full.at[slot],
                full.at[slot],
                send_weights.at[which, k],
                recv_weights.at[which, k],
                {"dp": lax.rem(d + k, dp)},
            )

        def each_peer(action):
            def body(k, carry):
                action(k)
                return carry

            lax.fori_loop(1, dp, body, 0)

        def weights_ready(which, into):
            each_peer(lambda k: weight_copy(which, k, lax.rem(d - k + dp, dp)).wait_recv())
            count, width = shards[which].shape
            for slot in range(dp):
                unpack(into, slot * count, count, width, fulls[which][slot].astype(f32))

        per = dp // groups

        def rows_copy(offset, source, target):
            return remote(
                all_out.at[pl.ds(target * per, per)],
                out_rows.at[source],
                send_rows.at[offset - 1],
                recv_rows.at[offset - 1],
                {"group": target},
            )

        @pl.when(i == 0)
        def _():
            barrier = pltpu.get_barrier_semaphore()
            for offset in range(1, groups):
                pl.semaphore_signal(
                    barrier, inc=1, device_id={"group": lax.rem(g + offset, groups)}, device_id_type=MESH
                )
            each_peer(
                lambda k: pl.semaphore_signal(
                    barrier, inc=1, device_id={"dp": lax.rem(d + k, dp)}, device_id_type=MESH
                )
            )
            flat[...] = jnp.zeros_like(flat)

            def pack_shard(which):
                pack(flat, shards[which][...])
                fulls[which][d] = flat[: fulls[which].shape[1], :].astype(bf16)

            pack_shard(QKV)
            pl.semaphore_wait(barrier, groups - 1 + dp - 1)
            each_peer(lambda k: weight_copy(QKV, k, d).start())
            for which in (OUT, UP, DOWN):
                pack_shard(which)

            def fetch_row(r, carry):
                inp_copy(r).start()
                gout_copy(r).start()
                return carry

            lax.fori_loop(0, rows, fetch_row, 0)
            find_places()
            spread_vectors()
            for ref in (g_qkv, g_out, g_up, g_down, sums):
                ref[...] = jnp.zeros_like(ref)
            weights_ready(QKV, wide_mat)
            for which in (OUT, UP, DOWN):
                each_peer(lambda k, which=which: weight_copy(which, k, d).start())
            mat = wide_mat[:, : 3 * local]
            wqkv[...] = mat.astype(bf16)
            wqkv_t[...] = mat.T.astype(bf16)

        @pl.when(i == RESIDUAL)
        def _():
            weights_ready(OUT, tall_mat)
            for offset in range(1, groups):
                rows_copy(offset, g, lax.rem(g + offset, groups)).start()
            out_rows[g] = all_out[pl.ds(g * per, per)]
            wout_t[...] = tall_mat[...].T.astype(bf16)

        @pl.when(i == FEED)
        def _():
            weights_ready(UP, wide_mat)
            mat = wide_mat[...]
            wup[...] = mat.astype(bf16)
            wup_t[...] = mat.T.astype(bf16)
            weights_ready(DOWN, tall_mat)
            mat = tall_mat[...]
            wdown[...] = mat.astype(bf16)
            wdown_t[...] = mat.T.astype(bf16)

        @pl.when(i == DELAY)
        def _():
            for offset in range(1, groups):
                rows_copy(offset, lax.rem(g + groups - offset, groups), g).wait_recv()
            count = local // per
            for p in range(groups):
                for n in range(per):
                    unpack(wide_mat, n * count, count, local, out_rows[p, n].astype(f32))
                tall_mat[p * local : (p + 1) * local, :] = wide_mat[:, :local].T
            wout_rows[...] = tall_mat[...].T.astype(bf16)

        stages = fulls
        lands = (land_qkv, land_out, land_up, land_down)

        def grad_copy(which, k, slot):
            return remote(
                stages[which].at[lax.rem(d + k, dp)],
                lands[which].at[slot],
                send_grads.at[which, k],
                recv_grads.at[which, k],
                {"dp": lax.rem(d + k, dp)},
            )

        def sums_copy(k, slot):
            return remote(
                all_sums.at[slot],
                all_sums.at[slot],
                send_grads.at[4, k],
                recv_grads.at[4, k],
                {"dp": lax.rem(d + k, dp)},
            )

        def send_grad(which, mat):
            stage = stages[which]
            count = shards[which].shape[0]
            for slot in range(dp):
                pack(flat, mat[slot * count : (slot + 1) * count])
                stage[slot] = flat[: stage.shape[1], :].astype(bf16)
            each_peer(lambda k: grad_copy(which, k, d).start())

        def grad_sum(which, out):
            count = stages[which].shape[1]
            flat[:count, :] = stages[which][d].astype(f32)

            def add(k):
                slot = lax.rem(d - k + dp, dp)
                grad_copy(which, k, slot).wait()
                flat[:count, :] += lands[which][slot].astype(f32)

            each_peer(add)
            unpack(out, 0, *out.shape, flat[...])

        def stage_residual(r):
            blocks_ready(ctx_all, CTX, r)
            attended = mm(wout_t[...], ctx_all[lax.rem(r, CTX_SLOTS)].reshape(channels, seq))
            xr = x_ring.at[lax.rem(r, ring)]
            for k, s in enumerate(lanes):
                x = xr[:, s].astype(f32) + attended[:, s] + col(B_OUT)
                x_one[:, s] = x
                mean = row_sum(x) * (1.0 / local)
                off = x - mean
                put_stat(ONE, k, mean)
                put_stat(ONE + parts, k, row_sum(off * off))
            blocks_sent(ctx_all, CTX, r)

        def stage_attend(r):
            slot = lax.rem(r, ring)
            inp_copy(r).wait()
            rolled = pltpu.roll(inp_rows[r].astype(f32), place[r, 0], 1).astype(bf16)
            x_ring[slot] = rolled
            mixed = mm(wqkv_t[...], rolled)
            for s in lanes:
                mix_ring[slot, :, s] = (mixed[:, s] + b_qkv[...]).astype(bf16)
            first, second = place[r, 2], place[r, 3]
            down = lax.broadcasted_iota(jnp.int32, (half, half), 0)
            along = lax.broadcasted_iota(jnp.int32, (half, half), 1)
            own = lambda at: (at >= first).astype(jnp.int32) + (at >= second).astype(jnp.int32)
            mask[...] = jnp.where(own(down) == own(along), 0.0, -1000000000.0)
            scale = math.log2(math.e) / math.sqrt(HD)
            blocks = [(h, b) for h in range(HG) for b in range(SPLIT)]

            def piece(part, n):
                h, b = blocks[n]
                start = part * local + h * HD
                return mix_ring[slot, start : start + HD, b * half : (b + 1) * half]

            def score(n):
                return mm_tn(piece(1, n), piece(0, n))

            def soften(n, scores):
                if blocks[n][1]:
                    scores = scores + mask[...]
                highest = jnp.max(scores, axis=0, keepdims=True)
                return jnp.exp2((scores - highest) * scale)

            def norm(n, exponent):
                chances = (exponent * (1.0 / row_sum(exponent))).astype(bf16)
                prob_ring[slot, n] = chances
                return chances

            def blend(n, chances):
                h, b = blocks[n]
                ctx_all[lax.rem(r, CTX_SLOTS), g, h * HD : (h + 1) * HD, b * half : (b + 1) * half] = mm(
                    piece(2, n), chances
                ).astype(bf16)

            held = {}
            for step in range(len(blocks) + 3):
                n = step - 0
                if 0 <= n < len(blocks):
                    held[0, n] = score(n)
                n = step - 1
                if 0 <= n < len(blocks):
                    held[1, n] = soften(n, held.pop((0, n)))
                n = step - 2
                if 0 <= n < len(blocks):
                    held[2, n] = norm(n, held.pop((1, n)))
                n = step - 3
                if 0 <= n < len(blocks):
                    blend(n, held.pop((2, n)))
            send_own(ctx_all, CTX, r)

        def stage_norm_back(r):
            slot = lax.rem(r, rog_ring.shape[0])
            kept = lax.rem(r, (NORM_BACK - FEED + 1))
            for k, s in enumerate(lanes):
                first = get_stat(BACK, k, 0, GRAD_LAG)
                second = get_stat(BACK + parts, k, 0, GRAD_LAG)
                for p in range(1, groups):
                    first += get_stat(BACK, k, p, GRAD_LAG)
                    second += get_stat(BACK + parts, k, p, GRAD_LAG)
                first = first * (1.0 / channels)
                second = second * (1.0 / channels)
                scaled = hid_grad[lax.rem(r, (GRAD_LAG + 1)), :, s] * col(GAIN1)
                back = inv_one[kept, k : k + 1, :] * (scaled - first - n_one[kept, :, s] * second)
                rog_ring[slot, :, s] = back
                low = back.astype(bf16)
                att_all[lax.rem(r, ATT_SLOTS), g, :, s] = low
                accumulate(S_BOUT, low.astype(f32))
            send_own(att_all, ATT, r)
            contexts = ctx_all[lax.rem(r, CTX_SLOTS)].reshape(channels, seq)
            g_out[...] += mm_nt(contexts, att_all[lax.rem(r, ATT_SLOTS), g])

        def stage_feed(r):
            kept = lax.rem(r, (NORM_BACK - FEED + 1))
            for k, s in enumerate(lanes):
                means = [get_stat(ONE, k, p) for p in range(groups)]
                center = sum(means[1:], means[0]) * (1.0 / groups)
                spread = get_stat(ONE + parts, k, 0)
                for p in range(1, groups):
                    spread += get_stat(ONE + parts, k, p)
                for mean in means:
                    spread += local * (mean - center) * (mean - center)
                inverse = lax.rsqrt(spread * (1.0 / channels) + eps)
                inv_one[kept, k : k + 1, :] = inverse
                normed = (x_one[:, s] - center) * inverse
                n_one[kept, :, s] = normed
                h = normed * col(GAIN1) + col(SHIFT1)
                hid[:, s] = h
                hid_low[:, s] = h.astype(bf16)
            pre[...] = mm(wup_t[...], hid_low[...])
            for j in range(hidden_units // local):
                units = slice(j * local, (j + 1) * local)
                for s in lanes:
                    u = pre[units, s] + b_up[units, :]
                    cdf = 0.5 + 0.5 * lax.erf(u * math.sqrt(0.5))
                    act[units, s] = (u * cdf).astype(bf16)
                    bell = jnp.exp2(u * u * (-0.5 * math.log2(math.e))) * (1.0 / math.sqrt(2.0 * math.pi))
                    slope[units, s] = cdf + u * bell
            branch = mm(wdown_t[...], act[...])
            gout_copy(r).wait()
            upstream[...] = pltpu.roll(gout_rows[r].astype(f32), place[r, 0], 1)
            for k, s in enumerate(lanes):
                x = hid[:, s] + branch[:, s] + col(B_DOWN)
                x_two[:, s] = x
                mean = row_sum(x) * (1.0 / local)
                off = x - mean
                scaled = upstream[:, s] * col(GAIN2)
                tile = (mean, row_sum(off * off), row_sum(scaled), row_sum(scaled * off))
                for n, value in enumerate(tile):
                    put_stat(TWO + n * parts, k, value)

        def stage_attend_back(r):
            slot = lax.rem(r, ring)
            blocks_ready(att_all, ATT, r)
            ctx_grad[...] = mm(
                wout_rows[...], att_all[lax.rem(r, ATT_SLOTS)].reshape(channels, seq)
            ).astype(bf16)
            factor = 1.0 / math.sqrt(HD)
            blocks = [(h, b) for h in range(HG) for b in range(SPLIT)]

            def at_block(part, n):
                h, b = blocks[n]
                start = part * local + h * HD
                return slice(start, start + HD), slice(b * half, (b + 1) * half)

            def piece(part, n):
                return mix_ring[slot, *at_block(part, n)]

            def spread(n):
                incoming = ctx_grad[at_block(0, n)]
                mix_grad[at_block(2, n)] = mm_nt(incoming, prob_ring[slot, n]).astype(bf16)

            def open_up(n):
                return mm_tn(piece(2, n), ctx_grad[at_block(0, n)])

            def center(n, prob_grad):
                at_n = at_block(0, n)
                inner = row_sum(ctx_grad[at_n].astype(f32) * ctx_all[lax.rem(r, CTX_SLOTS), g, *at_n].astype(f32))
                return (prob_ring[slot, n].astype(f32) * (prob_grad - inner)).astype(bf16)

            def queries(n, score_grad):
                mix_grad[at_block(0, n)] = (mm(piece(1, n), score_grad) * factor).astype(bf16)

            def keys(n, score_grad):
                mix_grad[at_block(1, n)] = (mm_nt(piece(0, n), score_grad) * factor).astype(bf16)

            held = {}
            for step in range(len(blocks) + 2):
                n = step - 0
                if 0 <= n < len(blocks):
                    held[0, n] = open_up(n)
                n = step - 0
                if 0 <= n < len(blocks):
                    spread(n)
                n = step - 1
                if 0 <= n < len(blocks):
                    held[1, n] = center(n, held.pop((0, n)))
                n = step - 2
                if 0 <= n < len(blocks):
                    queries(n, held[1, n])
                n = step - 2
                if 0 <= n < len(blocks):
                    keys(n, held.pop((1, n)))
            g_qkv[...] += mm_nt(mix_grad[...], x_ring[slot])
            blocks_sent(att_all, ATT, r)

            @pl.when(r >= 2)
            def _():
                grad_in_copy(r - 2).wait()

            total = mm(wqkv[...], mix_grad[...]) + rog_ring[lax.rem(r, rog_ring.shape[0])]
            gin_ring[lax.rem(r, 2)] = total
            grad_in_copy(r).start()
            base = 6 * local + hidden_units
            for n, start in ((0, 0), (1, 2 * local)):
                chunk = mix_grad[start : start + local, lanes[0]].astype(f32)
                for s in lanes[1:]:
                    chunk += mix_grad[start : start + local, s].astype(f32)
                sums[base + n * local : base + (n + 1) * local, :] += chunk

        def stage_feed_back(r):
            @pl.when(r >= 2)
            def _():
                result_copy(r - 2).wait()

            for k, s in enumerate(lanes):
                row = lambda p, n: get_stat(TWO + n * parts, k, p)
                means = [row(p, 0) for p in range(groups)]
                center = sum(means[1:], means[0]) * (1.0 / groups)
                spread, first, second = row(0, 1), row(0, 2), row(0, 3)
                for p in range(1, groups):
                    spread += row(p, 1)
                    first += row(p, 2)
                    second += row(p, 3)
                for p, mean in enumerate(means):
                    spread += local * (mean - center) * (mean - center)
                    second += (mean - center) * row(p, 2)
                inverse = lax.rsqrt(spread * (1.0 / channels) + eps)
                first = first * (1.0 / channels)
                second = second * inverse * (1.0 / channels)
                normed = (x_two[:, s] - center) * inverse
                res_ring[lax.rem(r, 2), :, s] = (normed * col(GAIN2) + col(SHIFT2)).astype(bf16)
                up = upstream[:, s]
                back = inverse * (up * col(GAIN2) - first - normed * second)
                rtg[:, s] = back
                low = back.astype(bf16)
                br_low[:, s] = low
                accumulate(S_GAIN2, up * normed)
                accumulate(S_SHIFT2, up)
                accumulate(S_BDOWN, low.astype(f32))
            result_copy(r).start()
            pre[...] = mm(wdown[...], br_low[...])
            g_down[...] += mm_nt(act[...], br_low[...])
            base = 6 * local
            for j in range(hidden_units // local):
                units = slice(j * local, (j + 1) * local)
                for s in lanes:
                    low = (slope[units, s] * pre[units, s]).astype(bf16)
                    pre_low[units, s] = low
                    sums[base + j * local : base + (j + 1) * local, :] += low.astype(f32)
            g_up[...] += mm_nt(pre_low[...], hid_low[...])
            change = mm(wup[...], pre_low[...])
            for k, s in enumerate(lanes):
                total = rtg[:, s] + change[:, s]
                hid_grad[lax.rem(r, (GRAD_LAG + 1)), :, s] = total
                normed = n_one[lax.rem(r, (NORM_BACK - FEED + 1)), :, s]
                scaled = total * col(GAIN1)
                put_stat(BACK, k, row_sum(scaled))
                put_stat(BACK + parts, k, row_sum(scaled * normed))
                accumulate(S_GAIN1, total * normed)
                accumulate(S_SHIFT1, total)

        def at(delay, stage):
            r = i - delay

            @pl.when(jnp.logical_and(r >= 0, r < rows))
            def _():
                stage(r)

        @pl.when(jnp.logical_and(i > RESIDUAL, i < rows + NORM_BACK))
        def _():
            stats_ready()

        at(FEED_BACK, stage_feed_back)
        at(FEED, stage_feed)
        at(RESIDUAL, stage_residual)

        @pl.when(jnp.logical_and(i >= RESIDUAL, i < rows + NORM_BACK - 1))
        def _():
            stats_send()

        at(0, stage_attend)
        at(NORM_BACK, stage_norm_back)

        @pl.when(i == rows - 1 + FEED_BACK)
        def _():
            for which in range(4):
                each_peer(lambda k, which=which: weight_copy(which, k, d).wait_send())
            for offset in range(1, groups):
                rows_copy(offset, g, lax.rem(g + offset, groups)).wait_send()
            send_grad(UP, g_up[...].T)
            send_grad(DOWN, g_down[...])

        @pl.when(i == rows - 1 + NORM_BACK)
        def _():
            send_grad(OUT, g_out[...])
            mine = all_sums.at[d]
            for n in range(6):
                mine[n : n + 1, :local] = row_sum(sums[n * local : (n + 1) * local, :].T)
            base = 6 * local
            mine[6:7, :] = row_sum(sums[base : base + hidden_units, :].T)

        at(PASS_CTX, lambda r: pass_on(ctx_all, CTX, r))
        at(DELAY, stage_attend_back)
        at(PASS_ATT, lambda r: pass_on(att_all, ATT, r))

        @pl.when(i == steps - 1)
        def _():
            send_grad(QKV, g_qkv[...].T)
            mine = all_sums.at[d]
            base = 6 * local + hidden_units
            mine[7:8, : 2 * local] = row_sum(sums[base : base + 2 * local, :].T)
            each_peer(lambda k: sums_copy(k, d).start())
            for which, out in ((UP, o_up), (DOWN, o_down), (OUT, o_out), (QKV, o_qkv)):
                grad_sum(which, out)
            each_peer(lambda k: sums_copy(k, lax.rem(d - k + dp, dp)).wait())
            o_sums[...] = jnp.sum(all_sums[...], axis=0)
        return carry

    lax.fori_loop(0, steps, step, 0)
    for r in (rows - 2, rows - 1):
        result_copy(r).wait()
        grad_in_copy(r).wait()


def run_layer(labels, inputs, grad_out, shards, b_qv, b_up, *vectors):
    groups = lax.axis_size("group")
    dp = lax.axis_size("dp")
    local, tok_count = inputs.shape
    rows, seq = labels.shape
    channels = groups * local
    half = seq // SPLIT
    parts = seq // LANES
    units = b_up.shape[1]
    ring = DELAY + 1
    vmem = pl.BlockSpec(memory_space=pltpu.VMEM)
    anywhere = pl.BlockSpec(memory_space=pl.ANY)
    acc_shapes = ((3 * local, local), (groups * local, local), (units, local), (units, local))
    sums_shape = (6 * local + units + 2 * local, LANES)
    shard_shapes = tuple(w.shape for w in shards)
    slots = tuple((dp, packed_rows(*s), LANES) for s in shard_shapes)
    row_sums = (8, units)
    block = (groups, local, seq)
    return pl.pallas_call(
        functools.partial(layer_kernel, rows, groups, dp),
        out_shape=(
            jax.ShapeDtypeStruct((local, tok_count), bf16),
            jax.ShapeDtypeStruct((local, tok_count), f32),
            *(jax.ShapeDtypeStruct(s, f32) for s in shard_shapes),
            jax.ShapeDtypeStruct(row_sums, f32),
            jax.ShapeDtypeStruct((rows, LANES), jnp.int32),
        ),
        in_specs=[vmem, anywhere, anywhere, *([vmem] * (len(shards) + 2 + len(vectors)))],
        out_specs=(anywhere, anywhere, *([vmem] * (len(shards) + 2))),
        scratch_shapes=[
            pltpu.SMEM((rows, LANES), jnp.int32),
            pltpu.VMEM((3 * local, LANES), f32),
            pltpu.VMEM((units, LANES), f32),
            pltpu.VMEM((6 * local, LANES), f32),
            pltpu.VMEM((rows, local, seq), bf16),
            pltpu.VMEM((rows, local, seq), bf16),
            pltpu.VMEM((2, local, seq), bf16),
            pltpu.VMEM((2, local, seq), f32),
            pltpu.VMEM((3 * local, local), bf16),
            pltpu.VMEM((local, 3 * local), bf16),
            pltpu.VMEM((local, channels), bf16),
            pltpu.VMEM((local, channels), bf16),
            pltpu.VMEM((units, local), bf16),
            pltpu.VMEM((local, units), bf16),
            pltpu.VMEM((local, units), bf16),
            pltpu.VMEM((units, local), bf16),
            *(pltpu.VMEM(s, bf16) for s in slots),
            pltpu.VMEM((groups, dp // groups, *slots[1][1:]), bf16),
            pltpu.VMEM((local, units), f32),
            pltpu.VMEM((units, local), f32),
            *(pltpu.VMEM(s, f32) for s in acc_shapes),
            pltpu.VMEM(sums_shape, f32),
            pltpu.VMEM((max(s[1] for s in slots), LANES), f32),
            *(pltpu.VMEM(s, bf16) for s in slots),
            pltpu.VMEM((dp, *row_sums), f32),
            pltpu.VMEM((CTX_SLOTS, *block), bf16),
            pltpu.VMEM((ATT_SLOTS, *block), bf16),
            pltpu.VMEM((rows + DELAY, groups, 8 * parts, LANES), f32),
            pltpu.VMEM((ring, local, seq), bf16),
            pltpu.VMEM((ring, 3 * local, seq), bf16),
            pltpu.VMEM((ring, HG * SPLIT, half, half), bf16),
            pltpu.VMEM((half, half), f32),
            pltpu.VMEM((local, seq), f32),
            pltpu.VMEM(((NORM_BACK - FEED + 1), local, seq), f32),
            pltpu.VMEM(((NORM_BACK - FEED + 1), parts, LANES), f32),
            pltpu.VMEM((local, seq), f32),
            pltpu.VMEM((local, seq), bf16),
            pltpu.VMEM((units, seq), f32),
            pltpu.VMEM((units, seq), bf16),
            pltpu.VMEM((units, seq), f32),
            pltpu.VMEM((local, seq), f32),
            pltpu.VMEM((local, seq), f32),
            pltpu.VMEM((local, seq), f32),
            pltpu.VMEM((local, seq), bf16),
            pltpu.VMEM((units, seq), bf16),
            pltpu.VMEM(((GRAD_LAG + 1), local, seq), f32),
            pltpu.VMEM((3, local, seq), f32),
            pltpu.VMEM((local, seq), bf16),
            pltpu.VMEM((3 * local, seq), bf16),
            pltpu.SemaphoreType.DMA((6, SEMS)),
            pltpu.SemaphoreType.DMA((6, SEMS)),
            pltpu.SemaphoreType.DMA((groups - 1, SEMS)),
            pltpu.SemaphoreType.DMA((groups - 1, SEMS)),
            pltpu.SemaphoreType.DMA((4, dp)),
            pltpu.SemaphoreType.DMA((4, dp)),
            pltpu.SemaphoreType.DMA((groups - 1,)),
            pltpu.SemaphoreType.DMA((groups - 1,)),
            pltpu.SemaphoreType.DMA((5, dp)),
            pltpu.SemaphoreType.DMA((5, dp)),
            pltpu.SemaphoreType.DMA((2, rows)),
            pltpu.SemaphoreType.DMA((2, 2)),
            pltpu.SemaphoreType.DMA,
        ],
        compiler_params=pltpu.CompilerParams(
            collective_id=0, has_side_effects=True, vmem_limit_bytes=63 << 20
        ),
        name="layer",
    )(labels, inputs, grad_out, *shards, b_qv, b_up, *(v.reshape(1, local) for v in vectors))


def finish_kernel(many, seq, result, grad_in, qkv, out, up, down, sums, place, *outs):
    i = pl.program_id(0)
    for n in range(many):
        toks = slice(n * seq, (n + 1) * seq)
        turn = place[i * many + n, 1]
        outs[0][:, toks] = pltpu.roll(result[:, toks].astype(f32), turn, 1).astype(bf16)
        outs[1][:, toks] = pltpu.roll(grad_in[:, toks], turn, 1)

    @pl.when(i == 0)
    def _():
        local = result.shape[0]
        for target, source in zip(outs[2:6], (qkv, out, up, down)):
            target[...] = source[...]
        for n in range(6):
            outs[6 + n][...] = sums[n : n + 1, :local]
        outs[12][...] = sums[6:7, :]
        outs[13][...] = sums[7:8, : 2 * local]


def finish(result, grad_in, *small):
    local, tok_count = result.shape
    rows = small[5].shape[0]
    seq = tok_count // rows
    units = small[4].shape[1]
    many = math.gcd(rows, FINISH_ROWS)
    block = pl.BlockSpec((local, many * seq), lambda i: (0, i))
    vmem = pl.BlockSpec(memory_space=pltpu.VMEM)
    shapes = (*(s.shape for s in small[:4]), *((1, local),) * 6, (1, units), (1, 2 * local))
    return pl.pallas_call(
        functools.partial(finish_kernel, many, seq),
        grid=(rows // many,),
        out_shape=(
            jax.ShapeDtypeStruct(result.shape, bf16),
            jax.ShapeDtypeStruct(grad_in.shape, f32),
            *(jax.ShapeDtypeStruct(s, f32) for s in shapes),
        ),
        in_specs=[block, block, *[vmem] * 5, pl.BlockSpec(memory_space=pltpu.SMEM)],
        out_specs=(block, block, *(vmem,) * len(shapes)),
        compiler_params=pltpu.CompilerParams(vmem_limit_bytes=60 << 20),
        name="finish",
    )(result, grad_in, *small)


def per_device(
    inputs,
    labels,
    w_qkv,
    b_qv,
    w_out,
    b_out,
    gain_one,
    shift_one,
    w_up,
    b_up,
    down_weight,
    down_bias,
    gain_two,
    shift_two,
    grad_out,
):
    shards = (w_qkv[0], w_out, w_up[0], down_weight[0])
    vectors = (b_out, gain_one, shift_one, down_bias, gain_two, shift_two)
    raw = run_layer(labels, inputs, grad_out, shards, b_qv, b_up, *vectors)
    result, input_grad, qkv, out, up, down, *sums = finish(*raw)
    flat = [s.reshape(-1) for s in sums]
    return (
        result,
        input_grad,
        qkv[None],
        sums[7],
        out,
        flat[0],
        flat[1],
        flat[2],
        up[None],
        sums[6],
        down[None],
        sums[3],
        flat[4],
        flat[5],
    )


def solution(mesh):
    placed = (
        P("group", "dp"),
        P("dp", None),
        P("group", "dp", None),
        P("group", None),
        P("dp", "group"),
        P("group"),
        P("group"),
        P("group"),
        P("group", "dp", None),
        P("group", None),
        P("group", "dp", None),
        P("group", None),
        P("group"),
        P("group"),
        P("group", "dp"),
    )
    return jax.shard_map(
        per_device,
        mesh=mesh,
        in_specs=placed,
        out_specs=(
            P("group", "dp"),
            P("group", "dp"),
            P("group", "dp", None),
            P("group", None),
            P("dp", "group"),
            P("group"),
            P("group"),
            P("group"),
            P("group", "dp", None),
            P("group", None),
            P("group", "dp", None),
            P("group", None),
            P("group"),
            P("group"),
        ),
        check_vma=False,
    )
```

time: 939 us -> 202 us (0.22); the launches traced: 926 us -> 201 us
  matrix products: 283 us -> 0 us
  blocking collectives: 209 us -> 0 us
  Pallas kernels: 0 us -> 201 us
  waiting for transfers between devices: 185 us -> 0 us
  local copies, waits for them, and re-layouts: 126 us -> 0 us
  other arithmetic: 84 us -> 0 us
  starting transfers between devices: 23.3 us -> 0 us
  between operations: 14.6 us -> 0.66 us
    dot_general x124 -> x0, matrix products: 283 us -> none  [the longest x4 94.6 us: contract_rows(): lax.dot_general(left, right, (((0,), (0,)), ((), ())), preferred_element_...]
    pallas_call x0 -> x2, Pallas kernels: none -> 201 us  [the longest x1 191 us: run_layer(): pl.pallas_call(functools.partial(layer_kernel, rows, groups, dp), out_sha...]
    all_gather x4 -> x0, blocking collectives: 128 us -> none  [the longest x1 33 us: per_device(): lax.all_gather(down_weight.astype(jnp.bfloat16), 'dp', axis=1, tiled=True)]
    unnamed x5 -> x0, waiting for transfers between devices: 115 us -> none
    psum x5 -> x0, blocking collectives: 81.6 us -> none  [the longest x1 37.6 us: per_device(): lax.psum((qv_sum[None], bout_sum, gain_one_sum, shift_one_sum, up_sum[Non...]
    psum x2 -> x0, waiting for transfers between devices: 62.7 us -> none  [norm_back(): lax.psum((jnp.sum(scaled, axis=0), jnp.sum(scaled * normed, axis=0)), 'gr...]
    reduce_sum x26 -> x0, other arithmetic: 44.5 us -> none  [the longest x16 11.2 us: attend_row(): totals = jnp.sum(exponent, axis=-1, keepdims=True)]
    unnamed x62 -> x0, local copies, waits for them, and re-layouts: 40 us -> none
  transfers between devices with their start and end apart: 8 -> 0, of which waited for: 4 -> 0; matrix products, arithmetic and copies ran while one was open for 5% -> 0% of each run, Pallas kernels for 0% -> 0%
where the time goes in v5:
time: 202 us; the launch traced here: 201 us
  Pallas kernels  201 us (100%)
    pallas_call x1, Pallas kernels, run_layer(): pl.pallas_call(functools.partial(layer_kernel, rows, groups, dp), out_sha...  191 us
    pallas_call x1, Pallas kernels, finish(): pl.pallas_call(functools.partial(finish_kernel, many, seq), grid=(rows //...  9.08 us

profile of v5, /device:TPU:0, one launch (start us, length us, event | category | flops | bytes accessed | tf_op | source)
XLA Modules:
  0.0 201.2 jit_solution(10834253576085306554)
XLA Ops:
  0.7 191.4 %layer.1 = (bf16[192,8192]{1,0:T(8,128)(2,1)}, f32[192,8192]{1,0:T(8,128)}, f32[24,576]{1,0:T(8,128)}, f32[96,192]{1,0:T(8,128)}, f32[24,768]{1,0:T(8,128)}, /*i...) custom-call(s32[16,512]{1,0:T(8,128)} %labels.1, bf16[192,8192]{1,0:T(8,128)(2,1)} %inp.1, ...), custom_call_target="tpu_custom_call" | custom-call | tf_op jit(solution)/shard_map/layer/pallas_call | solution.py:799
  192.1 9.1 %finish.1 = (bf16[192,8192]{1,0:T(8,128)(2,1)}, f32[192,8192]{1,0:T(8,128)}, f32[24,576]{1,0:T(8,128)}, f32[96,192]{1,0:T(8,128)}, f32[24,768]{1,0:T(8,128)}, /*...) custom-call(bf16[192,8192]{1,0:T(8,128)(2,1)} %get-tuple-element.36., ...), custom_call_target="tpu_custom_call" | custom-call | tf_op jit(solution)/shard_map/finish/pallas_call | solution.py:909

commit v6 on v5

--- a/solution.py
+++ b/solution.py
@@ -12,9 +12,10 @@
 HG = 3
 LANES = 128
 SPLIT = 2
-FINISH_ROWS = 4
+FINISH_ROWS = 8
 PASS_CTX, RESIDUAL, FEED, FEED_BACK, NORM_BACK, PASS_ATT, DELAY = 1, 3, 4, 5, 7, 8, 9
 CTX_SLOTS, ATT_SLOTS, SEMS = DELAY + 1, 5, 5
+FLATS = 4
 GRAD_LAG = NORM_BACK - FEED_BACK
 
 eps = 1e-12
@@ -134,7 +135,7 @@
     g_up,
     g_down,
     sums,
-    flat,
+    flats,
     land_qkv,
     land_out,
     land_up,
@@ -191,14 +192,12 @@
         return pltpu.make_async_copy(gout_in.at[:, toks], gout_rows.at[r], fetch.at[1, r])
 
     def result_copy(r):
-        toks = pl.ds(pl.multiple_of(r * seq, seq), seq)
         slot = lax.rem(r, 2)
-        return pltpu.make_async_copy(res_ring.at[slot], result.at[:, toks], store.at[0, slot])
+        return pltpu.make_async_copy(res_ring.at[slot], result.at[r], store.at[0, slot])
 
     def grad_in_copy(r):
-        toks = pl.ds(pl.multiple_of(r * seq, seq), seq)
         slot = lax.rem(r, 2)
-        return pltpu.make_async_copy(gin_ring.at[slot], grad_in.at[:, toks], store.at[1, slot])
+        return pltpu.make_async_copy(gin_ring.at[slot], grad_in.at[r], store.at[1, slot])
 
     def find_places():
         ids = labels[...]
@@ -364,11 +363,12 @@
                     barrier, inc=1, device_id={"dp": lax.rem(d + k, dp)}, device_id_type=MESH
                 )
             )
-            flat[...] = jnp.zeros_like(flat)
+            flats[...] = jnp.zeros_like(flats)
 
             def pack_shard(which):
-                pack(flat, shards[which][...])
-                fulls[which][d] = flat[: fulls[which].shape[1], :].astype(bf16)
+                buffer = flats.at[which]
+                pack(buffer, shards[which][...])
+                fulls[which][d] = buffer[: fulls[which].shape[1], :].astype(bf16)
 
             pack_shard(QKV)
             pl.semaphore_wait(barrier, groups - 1 + dp - 1)
@@ -387,11 +387,15 @@
             for ref in (g_qkv, g_out, g_up, g_down, sums):
                 ref[...] = jnp.zeros_like(ref)
             weights_ready(QKV, wide_mat)
-            for which in (OUT, UP, DOWN):
-                each_peer(lambda k, which=which: weight_copy(which, k, d).start())
+            each_peer(lambda k: weight_copy(OUT, k, d).start())
             mat = wide_mat[:, : 3 * local]
             wqkv[...] = mat.astype(bf16)
             wqkv_t[...] = mat.T.astype(bf16)
+
+        @pl.when(i == 1)
+        def _():
+            for which in (UP, DOWN):
+                each_peer(lambda k, which=which: weight_copy(which, k, d).start())
 
         @pl.when(i == RESIDUAL)
         def _():
@@ -448,12 +452,14 @@
             stage = stages[which]
             count = shards[which].shape[0]
             for slot in range(dp):
-                pack(flat, mat[slot * count : (slot + 1) * count])
-                stage[slot] = flat[: stage.shape[1], :].astype(bf16)
+                buffer = flats.at[slot % FLATS]
+                pack(buffer, mat[slot * count : (slot + 1) * count])
+                stage[slot] = buffer[: stage.shape[1], :].astype(bf16)
             each_peer(lambda k: grad_copy(which, k, d).start())
 
         def grad_sum(which, out):
             count = stages[which].shape[1]
+            flat = flats.at[which]
             flat[:count, :] = stages[which][d].astype(f32)
 
             def add(k):
@@ -799,8 +805,8 @@
     return pl.pallas_call(
         functools.partial(layer_kernel, rows, groups, dp),
         out_shape=(
-            jax.ShapeDtypeStruct((local, tok_count), bf16),
-            jax.ShapeDtypeStruct((local, tok_count), f32),
+            jax.ShapeDtypeStruct((rows, local, seq), bf16),
+            jax.ShapeDtypeStruct((rows, local, seq), f32),
             *(jax.ShapeDtypeStruct(s, f32) for s in shard_shapes),
             jax.ShapeDtypeStruct(row_sums, f32),
             jax.ShapeDtypeStruct((rows, LANES), jnp.int32),
@@ -830,7 +836,7 @@
             pltpu.VMEM((units, local), f32),
             *(pltpu.VMEM(s, f32) for s in acc_shapes),
             pltpu.VMEM(sums_shape, f32),
-            pltpu.VMEM((max(s[1] for s in slots), LANES), f32),
+            pltpu.VMEM((FLATS, max(s[1] for s in slots), LANES), f32),
             *(pltpu.VMEM(s, bf16) for s in slots),
             pltpu.VMEM((dp, *row_sums), f32),
             pltpu.VMEM((CTX_SLOTS, *block), bf16),
@@ -883,12 +889,12 @@
     for n in range(many):
         toks = slice(n * seq, (n + 1) * seq)
         turn = place[i * many + n, 1]
-        outs[0][:, toks] = pltpu.roll(result[:, toks].astype(f32), turn, 1).astype(bf16)
-        outs[1][:, toks] = pltpu.roll(grad_in[:, toks], turn, 1)
+        outs[0][:, toks] = pltpu.roll(result[n].astype(f32), turn, 1).astype(bf16)
+        outs[1][:, toks] = pltpu.roll(grad_in[n], turn, 1)
 
     @pl.when(i == 0)
     def _():
-        local = result.shape[0]
+        local = result.shape[1]
         for target, source in zip(outs[2:6], (qkv, out, up, down)):
             target[...] = source[...]
         for n in range(6):
@@ -898,11 +904,10 @@
 
 
 def finish(result, grad_in, *small):
-    local, tok_count = result.shape
-    rows = small[5].shape[0]
-    seq = tok_count // rows
+    rows, local, seq = result.shape
     units = small[4].shape[1]
     many = math.gcd(rows, FINISH_ROWS)
+    raw = pl.BlockSpec((many, local, seq), lambda i: (i, 0, 0))
     block = pl.BlockSpec((local, many * seq), lambda i: (0, i))
     vmem = pl.BlockSpec(memory_space=pltpu.VMEM)
     shapes = (*(s.shape for s in small[:4]), *((1, local),) * 6, (1, units), (1, 2 * local))
@@ -910,11 +915,11 @@
         functools.partial(finish_kernel, many, seq),
         grid=(rows // many,),
         out_shape=(
-            jax.ShapeDtypeStruct(result.shape, bf16),
-            jax.ShapeDtypeStruct(grad_in.shape, f32),
+            jax.ShapeDtypeStruct((local, rows * seq), bf16),
+            jax.ShapeDtypeStruct((local, rows * seq), f32),
             *(jax.ShapeDtypeStruct(s, f32) for s in shapes),
         ),
-        in_specs=[block, block, *[vmem] * 5, pl.BlockSpec(memory_space=pltpu.SMEM)],
+        in_specs=[raw, raw, *[vmem] * 5, pl.BlockSpec(memory_space=pltpu.SMEM)],
         out_specs=(block, block, *(vmem,) * len(shapes)),
         compiler_params=pltpu.CompilerParams(vmem_limit_bytes=60 << 20),
         name="finish",

time: 202 us -> 200 us (0.990)
  no operation moved by 1% of the time
where the time goes in v6:
time: 200 us
  Pallas kernels  199 us (100%)
    pallas_call x1, Pallas kernels, run_layer(): pl.pallas_call(functools.partial(layer_kernel, rows, groups, dp), out_sha...  191 us
    pallas_call x1, Pallas kernels, finish(): pl.pallas_call(functools.partial(finish_kernel, many, seq), grid=(rows //...  7.67 us

profile of v6, /device:TPU:0, one launch (start us, length us, event | category | flops | bytes accessed | tf_op | source)
XLA Modules:
  0.0 199.7 jit_solution(14792047506297887282)
XLA Ops:
  0.7 191.3 %layer.1 = (bf16[16,192,512]{2,1,0:T(8,128)(2,1)}, f32[16,192,512]{2,1,0:T(8,128)}, f32[24,576]{1,0:T(8,128)}, f32[96,192]{1,0:T(8,128)}, f32[24,768]{1,0:T(8,12...) custom-call(s32[16,512]{1,0:T(8,128)} %labels.1, bf16[192,8192]{1,0:T(8,128)(2,1)} %inp.1, ...), custom_call_target="tpu_custom_call" | custom-call | tf_op jit(solution)/shard_map/layer/pallas_call | solution.py:805
  192.0 7.7 %finish.1 = (bf16[192,8192]{1,0:T(8,128)(2,1)}, f32[192,8192]{1,0:T(8,128)}, f32[24,576]{1,0:T(8,128)}, f32[96,192]{1,0:T(8,128)}, f32[24,768]{1,0:T(8,128)}, /*...) custom-call(bf16[16,192,512]{2,1,0:T(8,128)(2,1)} %get-tuple-element, ...), custom_call_target="tpu_custom_call" | custom-call | tf_op jit(solution)/shard_map/finish/pallas_call | solution.py:914

commit v7 on v6

--- a/solution.py
+++ b/solution.py
@@ -13,8 +13,10 @@
 LANES = 128
 SPLIT = 2
 FINISH_ROWS = 8
-PASS_CTX, RESIDUAL, FEED, FEED_BACK, NORM_BACK, PASS_ATT, DELAY = 1, 3, 4, 5, 7, 8, 9
+PASS_CTX, RESIDUAL, FEED, FEED_BACK, NORM_BACK, PASS_ATT, DELAY = 1, 2, 4, 6, 8, 9, 10
 CTX_SLOTS, ATT_SLOTS, SEMS = DELAY + 1, 5, 5
+SLACK = 2
+FETCHED = 6
 FLATS = 4
 GRAD_LAG = NORM_BACK - FEED_BACK
 
@@ -129,7 +131,6 @@
     all_down,
     out_rows,
     wide_mat,
-    tall_mat,
     g_qkv,
     g_out,
     g_up,
@@ -147,7 +148,6 @@
     x_ring,
     mix_ring,
     prob_ring,
-    mask,
     x_one,
     n_one,
     inv_one,
@@ -158,12 +158,10 @@
     slope,
     x_two,
     upstream,
-    rtg,
     br_low,
     pre_low,
     hid_grad,
     rog_ring,
-    ctx_grad,
     mix_grad,
     send_blocks,
     recv_blocks,
@@ -180,16 +178,19 @@
     place_sem,
 ):
     steps = rows + DELAY
+    tall_mat = pre.at[:, : 2 * LANES]
     local = w_out.shape[1]
     seq = inp.shape[1] // rows
 
     def inp_copy(r):
         toks = pl.ds(pl.multiple_of(r * seq, seq), seq)
-        return pltpu.make_async_copy(inp.at[:, toks], inp_rows.at[r], fetch.at[0, r])
+        slot = lax.rem(r, FETCHED)
+        return pltpu.make_async_copy(inp.at[:, toks], inp_rows.at[slot], fetch.at[0, slot])
 
     def gout_copy(r):
         toks = pl.ds(pl.multiple_of(r * seq, seq), seq)
-        return pltpu.make_async_copy(gout_in.at[:, toks], gout_rows.at[r], fetch.at[1, r])
+        slot = lax.rem(r, FETCHED)
+        return pltpu.make_async_copy(gout_in.at[:, toks], gout_rows.at[slot], fetch.at[1, slot])
 
     def result_copy(r):
         slot = lax.rem(r, 2)
@@ -286,12 +287,12 @@
             block_copy(buf, base, 1, r, g).wait_send()
             block_copy(buf, base, 2, r, across).wait_send()
 
-        def stat_copy(step, offset, slot):
+        def stat_copy(at_step, offset, slot):
             return remote(
-                stats.at[step, slot],
-                stats.at[step, slot],
-                send_stats.at[offset - 1, lax.rem(step, SEMS)],
-                recv_stats.at[offset - 1, lax.rem(step, SEMS)],
+                stats.at[lax.rem(at_step, 8), slot],
+                stats.at[lax.rem(at_step, 8), slot],
+                send_stats.at[offset - 1, lax.rem(at_step, SEMS)],
+                recv_stats.at[offset - 1, lax.rem(at_step, SEMS)],
                 {"group": lax.rem(g + offset, groups)},
             )
 
@@ -301,14 +302,14 @@
 
         def stats_ready():
             for offset in range(1, groups):
-                stat_copy(i - 1, offset, lax.rem(g + groups - offset, groups)).wait_recv()
-                stat_copy(i - 1, offset, g).wait_send()
+                stat_copy(i - SLACK, offset, lax.rem(g + groups - offset, groups)).wait_recv()
+                stat_copy(i - SLACK, offset, g).wait_send()
 
         def put_stat(first, k, value):
-            stats[i, g, first + k : first + k + 1, :] = value
-
-        def get_stat(first, k, p, ago=1):
-            return stats[i - ago, p, first + k : first + k + 1, :]
+            stats[lax.rem(i, 8), g, first + k : first + k + 1, :] = value
+
+        def get_stat(first, k, p, ago):
+            return stats[lax.rem(i - ago, 8), p, first + k : first + k + 1, :]
 
         ONE, TWO, BACK = 0, 2 * parts, 6 * parts
         CTX, ATT = 0, 3
@@ -381,7 +382,7 @@
                 gout_copy(r).start()
                 return carry
 
-            lax.fori_loop(0, rows, fetch_row, 0)
+            lax.fori_loop(0, min(FETCHED, rows), fetch_row, 0)
             find_places()
             spread_vectors()
             for ref in (g_qkv, g_out, g_up, g_down, sums):
@@ -403,7 +404,7 @@
             for offset in range(1, groups):
                 rows_copy(offset, g, lax.rem(g + offset, groups)).start()
             out_rows[g] = all_out[pl.ds(g * per, per)]
-            wout_t[...] = tall_mat[...].T.astype(bf16)
+            wout_t[...] = tall_mat[:, :local].T.astype(bf16)
 
         @pl.when(i == FEED)
         def _():
@@ -412,7 +413,7 @@
             wup[...] = mat.astype(bf16)
             wup_t[...] = mat.T.astype(bf16)
             weights_ready(DOWN, tall_mat)
-            mat = tall_mat[...]
+            mat = tall_mat[:, :local]
             wdown[...] = mat.astype(bf16)
             wdown_t[...] = mat.T.astype(bf16)
 
@@ -424,8 +425,8 @@
             for p in range(groups):
                 for n in range(per):
                     unpack(wide_mat, n * count, count, local, out_rows[p, n].astype(f32))
-                tall_mat[p * local : (p + 1) * local, :] = wide_mat[:, :local].T
-            wout_rows[...] = tall_mat[...].T.astype(bf16)
+                tall_mat[p * local : (p + 1) * local, :local] = wide_mat[:, :local].T
+            wout_rows[...] = tall_mat[:, :local].T.astype(bf16)
 
         stages = fulls
         lands = (land_qkv, land_out, land_up, land_down)
@@ -476,7 +477,7 @@
             xr = x_ring.at[lax.rem(r, ring)]
             for k, s in enumerate(lanes):
                 x = xr[:, s].astype(f32) + attended[:, s] + col(B_OUT)
-                x_one[:, s] = x
+                x_one[lax.rem(r, FEED - RESIDUAL), :, s] = x
                 mean = row_sum(x) * (1.0 / local)
                 off = x - mean
                 put_stat(ONE, k, mean)
@@ -486,8 +487,15 @@
         def stage_attend(r):
             slot = lax.rem(r, ring)
             inp_copy(r).wait()
-            rolled = pltpu.roll(inp_rows[r].astype(f32), place[r, 0], 1).astype(bf16)
+            rolled = pltpu.roll(
+                inp_rows[lax.rem(r, FETCHED)].astype(f32), place[r, 0], 1
+            ).astype(bf16)
             x_ring[slot] = rolled
+
+            @pl.when(r + FETCHED < rows)
+            def _():
+                inp_copy(r + FETCHED).start()
+
             mixed = mm(wqkv_t[...], rolled)
             for s in lanes:
                 mix_ring[slot, :, s] = (mixed[:, s] + b_qkv[...]).astype(bf16)
@@ -495,7 +503,7 @@
             down = lax.broadcasted_iota(jnp.int32, (half, half), 0)
             along = lax.broadcasted_iota(jnp.int32, (half, half), 1)
             own = lambda at: (at >= first).astype(jnp.int32) + (at >= second).astype(jnp.int32)
-            mask[...] = jnp.where(own(down) == own(along), 0.0, -1000000000.0)
+            pre[:half, :half] = jnp.where(own(down) == own(along), 0.0, -1000000000.0)
             scale = math.log2(math.e) / math.sqrt(HD)
             blocks = [(h, b) for h in range(HG) for b in range(SPLIT)]
 
@@ -509,7 +517,7 @@
 
             def soften(n, scores):
                 if blocks[n][1]:
-                    scores = scores + mask[...]
+                    scores = scores + pre[:half, :half]
                 highest = jnp.max(scores, axis=0, keepdims=True)
                 return jnp.exp2((scores - highest) * scale)
 
@@ -562,40 +570,53 @@
             g_out[...] += mm_nt(contexts, att_all[lax.rem(r, ATT_SLOTS), g])
 
         def stage_feed(r):
+            act_r = act.at[lax.rem(r, FEED_BACK - FEED)]
+            slope_r = slope.at[lax.rem(r, FEED_BACK - FEED)]
+            hid_low_r = hid_low.at[lax.rem(r, FEED_BACK - FEED)]
+            x_two_r = x_two.at[lax.rem(r, FEED_BACK - FEED)]
+            upstream_r = upstream.at[lax.rem(r, FEED_BACK - FEED)]
+            x_one_r = x_one.at[lax.rem(r, FEED - RESIDUAL)]
             kept = lax.rem(r, (NORM_BACK - FEED + 1))
             for k, s in enumerate(lanes):
-                means = [get_stat(ONE, k, p) for p in range(groups)]
+                means = [get_stat(ONE, k, p, FEED - RESIDUAL) for p in range(groups)]
                 center = sum(means[1:], means[0]) * (1.0 / groups)
-                spread = get_stat(ONE + parts, k, 0)
+                spread = get_stat(ONE + parts, k, 0, FEED - RESIDUAL)
                 for p in range(1, groups):
-                    spread += get_stat(ONE + parts, k, p)
+                    spread += get_stat(ONE + parts, k, p, FEED - RESIDUAL)
                 for mean in means:
                     spread += local * (mean - center) * (mean - center)
                 inverse = lax.rsqrt(spread * (1.0 / channels) + eps)
                 inv_one[kept, k : k + 1, :] = inverse
-                normed = (x_one[:, s] - center) * inverse
+                normed = (x_one_r[:, s] - center) * inverse
                 n_one[kept, :, s] = normed
                 h = normed * col(GAIN1) + col(SHIFT1)
                 hid[:, s] = h
-                hid_low[:, s] = h.astype(bf16)
-            pre[...] = mm(wup_t[...], hid_low[...])
+                hid_low_r[:, s] = h.astype(bf16)
+            pre[...] = mm(wup_t[...], hid_low_r[...])
             for j in range(hidden_units // local):
                 units = slice(j * local, (j + 1) * local)
                 for s in lanes:
                     u = pre[units, s] + b_up[units, :]
                     cdf = 0.5 + 0.5 * lax.erf(u * math.sqrt(0.5))
-                    act[units, s] = (u * cdf).astype(bf16)
+                    act_r[units, s] = (u * cdf).astype(bf16)
                     bell = jnp.exp2(u * u * (-0.5 * math.log2(math.e))) * (1.0 / math.sqrt(2.0 * math.pi))
-                    slope[units, s] = cdf + u * bell
-            branch = mm(wdown_t[...], act[...])
+                    slope_r[units, s] = cdf + u * bell
+            branch = mm(wdown_t[...], act_r[...])
             gout_copy(r).wait()
-            upstream[...] = pltpu.roll(gout_rows[r].astype(f32), place[r, 0], 1)
+            upstream_r[...] = pltpu.roll(
+                gout_rows[lax.rem(r, FETCHED)].astype(f32), place[r, 0], 1
+            )
+
+            @pl.when(r + FETCHED < rows)
+            def _():
+                gout_copy(r + FETCHED).start()
+
             for k, s in enumerate(lanes):
                 x = hid[:, s] + branch[:, s] + col(B_DOWN)
-                x_two[:, s] = x
+                x_two_r[:, s] = x
                 mean = row_sum(x) * (1.0 / local)
                 off = x - mean
-                scaled = upstream[:, s] * col(GAIN2)
+                scaled = upstream_r[:, s] * col(GAIN2)
                 tile = (mean, row_sum(off * off), row_sum(scaled), row_sum(scaled * off))
                 for n, value in enumerate(tile):
                     put_stat(TWO + n * parts, k, value)
@@ -603,7 +624,7 @@
         def stage_attend_back(r):
             slot = lax.rem(r, ring)
             blocks_ready(att_all, ATT, r)
-            ctx_grad[...] = mm(
+            br_low[...] = mm(
                 wout_rows[...], att_all[lax.rem(r, ATT_SLOTS)].reshape(channels, seq)
             ).astype(bf16)
             factor = 1.0 / math.sqrt(HD)
@@ -618,15 +639,15 @@
                 return mix_ring[slot, *at_block(part, n)]
 
             def spread(n):
-                incoming = ctx_grad[at_block(0, n)]
+                incoming = br_low[at_block(0, n)]
                 mix_grad[at_block(2, n)] = mm_nt(incoming, prob_ring[slot, n]).astype(bf16)
 
             def open_up(n):
-                return mm_tn(piece(2, n), ctx_grad[at_block(0, n)])
+                return mm_tn(piece(2, n), br_low[at_block(0, n)])
 
             def center(n, prob_grad):
                 at_n = at_block(0, n)
-                inner = row_sum(ctx_grad[at_n].astype(f32) * ctx_all[lax.rem(r, CTX_SLOTS), g, *at_n].astype(f32))
+                inner = row_sum(br_low[at_n].astype(f32) * ctx_all[lax.rem(r, CTX_SLOTS), g, *at_n].astype(f32))
                 return (prob_ring[slot, n].astype(f32) * (prob_grad - inner)).astype(bf16)
 
             def queries(n, score_grad):
@@ -670,12 +691,17 @@
                 sums[base + n * local : base + (n + 1) * local, :] += chunk
 
         def stage_feed_back(r):
+            act_r = act.at[lax.rem(r, FEED_BACK - FEED)]
+            slope_r = slope.at[lax.rem(r, FEED_BACK - FEED)]
+            hid_low_r = hid_low.at[lax.rem(r, FEED_BACK - FEED)]
+            x_two_r = x_two.at[lax.rem(r, FEED_BACK - FEED)]
+            upstream_r = upstream.at[lax.rem(r, FEED_BACK - FEED)]
             @pl.when(r >= 2)
             def _():
                 result_copy(r - 2).wait()
 
             for k, s in enumerate(lanes):
-                row = lambda p, n: get_stat(TWO + n * parts, k, p)
+                row = lambda p, n: get_stat(TWO + n * parts, k, p, FEED_BACK - FEED)
                 means = [row(p, 0) for p in range(groups)]
                 center = sum(means[1:], means[0]) * (1.0 / groups)
                 spread, first, second = row(0, 1), row(0, 2), row(0, 3)
@@ -689,11 +715,11 @@
                 inverse = lax.rsqrt(spread * (1.0 / channels) + eps)
                 first = first * (1.0 / channels)
                 second = second * inverse * (1.0 / channels)
-                normed = (x_two[:, s] - center) * inverse
+                normed = (x_two_r[:, s] - center) * inverse
                 res_ring[lax.rem(r, 2), :, s] = (normed * col(GAIN2) + col(SHIFT2)).astype(bf16)
-                up = upstream[:, s]
+                up = upstream_r[:, s]
                 back = inverse * (up * col(GAIN2) - first - normed * second)
-                rtg[:, s] = back
+                hid[:, s] = back
                 low = back.astype(bf16)
                 br_low[:, s] = low
                 accumulate(S_GAIN2, up * normed)
@@ -701,18 +727,18 @@
                 accumulate(S_BDOWN, low.astype(f32))
             result_copy(r).start()
             pre[...] = mm(wdown[...], br_low[...])
-            g_down[...] += mm_nt(act[...], br_low[...])
+            g_down[...] += mm_nt(act_r[...], br_low[...])
             base = 6 * local
             for j in range(hidden_units // local):
                 units = slice(j * local, (j + 1) * local)
                 for s in lanes:
-                    low = (slope[units, s] * pre[units, s]).astype(bf16)
+                    low = (slope_r[units, s] * pre[units, s]).astype(bf16)
                     pre_low[units, s] = low
                     sums[base + j * local : base + (j + 1) * local, :] += low.astype(f32)
-            g_up[...] += mm_nt(pre_low[...], hid_low[...])
+            g_up[...] += mm_nt(pre_low[...], hid_low_r[...])
             change = mm(wup[...], pre_low[...])
             for k, s in enumerate(lanes):
-                total = rtg[:, s] + change[:, s]
+                total = hid[:, s] + change[:, s]
                 hid_grad[lax.rem(r, (GRAD_LAG + 1)), :, s] = total
                 normed = n_one[lax.rem(r, (NORM_BACK - FEED + 1)), :, s]
                 scaled = total * col(GAIN1)
@@ -728,10 +754,12 @@
             def _():
                 stage(r)
 
-        @pl.when(jnp.logical_and(i > RESIDUAL, i < rows + NORM_BACK))
+        @pl.when(jnp.logical_and(i >= RESIDUAL + SLACK, i < rows + NORM_BACK - 1 + SLACK))
         def _():
             stats_ready()
 
+        at(0, stage_attend)
+        at(NORM_BACK, stage_norm_back)
         at(FEED_BACK, stage_feed_back)
         at(FEED, stage_feed)
         at(RESIDUAL, stage_residual)
@@ -740,8 +768,6 @@
         def _():
             stats_send()
 
-        at(0, stage_attend)
-        at(NORM_BACK, stage_norm_back)
 
         @pl.when(i == rows - 1 + FEED_BACK)
         def _():
@@ -818,8 +844,8 @@
             pltpu.VMEM((3 * local, LANES), f32),
             pltpu.VMEM((units, LANES), f32),
             pltpu.VMEM((6 * local, LANES), f32),
-            pltpu.VMEM((rows, local, seq), bf16),
-            pltpu.VMEM((rows, local, seq), bf16),
+            pltpu.VMEM((FETCHED, local, seq), bf16),
+            pltpu.VMEM((FETCHED, local, seq), bf16),
             pltpu.VMEM((2, local, seq), bf16),
             pltpu.VMEM((2, local, seq), f32),
             pltpu.VMEM((3 * local, local), bf16),
@@ -833,7 +859,6 @@
             *(pltpu.VMEM(s, bf16) for s in slots),
             pltpu.VMEM((groups, dp // groups, *slots[1][1:]), bf16),
             pltpu.VMEM((local, units), f32),
-            pltpu.VMEM((units, local), f32),
             *(pltpu.VMEM(s, f32) for s in acc_shapes),
             pltpu.VMEM(sums_shape, f32),
             pltpu.VMEM((FLATS, max(s[1] for s in slots), LANES), f32),
@@ -841,27 +866,24 @@
             pltpu.VMEM((dp, *row_sums), f32),
             pltpu.VMEM((CTX_SLOTS, *block), bf16),
             pltpu.VMEM((ATT_SLOTS, *block), bf16),
-            pltpu.VMEM((rows + DELAY, groups, 8 * parts, LANES), f32),
+            pltpu.VMEM((8, groups, 8 * parts, LANES), f32),
             pltpu.VMEM((ring, local, seq), bf16),
             pltpu.VMEM((ring, 3 * local, seq), bf16),
             pltpu.VMEM((ring, HG * SPLIT, half, half), bf16),
-            pltpu.VMEM((half, half), f32),
-            pltpu.VMEM((local, seq), f32),
+            pltpu.VMEM((FEED - RESIDUAL, local, seq), f32),
             pltpu.VMEM(((NORM_BACK - FEED + 1), local, seq), f32),
             pltpu.VMEM(((NORM_BACK - FEED + 1), parts, LANES), f32),
             pltpu.VMEM((local, seq), f32),
-            pltpu.VMEM((local, seq), bf16),
+            pltpu.VMEM((FEED_BACK - FEED, local, seq), bf16),
             pltpu.VMEM((units, seq), f32),
-            pltpu.VMEM((units, seq), bf16),
-            pltpu.VMEM((units, seq), f32),
-            pltpu.VMEM((local, seq), f32),
-            pltpu.VMEM((local, seq), f32),
-            pltpu.VMEM((local, seq), f32),
+            pltpu.VMEM((FEED_BACK - FEED, units, seq), bf16),
+            pltpu.VMEM((FEED_BACK - FEED, units, seq), f32),
+            pltpu.VMEM((FEED_BACK - FEED, local, seq), f32),
+            pltpu.VMEM((FEED_BACK - FEED, local, seq), f32),
             pltpu.VMEM((local, seq), bf16),
             pltpu.VMEM((units, seq), bf16),
             pltpu.VMEM(((GRAD_LAG + 1), local, seq), f32),
             pltpu.VMEM((3, local, seq), f32),
-            pltpu.VMEM((local, seq), bf16),
             pltpu.VMEM((3 * local, seq), bf16),
             pltpu.SemaphoreType.DMA((6, SEMS)),
             pltpu.SemaphoreType.DMA((6, SEMS)),
@@ -873,12 +895,12 @@
             pltpu.SemaphoreType.DMA((groups - 1,)),
             pltpu.SemaphoreType.DMA((5, dp)),
             pltpu.SemaphoreType.DMA((5, dp)),
-            pltpu.SemaphoreType.DMA((2, rows)),
+            pltpu.SemaphoreType.DMA((2, FETCHED)),
             pltpu.SemaphoreType.DMA((2, 2)),
             pltpu.SemaphoreType.DMA,
         ],
         compiler_params=pltpu.CompilerParams(
-            collective_id=0, has_side_effects=True, vmem_limit_bytes=63 << 20
+            collective_id=0, has_side_effects=True, vmem_limit_bytes=65400 << 10
         ),
         name="layer",
     )(labels, inputs, grad_out, *shards, b_qv, b_up, *(v.reshape(1, local) for v in vectors))

time: 200 us -> 194 us (0.970)
  Pallas kernels: 199 us -> 193 us
    pallas_call x1, Pallas kernels: 191 us -> 185 us  [run_layer(): pl.pallas_call(functools.partial(layer_kernel, rows, groups, dp), out_sha...]
where the time goes in v7:
time: 194 us
  Pallas kernels  193 us (99%)
    pallas_call x1, Pallas kernels, run_layer(): pl.pallas_call(functools.partial(layer_kernel, rows, groups, dp), out_sha...  185 us
    pallas_call x1, Pallas kernels, finish(): pl.pallas_call(functools.partial(finish_kernel, many, seq), grid=(rows //...  7.67 us

profile of v7, /device:TPU:0, one launch (start us, length us, event | category | flops | bytes accessed | tf_op | source)
XLA Modules:
  0.0 193.8 jit_solution(6039902926801985260)
XLA Ops:
  0.7 185.5 %layer.1 = (bf16[16,192,512]{2,1,0:T(8,128)(2,1)}, f32[16,192,512]{2,1,0:T(8,128)}, f32[24,576]{1,0:T(8,128)}, f32[96,192]{1,0:T(8,128)}, f32[24,768]{1,0:T(8,12...) custom-call(s32[16,512]{1,0:T(8,128)} %labels.1, bf16[192,8192]{1,0:T(8,128)(2,1)} %inp.1, ...), custom_call_target="tpu_custom_call" | custom-call | tf_op jit(solution)/shard_map/layer/pallas_call | solution.py:831
  186.1 7.7 %finish.1 = (bf16[192,8192]{1,0:T(8,128)(2,1)}, f32[192,8192]{1,0:T(8,128)}, f32[24,576]{1,0:T(8,128)}, f32[96,192]{1,0:T(8,128)}, f32[24,768]{1,0:T(8,128)}, /*...) custom-call(bf16[16,192,512]{2,1,0:T(8,128)(2,1)} %get-tuple-element, ...), custom_call_target="tpu_custom_call" | custom-call | tf_op jit(solution)/shard_map/finish/pallas_call | solution.py:936
